TPU v7x, 128 devices: a whole 4x4x4 slice. The times are simulated.
128 devices in a mesh: ia: 8 (over z, core), ja: 4 (over x), ka: 4 (over y).
Axes of the slice: x: 4, y: 4, z: 4, core: 2. Of those that a mesh axis runs over, the one named last changes fastest.
Arguments:
- tensor: float32 [32, 128, 256, 512], P(None, 'ia', 'ja', 'ka'), may hold values from -9 to 9
- factor_b: float32 [32, 4, 64, 64], P(None, 'ja', ('ia', 'ka')), may hold values from -3 to 3
- factor_c: float32 [32, 4, 128, 64], P(None, 'ka', ('ia', 'ja')), may hold values from -3 to 3
Outputs:
- factor_a: float32 [32, 8, 16, 64], P(None, 'ia', ('ja', 'ka'))
- gram_a: float32 [32, 64, 64], replicated
All inputs are finite; a program needn't handle non-finite values.
Results may differ from a plain program's by a relative error of at most 0.00045.
Values sent between devices are 32-bit elements; how exact they have to be, the bound alone decides.
No kernel may reach another device: no remote copies, remote signals or barrier semaphores. Data moves between devices by JAX's collectives and lax.ppermute only.
A program may use at most 128 MiB of HBM per device.

v0:
```python
import jax
import jax.numpy as jnp
from jax import lax
from jax.sharding import PartitionSpec as P

HIGH = lax.Precision.HIGHEST


def gram_of(rows):
    return jnp.einsum("fjr,fjs->frs", rows, rows, precision=HIGH)


def solve_one(lower, rhs):
    return jax.scipy.linalg.cho_solve((lower, True), rhs.T).T


def on_device(tensor, factor_b, factor_c):
    gathered_b = lax.all_gather(factor_b, ("ia", "ka"), axis=2, tiled=True)[:, 0]
    gathered_c = lax.all_gather(factor_c, ("ia", "ja"), axis=2, tiled=True)[:, 0]
    gram_b, gram_c = lax.psum(
        (gram_of(factor_b[:, 0]), gram_of(factor_c[:, 0])), ("ia", "ja", "ka")
    )
    inner = jnp.einsum("fijk,fjr->frik", tensor, gathered_b, precision=HIGH)
    mttkrp_part = jnp.einsum("frik,fkr->fir", inner, gathered_c, precision=HIGH)
    lower = jax.vmap(jnp.linalg.cholesky)(gram_b * gram_c)
    total_rows = float(lax.axis_size("ia") * tensor.shape[1])
    owned = lax.psum_scatter(mttkrp_part, ("ja", "ka"), scatter_dimension=1, tiled=True)
    rows_a = jax.vmap(solve_one)(lower, owned)
    gram_a = lax.psum(gram_of(rows_a), ("ia", "ja", "ka")) / total_rows
    return (rows_a[:, None], gram_a)


def solution(mesh):
    return jax.shard_map(
        on_device,
        mesh=mesh,
        in_specs=(
            P(None, "ia", "ja", "ka"),
            P(None, "ja", ("ia", "ka"), None),
            P(None, "ka", ("ia", "ja"), None),
        ),
        out_specs=(P(None, "ia", ("ja", "ka"), None), P()),
        check_vma=False,
    )
```

profile of v0, /device:TPU:1, one launch (start us, length us, event | category | flops | bytes accessed | tf_op | source)
XLA Modules:
  0.0 621.5 jit_solution(1272839765207351690)
XLA Ops:
  8.0 0.0 all-reduce.7.cloned.1.call-start
  8.1 3.6 fusion.4
  11.7 3.7 fusion.2
  15.4 0.0 all-reduce.7.cloned.1.call-update
  15.4 0.0 all-gather.2.cloned.1.call-start
  15.5 0.6 copy.22
  16.1 0.0 all-gather.2.cloned.1.call-update
  16.1 0.0 reduce-scatter.4.cloned.1.call-start
  16.2 48.4 %all_gather.6 = f32[32,1,64,64]{3,0,1,2:T(8,128)S(1)} all-gather(f32[32,1,2,64]{3,0,1,2:T(8,128)S(1)} %copy.20), channel_id=1, replica_groups=mesh['ia'=8,'ja'=4,'ka'=4] {'ia','ka'}, dimensions={2}, use_global_device_ids=true | all-gather | bytes 540672 | tf_op jit(solution)/shard_map/all_gather | solution.py:18
  64.6 1.6 copy.21
  66.2 103.7 %all-reduce.7.cloned.1.call-done = (f32[32,64,64]{1,2,0:T(8,128)}, f32[32,64,64]{1,2,0:T(8,128)}) async-done(((f32[32,64,64]{1,2,0:T(8,128)}, f32[32,64,64]{1,2,0:T(8,128)}), (f32[32,64,64]{1,2,0:T(8,128)}, f32[32,64,64]{1,2,0:T(8,128)})) %all-reduce.7.cloned.1.call-update) | async-done | bytes 1048592 | tf_op jit(solution)/shard_map/psum | solution.py:20
  170.0 1.7 mul.3
  171.7 0.3 copy.17
  172.0 0.2 fusion.1
  172.2 188.3 %custom-call.11 = f32[32,64,64]{2,1,0:T(8,128)} custom-call(f32[32,64,64]{2,1,0:T(8,128)S(1)} %fusion.1), custom_call_target="Cholesky" | custom-call | tf_op jit(solution)/shard_map/vmap(jit(cholesky))/cholesky | solution.py:25
  360.6 1.9 copy.18
  362.4 0.7 select_reduce_fusion
  363.2 0.0 all-gather.2.cloned.1.call-done
  363.2 2.7 copy.40
  365.9 22.9 %multiply_reduce_fusion = f32[32,64,16]{1,2,0:T(8,128)S(1)} fusion(f32[32,16,64,128]{3,2,1,0:T(8,128)} %param.3, f32[32,64,128]{2,1,0:T(8,128)S(1)} %copy.40, f32[32,1,64,64]{2,3,0,1:T(8,128)} %copy.21), kind=kOutput, calls=%fused_computation | convolution fusion | flops 3229581312 | bytes 18481152 | tf_op jit(solution)/shard_map/fijk,fjr->frik/dot_general | solution.py:23
  388.8 0.8 copy.43
  389.6 0.0 reduce-scatter.4.cloned.1.call-update
  389.6 0.0 all-reduce.5.cloned.1.call-start
  389.6 2.0 select_bitcast_fusion
  391.6 67.2 %custom-call.12 = f32[32,1,64,64]{0,2,3,1:T(8,128)S(1)} custom-call(f32[32,1,64,64]{0,3,2,1:T(8,128)} %select_bitcast_fusion), custom_call_target="InvertDiagBlocksLowerTriangular" | custom-call | tf_op jit(solution)/shard_map/vmap(jit(_cho_solve))/triangular_solve | solution.py:14
  458.9 0.9 copy.37
  459.8 0.0 reduce-scatter.4.cloned.1.call-done
  459.8 1.7 convolution_bitcast_fusion
  461.6 1.7 fusion.6
  463.3 1.3 broadcast_multiply_fusion.1
  464.6 147.1 %all-reduce.5.cloned.1.call-done = f32[32,64,64]{2,1,0:T(8,128)} async-done(((f32[32,64,64]{2,1,0:T(8,128)}), f32[32,64,64]{2,1,0:T(8,128)}) %all-reduce.5.cloned.1.call-update) | async-done | bytes 524304 | tf_op jit(solution)/shard_map/psum | solution.py:29
  611.7 2.3 broadcast_multiply_fusion
  (11 shorter events, 0.1 us)
Async XLA Ops:
  8.0 8.2 %copy-start.2 = (f32[32,1,2,64]{3,2,1,0:T(2,128)S(1)}, f32[32,1,2,64]{3,2,1,0:T(2,128)}, u32[]{:S(2)}) copy-start(f32[32,1,2,64]{3,2,1,0:T(2,128)} %param.4) | copy-start | bytes 49156
  8.0 7.5 %copy-start = (f32[32,1,4,64]{3,2,1,0:T(4,128)S(1)}, f32[32,1,4,64]{3,2,1,0:T(4,128)}, u32[]{:S(2)}) copy-start(f32[32,1,4,64]{3,2,1,0:T(4,128)} %param.5) | copy-start | bytes 98308
  8.0 162.0 %all-reduce.7.cloned.1.call-start = ((), (), s32[]{:S(2)}) async-start(), calls=%async_computation.4 | async-start | bytes 4194304 | tf_op jit(solution)/shard_map/psum | solution.py:20
  15.4 347.8 %all-gather.2.cloned.1.call-start = ((), (), s32[]{:S(2)}) async-start(), calls=%async_computation.1 | async-start | bytes 2162688 | tf_op jit(solution)/shard_map/all_gather | solution.py:19
  16.1 443.7 %reduce-scatter.4.cloned.1.call-start = ((), (), s32[]{:S(2)}) async-start(), calls=%async_computation.3 | async-start | bytes 278528
  389.6 222.1 %all-reduce.5.cloned.1.call-start = ((), (), s32[]{:S(2)}) async-start(), calls=%async_computation.2 | async-start | bytes 2097152 | tf_op jit(solution)/shard_map/psum | solution.py:29
  463.3 150.7 %copy-start.1 = (f32[32,1,64]{2,1,0:T(1,128)}, f32[32,1,64]{2,1,0:T(1,128)S(1)}, u32[]{:S(2)}) copy-start(f32[32,1,64]{2,1,0:T(1,128)S(1)} %fusion.6) | copy-start | bytes 24580
Sparse Core Ops, SparseCore 0:
  15.6 154.3 all-reduce.6
  464.8 146.8 all-reduce.4
Sparse Core Ops, SparseCore 1:
  18.2 47.8 all-gather.1
  389.7 68.4 reduce-scatter.3
where the time goes:
time: 622 us; the launch traced here: 621 us
  other arithmetic  264 us (42%)
  waiting for transfers between devices  251 us (40%)
  blocking collectives  48.4 us (8%)
  matrix products  33.7 us (5%)
  between operations  15.6 us (3%)
  local copies, waits for them, and re-layouts  8.86 us (1%)
    another operation x4, other arithmetic, on_device(): lower = jax.vmap(jnp.linalg.cholesky)(gram_b * gram_c)  189 us
    psum x1, waiting for transfers between devices, on_device(): gram_a = lax.psum(gram_of(rows_a), ('ia', 'ja', 'ka')) / total_rows  147 us
    psum x1, waiting for transfers between devices, on_device(): lax.psum((gram_of(factor_b[:, 0]), gram_of(factor_c[:, 0])), ('ia', 'ja',...  104 us
    another operation x3, other arithmetic, solve_one(): return jax.scipy.linalg.cho_solve((lower, True), rhs.T).T  69.2 us
    all_gather x1, blocking collectives, on_device(): lax.all_gather(factor_b, ('ia', 'ka'), axis=2, tiled=True)[:, 0]  48.4 us
    dot_general x1, matrix products, on_device(): inner = jnp.einsum('fijk,fjr->frik', tensor, gathered_b, precision=HIGH)  22.9 us
  transfers between devices with their start and end apart: 4, of which 2 were waited for; matrix products, arithmetic and copies ran while one was open for 43% of the time, Pallas kernels for 0%

commit v1 on v0

v1 whole, which is shorter than its diff:
```python
import functools

import jax
import jax.numpy as jnp
from jax import lax
from jax.experimental import pallas as pl
from jax.experimental.pallas import tpu as pltpu
from jax.sharding import PartitionSpec as P

FIELDS, RANK = 32, 64
PAIRS = FIELDS // 2
ID, JD, KD = 16, 64, 128
N_IA, N_JA, N_KA = 8, 4, 4
N_Z = N_IA // 2
B_OWN = JD // (N_IA * N_KA)
C_OWN = KD // (N_IA * N_JA)
I_ALL = N_IA * ID
B_PART = JD // N_KA
C_PART = KD // N_JA
HIGH = lax.Precision.HIGHEST
MIB = 1024 * 1024
VMEM = pl.BlockSpec(memory_space=pltpu.VMEM)
ANY = pl.BlockSpec(memory_space=pl.ANY)
SLOTS = 4


def call(kernel, out_shape, operands, *, specs=None, scratch=(), vmem=16, cost=None):
    return pl.pallas_call(
        kernel,
        out_shape=out_shape,
        in_specs=[VMEM] * len(operands) if specs is None else specs,
        out_specs=jax.tree.map(lambda _: VMEM, out_shape),
        scratch_shapes=list(scratch),
        cost_estimate=cost,
        compiler_params=pltpu.CompilerParams(vmem_limit_bytes=vmem * MIB),
    )(*operands)


def f32(*shape):
    return jax.ShapeDtypeStruct(shape, jnp.float32)


def place():
    ia = lax.axis_index("ia")
    return ia // 2, lax.rem(ia, 2), lax.axis_index("ja"), lax.axis_index("ka")


def split_kernel(x_hbm, out, buffer, sems):
    def copy(f):
        slot = lax.rem(f, SLOTS)
        return pltpu.make_async_copy(x_hbm.at[f], buffer.at[slot], sems.at[slot])

    for f in range(SLOTS):
        copy(f).start()

    def step(f, carry):
        copy(f).wait()
        x = buffer[lax.rem(f, SLOTS)].reshape(ID * JD, KD)
        high = x.astype(jnp.bfloat16)
        low = (x - high.astype(jnp.float32)).astype(jnp.bfloat16)
        out[f, :, :KD] = high
        out[f, :, KD:] = low

        @pl.when(f + SLOTS < FIELDS)
        def _():
            copy(f + SLOTS).start()

        return carry

    lax.fori_loop(0, FIELDS, step, 0)


def pack_kernel(b, c, out):
    for p in range(PAIRS):
        for side in range(2):
            lanes = slice(side * RANK, (side + 1) * RANK)
            out[p, 0:B_OWN, lanes] = b[2 * p + side]
            out[p, B_OWN : B_OWN + C_OWN, lanes] = c[2 * p + side]
        out[p, B_OWN + C_OWN :, :] = jnp.zeros((8 - B_OWN - C_OWN, 2 * RANK), jnp.float32)


def in_order(pieces, first, rows):
    n = len(pieces)
    rising = jnp.concatenate([pieces[-t % n] for t in range(n)], axis=0)
    return pltpu.roll(rising, first * rows, 0)


def along_z_kernel(m0, m1, m2, m3, b, c):
    z, _, _, _ = place()
    parts = (m0, m1, m2, m3)
    for p in range(PAIRS):
        b[p] = in_order([m[p, :B_OWN, :] for m in parts], z, B_OWN)
        c[p] = in_order([m[p, B_OWN : B_OWN + C_OWN, :] for m in parts], z, C_OWN)


def along_xy_kernel(b0, b1, b2, b3, c0, c1, c2, c3, out):
    _, _, x, y = place()
    for p in range(PAIRS):
        for z in range(N_Z):
            rows = slice(z * B_OWN, (z + 1) * B_OWN)
            n = B_OWN * N_KA
            out[p, z * n : (z + 1) * n, :] = in_order([b[p, rows, :] for b in (b0, b1, b2, b3)], y, B_OWN)
        for z in range(N_Z):
            rows = slice(z * C_OWN, (z + 1) * C_OWN)
            n = C_OWN * N_JA
            at = JD // 2 + z * n
            out[p, at : at + n, :] = in_order([c[p, rows, :] for c in (c0, c1, c2, c3)], x, C_OWN)


def swap_halves(v):
    return pltpu.roll(v, RANK, 1)


def mttkrp_kernel(xs, mine, other, out, rows_b, rows_c, weights, scaled):
    _, core, x, y = place()
    lane = lax.broadcasted_iota(jnp.int32, (1, 2 * RANK), 1)
    left = lane < RANK
    nb, nc = B_OWN * N_KA, C_OWN * N_JA

    def step(p, carry):
        for z in range(N_Z):
            for source, c in ((mine, core), (other, 1 - core)):
                at = pl.multiple_of(z * 2 * nb + c * nb, nb)
                rows_b[pl.ds(at, nb), :] = source[p, z * nb : (z + 1) * nb, :]
                at = pl.multiple_of(z * 2 * nc + c * nc, nc)
                rows_c[pl.ds(at, nc), :] = source[p, JD // 2 + z * nc : JD // 2 + (z + 1) * nc, :]
        b, c = rows_b[...], rows_c[...]
        out[p, ID : ID + B_PART, :] = rows_b[pl.ds(pl.multiple_of(y * B_PART, B_PART), B_PART), :]
        out[p, ID + B_PART :, :] = rows_c[pl.ds(pl.multiple_of(x * C_PART, C_PART), C_PART), :]
        c1 = c.astype(jnp.bfloat16).astype(jnp.float32)
        c2 = (c - c1).astype(jnp.bfloat16).astype(jnp.float32)
        c3 = c - c1 - c2
        sums = []
        for side in range(2):
            if side == 0:
                first = jnp.where(left, c1, swap_halves(c2))
                second = jnp.where(left, c3, 0.0)
                weight = jnp.where(left, b, swap_halves(b))
            else:
                first = jnp.where(left, swap_halves(c1), c2)
                second = jnp.where(left, swap_halves(c3), 0.0)
                weight = jnp.where(left, swap_halves(b), b)
            for half in range(2):
                rows = slice(half * KD, (half + 1) * KD)
                weights[side, rows, :KD] = first.astype(jnp.bfloat16)
                weights[side, rows, KD:] = second.astype(jnp.bfloat16)
            product = jnp.dot(xs[2 * p + side], weights[side], preferred_element_type=jnp.float32)
            product = product.reshape(ID, JD, 4 * RANK)
            total = jnp.sum(product[:, :, :KD] * weight + product[:, :, KD:] * weight, axis=1)
            sums.append(total)
        even = sums[0] + swap_halves(sums[0])
        odd = sums[1] + swap_halves(sums[1])
        out[p, :ID, :] = jnp.where(left, even, odd)
        return carry

    lax.fori_loop(0, PAIRS, step, 0)


def total_kernel(received, out):
    total = received[0, :ID, :]
    for s in range(1, N_JA * N_KA):
        total = total + received[s, :ID, :]
    out[...] = total


def rows_gram(rows):
    return lax.dot_general(rows, rows, (((0,), (0,)), ((), ())), precision=HIGH, preferred_element_type=jnp.float32)


def factor_kernel(received, out):
    n = N_JA * N_KA
    gram = rows_gram(received[:, ID : ID + B_PART, :].reshape(n * B_PART, 2 * RANK))
    gram = gram * rows_gram(received[:, ID + B_PART :, :].reshape(n * C_PART, 2 * RANK))
    lane = lax.broadcasted_iota(jnp.int32, (RANK, 2 * RANK), 1)
    row = lax.broadcasted_iota(jnp.int32, (RANK, 2 * RANK), 0)
    eye = jnp.where(lane == row + RANK, 1.0, 0.0)
    sides = (gram[:RANK], swap_halves(gram[RANK:]))
    tiles = [[jnp.where(lane < RANK, s, eye)[8 * t : 8 * t + 8] for t in range(RANK // 8)] for s in sides]
    sub = lax.broadcasted_iota(jnp.int32, (8, 1), 0)
    for k in range(RANK):
        t, r = divmod(k, 8)
        for z in tiles:
            pivot_row = z[t][r : r + 1, :]
            step = pivot_row * (1.0 / pivot_row[:, k : k + 1])
            for u in range(t, RANK // 8):
                column = z[u][:, k : k + 1]
                if u == t:
                    if r == 7:
                        continue
                    column = jnp.where(sub > r, column, 0.0)
                z[u] = z[u] - column * step
    for side, z in enumerate(tiles):
        z = jnp.concatenate(z, axis=0)
        pivots = jnp.sum(jnp.where(lane == row, z, 0.0), axis=1, keepdims=True)
        inverse = jnp.where(lane >= RANK, z * lax.rsqrt(pivots), 0.0)
        out[side * RANK : (side + 1) * RANK, :] = inverse if side else swap_halves(inverse)


def finish_kernel(w0, w1, w2, w3, v0, v1, v2, v3, inverse, out, every, rows):
    z, core, _, _ = place()
    for parts, c in (((w0, w1, w2, w3), core), ((v0, v1, v2, v3), 1 - core)):
        for s, part in enumerate(parts):
            at = (lax.rem(z - s + N_Z, N_Z) * 2 + c) * ID
            every[pl.ds(pl.multiple_of(at, ID), ID), :] = part[...]
    inv = inverse[...]
    half = lax.dot_general(every[...], inv, (((1,), (1,)), ((), ())), precision=HIGH, preferred_element_type=jnp.float32)
    solved = jnp.dot(half, inv, precision=HIGH, preferred_element_type=jnp.float32)
    rows[...] = solved
    gram = rows_gram(solved) * (1.0 / I_ALL)
    lane = lax.broadcasted_iota(jnp.int32, (RANK, 2 * RANK), 1)
    gram = jnp.where(lane < RANK, gram[:RANK], gram[RANK:])
    own = rows[pl.ds(pl.multiple_of((z * 2 + core) * ID, ID), ID), :]
    for q in range(ID):
        out[q, :RANK, :] = gram
        out[q, RANK:, :] = jnp.broadcast_to(own[q : q + 1], (8, 2 * RANK))


def unpack_kernel(received, rows, gram):
    for p in range(PAIRS):
        for side in range(2):
            lanes = slice(side * RANK, (side + 1) * RANK)
            gram[2 * p + side] = received[p, :RANK, lanes]
            rows[2 * p + side, 0] = received[p, RANK : RANK + 1, lanes]


def shifts(n, stride=1):
    return [[(i, (i + s * stride) % (n * stride)) for i in range(n * stride)] for s in range(1, n)]


CORE_SWAP = [(i, i ^ 1) for i in range(N_IA)]


def around(value, axis, perms):
    return [value] + [lax.ppermute(value, axis, perm) for perm in perms]


def on_device(tensor, factor_b, factor_c):
    z_shifts, line = shifts(N_Z, 2), shifts(4)
    packed = call(pack_kernel, f32(PAIRS, 8, 2 * RANK), (factor_b[:, 0], factor_c[:, 0]))
    xs = call(
        split_kernel,
        pltpu.VMEM((FIELDS, ID * JD, 2 * KD), jnp.bfloat16),
        (tensor,),
        specs=[ANY],
        scratch=[pltpu.VMEM((SLOTS, ID, JD, KD), jnp.float32), pltpu.SemaphoreType.DMA((SLOTS,))],
        vmem=24,
        cost=pl.CostEstimate(flops=5 * tensor.size, bytes_accessed=4 * tensor.size, transcendentals=0),
    )
    parts = around(packed, "ia", z_shifts)
    b, c = call(along_z_kernel, (f32(PAIRS, 8, 2 * RANK), f32(PAIRS, 16, 2 * RANK)), parts)
    parts = around(b, "ka", line) + around(c, "ja", line)
    mine = call(along_xy_kernel, f32(PAIRS, 96, 2 * RANK), parts)
    other = lax.ppermute(mine, "ia", CORE_SWAP)
    sent = call(
        mttkrp_kernel,
        f32(PAIRS, ID + B_PART + C_PART, 2 * RANK),
        (xs, mine, other),
        scratch=[
            pltpu.VMEM((JD, 2 * RANK), jnp.float32),
            pltpu.VMEM((KD, 2 * RANK), jnp.float32),
            pltpu.VMEM((2, 2 * KD, 4 * RANK), jnp.bfloat16),
            pltpu.VMEM((8, 128), jnp.float32),
        ],
        vmem=40,
    )
    received = lax.all_to_all(sent, ("ja", "ka"), 0, 0)
    owned = call(total_kernel, f32(ID, 2 * RANK), (received,))
    parts = around(owned, "ia", z_shifts)
    inverse = call(
        factor_kernel,
        f32(2 * RANK, 2 * RANK),
        (received,),
        cost=pl.CostEstimate(flops=64 * 64 * 64 * 64, bytes_accessed=MIB, transcendentals=0),
    )
    parts = parts + [lax.ppermute(part, "ia", CORE_SWAP) for part in parts]
    sent = call(
        finish_kernel,
        f32(PAIRS, RANK + 8, 2 * RANK),
        (*parts, inverse),
        scratch=[pltpu.VMEM((I_ALL, 2 * RANK), jnp.float32)] * 2,
    )
    received = lax.all_to_all(sent, ("ja", "ka"), 0, 0)
    rows, gram = call(unpack_kernel, (f32(FIELDS, 1, 1, RANK), f32(FIELDS, RANK, RANK)), (received,))
    return rows, gram


def solution(mesh):
    return jax.shard_map(
        on_device,
        mesh=mesh,
        in_specs=(
            P(None, "ia", "ja", "ka"),
            P(None, "ja", ("ia", "ka"), None),
            P(None, "ka", ("ia", "ja"), None),
        ),
        out_specs=(P(None, "ia", ("ja", "ka"), None), P()),
        check_vma=False,
    )
```

time: 622 us -> 106 us (0.17)
  other arithmetic: 264 us -> 0 us
  waiting for transfers between devices: 251 us -> 8.91 us
  Pallas kernels: 0 us -> 34 us
  matrix products: 33.7 us -> 0 us
  starting transfers between devices: 0.17 us -> 25.9 us
  blocking collectives: 48.4 us -> 29 us
  between operations: 15.6 us -> 0.72 us
    another operation x7 -> x0, other arithmetic: 258 us -> none  [the longest x4 189 us: on_device(): lower = jax.vmap(jnp.linalg.cholesky)(gram_b * gram_c)]
    psum x2 -> x0, waiting for transfers between devices: 251 us -> none  [the longest x1 147 us: on_device(): gram_a = lax.psum(gram_of(rows_a), ('ia', 'ja', 'ka')) / total_rows]
    all_gather x1 -> x0, blocking collectives: 48.4 us -> none  [on_device(): lax.all_gather(factor_b, ('ia', 'ka'), axis=2, tiled=True)[:, 0]]
    pallas_call x0 -> x9, Pallas kernels: none -> 34 us  [call(): pl.pallas_call(kernel, out_shape=out_shape, in_specs=[VMEM] * len(operand...]
    dot_general x3 -> x0, matrix products: 30.2 us -> none  [the longest x1 22.9 us: on_device(): inner = jnp.einsum('fijk,fjr->frik', tensor, gathered_b, precision=HIGH)]
    all_to_all x0 -> x2, blocking collectives: none -> 29 us  [on_device(): received = lax.all_to_all(sent, ('ja', 'ka'), 0, 0)]
    ppermute x0 -> x17, starting transfers between devices: none -> 25.9 us  [the longest x12 15.1 us: around(): return [value] + [lax.ppermute(value, axis, perm) for perm in perms]]
    ppermute x0 -> x17, waiting for transfers between devices: none -> 8.91 us  [the longest x12 8.89 us: around(): return [value] + [lax.ppermute(value, axis, perm) for perm in perms]]
  transfers between devices with their start and end apart: 4 -> 17, of which waited for: 2 -> 6; matrix products, arithmetic and copies ran while one was open for 43% -> 0% of each run, Pallas kernels for 0% -> 15%
where the time goes in v1:
time: 106 us
  Pallas kernels  34 us (32%)
  blocking collectives  29 us (27%)
  starting transfers between devices  25.9 us (24%)
  waiting for transfers between devices  8.91 us (8%)
  local copies, waits for them, and re-layouts  7.32 us (7%)
    pallas_call x9, Pallas kernels, call(): pl.pallas_call(kernel, out_shape=out_shape, in_specs=[VMEM] * len(operand...  34 us
    all_to_all x2, blocking collectives, on_device(): received = lax.all_to_all(sent, ('ja', 'ka'), 0, 0)  29 us
    ppermute x12, starting transfers between devices, around(): return [value] + [lax.ppermute(value, axis, perm) for perm in perms]  15.1 us
    ppermute x12, waiting for transfers between devices, around(): return [value] + [lax.ppermute(value, axis, perm) for perm in perms]  8.89 us
    unnamed x6, local copies, waits for them, and re-layouts  7.32 us
    ppermute x4, starting transfers between devices, on_device(): parts = parts + [lax.ppermute(part, 'ia', CORE_SWAP) for part in parts]  6.67 us
    ppermute x1, starting transfers between devices, on_device(): other = lax.ppermute(mine, 'ia', CORE_SWAP)  4.2 us
  transfers between devices with their start and end apart: 17, of which 6 were waited for; matrix products, arithmetic and copies ran while one was open for 0% of the time, Pallas kernels for 15%

profile of v1, /device:TPU:1, one launch (start us, length us, event | category | flops | bytes accessed | tf_op | source)
XLA Modules:
  0.0 105.9 jit_solution(2887304494544390398)
XLA Ops:
  0.6 0.8 copy-done.1
  1.5 0.8 copy-done.2
  2.3 4.7 %collective-permute-start.2 = (f32[16,8,128]{2,1,0:T(8,128)S(1)}, f32[16,8,128]{2,1,0:T(8,128)S(1)}, u32[]{:S(2)}, u32[]{:S(2)}) collective-permute-start(f32[16,8,128]{2,1,0:T(8,128)S(1)} %shard_map.51.m0), channel_id=1, source_target_pairs={{0,96},{16,112},{32,0},{48,16},{64,32},{80,48},{96,64},{112,80},{1... | collective-permute-start | bytes 196616 | tf_op jit(solution)/shard_map/ppermute | solution.py:234
  7.0 0.7 collective-permute-start
  7.7 0.6 collective-permute-done.2.m3
  8.3 3.4 %collective-permute-done.1.m2 = f32[16,8,128]{2,1,0:T(8,128)S(1)} collective-permute-done((f32[16,8,128]{2,1,0:T(8,128)S(1)}, f32[16,8,128]{2,1,0:T(8,128)S(1)}, u32[]{:S(2)}, u32[]{:S(2)}) %collective-permute-start.1) | collective-permute-done | bytes 65568 | tf_op jit(solution)/shard_map/ppermute | solution.py:234
  11.7 0.3 collective-permute-done.m1
  12.1 2.8 %collective-permute-start.5 = (f32[16,8,128]{2,1,0:T(8,128)S(1)}, f32[16,8,128]{2,1,0:T(8,128)S(1)}, u32[]{:S(2)}, u32[]{:S(2)}) collective-permute-start(f32[16,8,128]{2,1,0:T(8,128)S(1)} %get-tuple-element.4.b0), channel_id=1, source_target_pairs={{0,3},{1,0},{2,1},{3,2},{4,7},{5,4},{6,5},{7,6},{8,11},{9,8},{10,9... | collective-permute-start | bytes 196616 | tf_op jit(solution)/shard_map/ppermute | solution.py:234
  14.9 2.5 %collective-permute-start.8 = (f32[16,16,128]{2,1,0:T(8,128)S(1)}, f32[16,16,128]{2,1,0:T(8,128)S(1)}, u32[]{:S(2)}, u32[]{:S(2)}) collective-permute-start(f32[16,16,128]{2,1,0:T(8,128)S(1)} %get-tuple-element.5.c0), channel_id=1, source_target_pairs={{0,12},{4,0},{8,4},{12,8},{1,13},{5,1},{9,5},{13,9},{2,14},{6,2},{... | collective-permute-start | bytes 393224 | tf_op jit(solution)/shard_map/ppermute | solution.py:234
  17.4 0.5 collective-permute-start.7
  17.9 0.6 collective-permute-start.6
  18.5 0.3 collective-permute-start.4
  18.8 0.7 collective-permute-start.3
  19.5 3.6 %collective-permute-done.4.b2 = f32[16,8,128]{2,1,0:T(8,128)S(1)} collective-permute-done((f32[16,8,128]{2,1,0:T(8,128)S(1)}, f32[16,8,128]{2,1,0:T(8,128)S(1)}, u32[]{:S(2)}, u32[]{:S(2)}) %collective-permute-start.4) | collective-permute-done | bytes 65568 | tf_op jit(solution)/shard_map/ppermute | solution.py:234
  23.2 0.6 collective-permute-done.3.b1
  23.8 0.3 collective-permute-done.6.c1
  24.2 4.2 %collective-permute-start.9 = (f32[16,96,128]{2,1,0:T(8,128)S(1)}, f32[16,96,128]{2,1,0:T(8,128)S(1)}, u32[]{:S(2)}, u32[]{:S(2)}) collective-permute-start(f32[16,96,128]{2,1,0:T(8,128)S(1)} %shard_map.53.mine), channel_id=1, source_target_pairs={{0,16},{16,0},{32,48},{48,32},{64,80},{80,64},{96,112},{112,96},{1... | collective-permute-start | bytes 2359304 | tf_op jit(solution)/shard_map/ppermute | solution.py:253
  28.4 10.0 %shard_map.50.xs = bf16[32,1024,256]{2,1,0:T(8,128)(2,1)S(1)} custom-call(f32[32,16,64,128]{3,2,1,0:T(8,128)} %x_hbm.1), custom_call_target="tpu_custom_call" | custom-call | flops 20971520 | bytes 16777216 | tf_op jit(solution)/shard_map/pallas_call | solution.py:28
  38.5 5.7 %copy-done = bf16[32,1024,256]{2,1,0:T(8,128)(2,1)} copy-done((bf16[32,1024,256]{2,1,0:T(8,128)(2,1)}, bf16[32,1024,256]{2,1,0:T(8,128)(2,1)S(1)}, u32[]{:S(2)}) %copy-start) | copy-done | bytes 16777240
  44.2 15.7 %shard_map.54 = f32[16,64,128]{2,1,0:T(8,128)S(1)} custom-call(bf16[32,1024,256]{2,1,0:T(8,128)(2,1)} %copy-done, f32[16,96,128]{2,1,0:T(8,128)S(1)} %shard_map.53.mine, f32[16,96,128]{2,1,0:T(8,128)S(1)} %collective-permute-done.9.other), custom_call_target="tpu_custom_call" | custom-call | tf_op jit(solution)/shard_map/pallas_call | solution.py:28
  59.9 14.1 %all_to_all.10.received = f32[16,64,128]{2,1,0:T(8,128)S(1)} all-to-all(f32[16,64,128]{2,1,0:T(8,128)S(1)} %shard_map.54), channel_id=1, replica_groups=mesh['ia'=8,'ja'=4,'ka'=4] {'ja','ka'}, dimensions={0} | all-to-all | bytes 1048576 | tf_op jit(solution)/shard_map/all_to_all | solution.py:266
  74.1 0.6 collective-permute-start.12
  74.7 0.9 collective-permute-start.11
  75.6 0.8 collective-permute-start.10
  76.3 3.1 %collective-permute-start.13 = (f32[16,128]{1,0:T(8,128)S(1)}, f32[16,128]{1,0:T(8,128)S(1)}, u32[]{:S(2)}, u32[]{:S(2)}) collective-permute-start(f32[16,128]{1,0:T(8,128)S(1)} %shard_map.55.w0), channel_id=1, source_target_pairs={{0,16},{16,0},{32,48},{48,32},{64,80},{80,64},{96,112},{112,96},{1... | collective-permute-start | bytes 24584 | tf_op jit(solution)/shard_map/ppermute | solution.py:275
  79.5 0.6 collective-permute-start.16
  80.1 2.4 %collective-permute-start.15 = (f32[16,128]{1,0:T(8,128)S(1)}, f32[16,128]{1,0:T(8,128)S(1)}, u32[]{:S(2)}, u32[]{:S(2)}) collective-permute-start(f32[16,128]{1,0:T(8,128)S(1)} %collective-permute-done.11.w2), channel_id=1, source_target_pairs={{0,16},{16,0},{32,48},{48,32},{64,80},{80,64},{96,112},{112,96},{1... | collective-permute-start | bytes 24584 | tf_op jit(solution)/shard_map/ppermute | solution.py:275
  82.4 0.6 collective-permute-start.14
  83.0 5.9 %shard_map.56.inverse = f32[128,128]{1,0:T(8,128)S(1)} custom-call(f32[16,64,128]{2,1,0:T(8,128)S(1)} %all_to_all.10.received), custom_call_target="tpu_custom_call" | custom-call | flops 16777216 | bytes 1048576 | tf_op jit(solution)/shard_map/pallas_call | solution.py:28
  89.0 0.9 shard_map.57
  89.9 14.9 %all_to_all.11.received = f32[16,72,128]{2,1,0:T(8,128)S(1)} all-to-all(f32[16,72,128]{2,1,0:T(8,128)S(1)} %shard_map.57), channel_id=1, replica_groups=mesh['ia'=8,'ja'=4,'ka'=4] {'ja','ka'}, dimensions={0} | all-to-all | bytes 1179648 | tf_op jit(solution)/shard_map/all_to_all | solution.py:282
  104.7 1.2 %shard_map.58 = (f32[32,1,1,64]{3,2,1,0:T(1,128)}, f32[32,64,64]{2,1,0:T(8,128)}) custom-call(f32[16,72,128]{2,1,0:T(8,128)S(1)} %all_to_all.11.received), custom_call_target="tpu_custom_call" | custom-call | tf_op jit(solution)/shard_map/pallas_call | solution.py:28
  (19 shorter events, 0.4 us)
Async XLA Ops:
  0.6 0.8 copy-start.1
  1.5 0.8 copy-start.2
  2.3 6.0 %collective-permute-start.2 = (f32[16,8,128]{2,1,0:T(8,128)S(1)}, f32[16,8,128]{2,1,0:T(8,128)S(1)}, u32[]{:S(2)}, u32[]{:S(2)}) collective-permute-start(f32[16,8,128]{2,1,0:T(8,128)S(1)} %shard_map.51.m0), channel_id=1, source_target_pairs={{0,96},{16,112},{32,0},{48,16},{64,32},{80,48},{96,64},{112,80},{1... | collective-permute-start | bytes 196616 | tf_op jit(solution)/shard_map/ppermute | solution.py:234
  7.0 4.7 %collective-permute-start.1 = (f32[16,8,128]{2,1,0:T(8,128)S(1)}, f32[16,8,128]{2,1,0:T(8,128)S(1)}, u32[]{:S(2)}, u32[]{:S(2)}) collective-permute-start(f32[16,8,128]{2,1,0:T(8,128)S(1)} %shard_map.51.m0), channel_id=1, source_target_pairs={{0,64},{16,80},{32,96},{48,112},{64,0},{80,16},{96,32},{112,48},{1... | collective-permute-start | bytes 196616 | tf_op jit(solution)/shard_map/ppermute | solution.py:234
  7.0 5.0 %collective-permute-start = (f32[16,8,128]{2,1,0:T(8,128)S(1)}, f32[16,8,128]{2,1,0:T(8,128)S(1)}, u32[]{:S(2)}, u32[]{:S(2)}) collective-permute-start(f32[16,8,128]{2,1,0:T(8,128)S(1)} %shard_map.51.m0), channel_id=1, source_target_pairs={{0,32},{16,48},{32,64},{48,80},{64,96},{80,112},{96,0},{112,16},{1... | collective-permute-start | bytes 196616 | tf_op jit(solution)/shard_map/ppermute | solution.py:234
  12.1 6.8 %collective-permute-start.5 = (f32[16,8,128]{2,1,0:T(8,128)S(1)}, f32[16,8,128]{2,1,0:T(8,128)S(1)}, u32[]{:S(2)}, u32[]{:S(2)}) collective-permute-start(f32[16,8,128]{2,1,0:T(8,128)S(1)} %get-tuple-element.4.b0), channel_id=1, source_target_pairs={{0,3},{1,0},{2,1},{3,2},{4,7},{5,4},{6,5},{7,6},{8,11},{9,8},{10,9... | collective-permute-start | bytes 196616 | tf_op jit(solution)/shard_map/ppermute | solution.py:234
  14.9 8.9 %collective-permute-start.8 = (f32[16,16,128]{2,1,0:T(8,128)S(1)}, f32[16,16,128]{2,1,0:T(8,128)S(1)}, u32[]{:S(2)}, u32[]{:S(2)}) collective-permute-start(f32[16,16,128]{2,1,0:T(8,128)S(1)} %get-tuple-element.5.c0), channel_id=1, source_target_pairs={{0,12},{4,0},{8,4},{12,8},{1,13},{5,1},{9,5},{13,9},{2,14},{6,2},{... | collective-permute-start | bytes 393224 | tf_op jit(solution)/shard_map/ppermute | solution.py:234
  17.4 6.5 %collective-permute-start.7 = (f32[16,16,128]{2,1,0:T(8,128)S(1)}, f32[16,16,128]{2,1,0:T(8,128)S(1)}, u32[]{:S(2)}, u32[]{:S(2)}) collective-permute-start(f32[16,16,128]{2,1,0:T(8,128)S(1)} %get-tuple-element.5.c0), channel_id=1, source_target_pairs={{0,8},{4,12},{8,0},{12,4},{1,9},{5,13},{9,1},{13,5},{2,10},{6,14},... | collective-permute-start | bytes 393224 | tf_op jit(solution)/shard_map/ppermute | solution.py:234
  17.9 6.2 %collective-permute-start.6 = (f32[16,16,128]{2,1,0:T(8,128)S(1)}, f32[16,16,128]{2,1,0:T(8,128)S(1)}, u32[]{:S(2)}, u32[]{:S(2)}) collective-permute-start(f32[16,16,128]{2,1,0:T(8,128)S(1)} %get-tuple-element.5.c0), channel_id=1, source_target_pairs={{0,4},{4,8},{8,12},{12,0},{1,5},{5,9},{9,13},{13,1},{2,6},{6,10},{... | collective-permute-start | bytes 393224 | tf_op jit(solution)/shard_map/ppermute | solution.py:234
  18.5 4.7 %collective-permute-start.4 = (f32[16,8,128]{2,1,0:T(8,128)S(1)}, f32[16,8,128]{2,1,0:T(8,128)S(1)}, u32[]{:S(2)}, u32[]{:S(2)}) collective-permute-start(f32[16,8,128]{2,1,0:T(8,128)S(1)} %get-tuple-element.4.b0), channel_id=1, source_target_pairs={{0,2},{1,3},{2,0},{3,1},{4,6},{5,7},{6,4},{7,5},{8,10},{9,11},{10,... | collective-permute-start | bytes 196616 | tf_op jit(solution)/shard_map/ppermute | solution.py:234
  18.8 5.0 %collective-permute-start.3 = (f32[16,8,128]{2,1,0:T(8,128)S(1)}, f32[16,8,128]{2,1,0:T(8,128)S(1)}, u32[]{:S(2)}, u32[]{:S(2)}) collective-permute-start(f32[16,8,128]{2,1,0:T(8,128)S(1)} %get-tuple-element.4.b0), channel_id=1, source_target_pairs={{0,1},{1,2},{2,3},{3,0},{4,5},{5,6},{6,7},{7,4},{8,9},{9,10},{10,1... | collective-permute-start | bytes 196616 | tf_op jit(solution)/shard_map/ppermute | solution.py:234
  24.2 19.9 %collective-permute-start.9 = (f32[16,96,128]{2,1,0:T(8,128)S(1)}, f32[16,96,128]{2,1,0:T(8,128)S(1)}, u32[]{:S(2)}, u32[]{:S(2)}) collective-permute-start(f32[16,96,128]{2,1,0:T(8,128)S(1)} %shard_map.53.mine), channel_id=1, source_target_pairs={{0,16},{16,0},{32,48},{48,32},{64,80},{80,64},{96,112},{112,96},{1... | collective-permute-start | bytes 2359304 | tf_op jit(solution)/shard_map/ppermute | solution.py:253
  38.4 5.7 %copy-start = (bf16[32,1024,256]{2,1,0:T(8,128)(2,1)}, bf16[32,1024,256]{2,1,0:T(8,128)(2,1)S(1)}, u32[]{:S(2)}) copy-start(bf16[32,1024,256]{2,1,0:T(8,128)(2,1)S(1)} %shard_map.50.xs) | copy-start | bytes 50331652
  74.1 5.4 %collective-permute-start.12 = (f32[16,128]{1,0:T(8,128)S(1)}, f32[16,128]{1,0:T(8,128)S(1)}, u32[]{:S(2)}, u32[]{:S(2)}) collective-permute-start(f32[16,128]{1,0:T(8,128)S(1)} %shard_map.55.w0), channel_id=1, source_target_pairs={{0,96},{16,112},{32,0},{48,16},{64,32},{80,48},{96,64},{112,80},{1... | collective-permute-start | bytes 24584 | tf_op jit(solution)/shard_map/ppermute | solution.py:234
  74.7 5.4 %collective-permute-start.11 = (f32[16,128]{1,0:T(8,128)S(1)}, f32[16,128]{1,0:T(8,128)S(1)}, u32[]{:S(2)}, u32[]{:S(2)}) collective-permute-start(f32[16,128]{1,0:T(8,128)S(1)} %shard_map.55.w0), channel_id=1, source_target_pairs={{0,64},{16,80},{32,96},{48,112},{64,0},{80,16},{96,32},{112,48},{1... | collective-permute-start | bytes 24584 | tf_op jit(solution)/shard_map/ppermute | solution.py:234
  75.6 6.9 %collective-permute-start.10 = (f32[16,128]{1,0:T(8,128)S(1)}, f32[16,128]{1,0:T(8,128)S(1)}, u32[]{:S(2)}, u32[]{:S(2)}) collective-permute-start(f32[16,128]{1,0:T(8,128)S(1)} %shard_map.55.w0), channel_id=1, source_target_pairs={{0,32},{16,48},{32,64},{48,80},{64,96},{80,112},{96,0},{112,16},{1... | collective-permute-start | bytes 24584 | tf_op jit(solution)/shard_map/ppermute | solution.py:234
  76.3 12.6 %collective-permute-start.13 = (f32[16,128]{1,0:T(8,128)S(1)}, f32[16,128]{1,0:T(8,128)S(1)}, u32[]{:S(2)}, u32[]{:S(2)}) collective-permute-start(f32[16,128]{1,0:T(8,128)S(1)} %shard_map.55.w0), channel_id=1, source_target_pairs={{0,16},{16,0},{32,48},{48,32},{64,80},{80,64},{96,112},{112,96},{1... | collective-permute-start | bytes 24584 | tf_op jit(solution)/shard_map/ppermute | solution.py:275
  79.5 9.5 %collective-permute-start.16 = (f32[16,128]{1,0:T(8,128)S(1)}, f32[16,128]{1,0:T(8,128)S(1)}, u32[]{:S(2)}, u32[]{:S(2)}) collective-permute-start(f32[16,128]{1,0:T(8,128)S(1)} %collective-permute-done.12.w3), channel_id=1, source_target_pairs={{0,16},{16,0},{32,48},{48,32},{64,80},{80,64},{96,112},{112,96},{1... | collective-permute-start | bytes 24584 | tf_op jit(solution)/shard_map/ppermute | solution.py:275
  80.1 8.9 %collective-permute-start.15 = (f32[16,128]{1,0:T(8,128)S(1)}, f32[16,128]{1,0:T(8,128)S(1)}, u32[]{:S(2)}, u32[]{:S(2)}) collective-permute-start(f32[16,128]{1,0:T(8,128)S(1)} %collective-permute-done.11.w2), channel_id=1, source_target_pairs={{0,16},{16,0},{32,48},{48,32},{64,80},{80,64},{96,112},{112,96},{1... | collective-permute-start | bytes 24584 | tf_op jit(solution)/shard_map/ppermute | solution.py:275
  82.4 6.5 %collective-permute-start.14 = (f32[16,128]{1,0:T(8,128)S(1)}, f32[16,128]{1,0:T(8,128)S(1)}, u32[]{:S(2)}, u32[]{:S(2)}) collective-permute-start(f32[16,128]{1,0:T(8,128)S(1)} %collective-permute-done.10.w1), channel_id=1, source_target_pairs={{0,16},{16,0},{32,48},{48,32},{64,80},{80,64},{96,112},{112,96},{1... | collective-permute-start | bytes 24584 | tf_op jit(solution)/shard_map/ppermute | solution.py:275

commit v2 on v1

--- a/solution.py
+++ b/solution.py
@@ -21,7 +21,7 @@
 MIB = 1024 * 1024
 VMEM = pl.BlockSpec(memory_space=pltpu.VMEM)
 ANY = pl.BlockSpec(memory_space=pl.ANY)
-SLOTS = 4
+UNROLL = 4
 
 
 def call(kernel, out_shape, operands, *, specs=None, scratch=(), vmem=16, cost=None):
@@ -45,32 +45,12 @@
     return ia // 2, lax.rem(ia, 2), lax.axis_index("ja"), lax.axis_index("ka")
 
 
-def split_kernel(x_hbm, out, buffer, sems):
-    def copy(f):
-        slot = lax.rem(f, SLOTS)
-        return pltpu.make_async_copy(x_hbm.at[f], buffer.at[slot], sems.at[slot])
-
-    for f in range(SLOTS):
-        copy(f).start()
-
-    def step(f, carry):
-        copy(f).wait()
-        x = buffer[lax.rem(f, SLOTS)].reshape(ID * JD, KD)
-        high = x.astype(jnp.bfloat16)
-        low = (x - high.astype(jnp.float32)).astype(jnp.bfloat16)
-        out[f, :, :KD] = high
-        out[f, :, KD:] = low
-
-        @pl.when(f + SLOTS < FIELDS)
-        def _():
-            copy(f + SLOTS).start()
-
-        return carry
-
-    lax.fori_loop(0, FIELDS, step, 0)
-
-
-def pack_kernel(b, c, out):
+def pack_kernel(b_hbm, c_hbm, tensor, out, b, c, sems):
+    copies = [pltpu.make_async_copy(b_hbm, b, sems.at[0]), pltpu.make_async_copy(c_hbm, c, sems.at[1])]
+    for copy in copies:
+        copy.start()
+    for copy in copies:
+        copy.wait()
     for p in range(PAIRS):
         for side in range(2):
             lanes = slice(side * RANK, (side + 1) * RANK)
@@ -111,22 +91,22 @@
     return pltpu.roll(v, RANK, 1)
 
 
-def mttkrp_kernel(xs, mine, other, out, rows_b, rows_c, weights, scaled):
+def mttkrp_kernel(tensor, mine, other, out):
     _, core, x, y = place()
     lane = lax.broadcasted_iota(jnp.int32, (1, 2 * RANK), 1)
     left = lane < RANK
+    first_core = core == 0
     nb, nc = B_OWN * N_KA, C_OWN * N_JA
 
-    def step(p, carry):
-        for z in range(N_Z):
-            for source, c in ((mine, core), (other, 1 - core)):
-                at = pl.multiple_of(z * 2 * nb + c * nb, nb)
-                rows_b[pl.ds(at, nb), :] = source[p, z * nb : (z + 1) * nb, :]
-                at = pl.multiple_of(z * 2 * nc + c * nc, nc)
-                rows_c[pl.ds(at, nc), :] = source[p, JD // 2 + z * nc : JD // 2 + (z + 1) * nc, :]
-        b, c = rows_b[...], rows_c[...]
-        out[p, ID : ID + B_PART, :] = rows_b[pl.ds(pl.multiple_of(y * B_PART, B_PART), B_PART), :]
-        out[p, ID + B_PART :, :] = rows_c[pl.ds(pl.multiple_of(x * C_PART, C_PART), C_PART), :]
+    def both(p, at, rows):
+        here, there = mine[p, pl.ds(at, rows), :], other[p, pl.ds(at, rows), :]
+        return [jnp.where(first_core, here, there), jnp.where(first_core, there, here)]
+
+    def pair(p):
+        b = jnp.concatenate([part for z in range(N_Z) for part in both(p, z * nb, nb)], axis=0)
+        c = jnp.concatenate([part for z in range(N_Z) for part in both(p, JD // 2 + z * nc, nc)], axis=0)
+        out[p, ID : ID + B_PART, :] = jnp.concatenate(both(p, pl.multiple_of(y * nb, nb), nb), axis=0)
+        out[p, ID + B_PART :, :] = jnp.concatenate(both(p, pl.multiple_of(JD // 2 + x * nc, nc), nc), axis=0)
         c1 = c.astype(jnp.bfloat16).astype(jnp.float32)
         c2 = (c - c1).astype(jnp.bfloat16).astype(jnp.float32)
         c3 = c - c1 - c2
@@ -140,20 +120,27 @@
                 first = jnp.where(left, swap_halves(c1), c2)
                 second = jnp.where(left, swap_halves(c3), 0.0)
                 weight = jnp.where(left, swap_halves(b), b)
-            for half in range(2):
-                rows = slice(half * KD, (half + 1) * KD)
-                weights[side, rows, :KD] = first.astype(jnp.bfloat16)
-                weights[side, rows, KD:] = second.astype(jnp.bfloat16)
-            product = jnp.dot(xs[2 * p + side], weights[side], preferred_element_type=jnp.float32)
-            product = product.reshape(ID, JD, 4 * RANK)
-            total = jnp.sum(product[:, :, :KD] * weight + product[:, :, KD:] * weight, axis=1)
-            sums.append(total)
+            pieces = jnp.concatenate([first.astype(jnp.bfloat16), second.astype(jnp.bfloat16)], axis=1)
+            block = tensor[2 * p + side].reshape(ID * JD, KD)
+            high = block.astype(jnp.bfloat16)
+            low = (block - high.astype(jnp.float32)).astype(jnp.bfloat16)
+            product = jnp.dot(
+                jnp.concatenate([high, low], axis=1),
+                jnp.concatenate([pieces, pieces], axis=0),
+                preferred_element_type=jnp.float32,
+            )
+            product = (product[:, :KD] + product[:, KD:]).reshape(ID, JD, KD) * weight
+            sums.append(jnp.sum(product.reshape(ID, JD // 8, 8, KD).sum(axis=1), axis=1))
         even = sums[0] + swap_halves(sums[0])
         odd = sums[1] + swap_halves(sums[1])
         out[p, :ID, :] = jnp.where(left, even, odd)
+
+    def step(n, carry):
+        for u in range(UNROLL):
+            pair(n * UNROLL + u)
         return carry
 
-    lax.fori_loop(0, PAIRS, step, 0)
+    lax.fori_loop(0, PAIRS // UNROLL, step, 0)
 
 
 def total_kernel(received, out):
@@ -236,17 +223,19 @@
 
 def on_device(tensor, factor_b, factor_c):
     z_shifts, line = shifts(N_Z, 2), shifts(4)
-    packed = call(pack_kernel, f32(PAIRS, 8, 2 * RANK), (factor_b[:, 0], factor_c[:, 0]))
-    xs = call(
-        split_kernel,
-        pltpu.VMEM((FIELDS, ID * JD, 2 * KD), jnp.bfloat16),
-        (tensor,),
-        specs=[ANY],
-        scratch=[pltpu.VMEM((SLOTS, ID, JD, KD), jnp.float32), pltpu.SemaphoreType.DMA((SLOTS,))],
-        vmem=24,
-        cost=pl.CostEstimate(flops=5 * tensor.size, bytes_accessed=4 * tensor.size, transcendentals=0),
+    packed = call(
+        pack_kernel,
+        f32(PAIRS, 8, 2 * RANK),
+        [pltpu.with_memory_space_constraint(f, pltpu.HBM) for f in (factor_b[:, 0], factor_c[:, 0], tensor)],
+        specs=[ANY, ANY, ANY],
+        scratch=[
+            pltpu.VMEM((FIELDS, B_OWN, RANK), jnp.float32),
+            pltpu.VMEM((FIELDS, C_OWN, RANK), jnp.float32),
+            pltpu.SemaphoreType.DMA((2,)),
+        ],
     )
     parts = around(packed, "ia", z_shifts)
+    near = pltpu.with_memory_space_constraint(tensor, pltpu.VMEM)
     b, c = call(along_z_kernel, (f32(PAIRS, 8, 2 * RANK), f32(PAIRS, 16, 2 * RANK)), parts)
     parts = around(b, "ka", line) + around(c, "ja", line)
     mine = call(along_xy_kernel, f32(PAIRS, 96, 2 * RANK), parts)
@@ -254,14 +243,9 @@
     sent = call(
         mttkrp_kernel,
         f32(PAIRS, ID + B_PART + C_PART, 2 * RANK),
-        (xs, mine, other),
-        scratch=[
-            pltpu.VMEM((JD, 2 * RANK), jnp.float32),
-            pltpu.VMEM((KD, 2 * RANK), jnp.float32),
-            pltpu.VMEM((2, 2 * KD, 4 * RANK), jnp.bfloat16),
-            pltpu.VMEM((8, 128), jnp.float32),
-        ],
-        vmem=40,
+        (near, mine, other),
+        vmem=28,
+        cost=pl.CostEstimate(flops=8 * 2 * tensor.size * RANK, bytes_accessed=4 * tensor.size, transcendentals=0),
     )
     received = lax.all_to_all(sent, ("ja", "ka"), 0, 0)
     owned = call(total_kernel, f32(ID, 2 * RANK), (received,))
@@ -270,8 +254,9 @@
         factor_kernel,
         f32(2 * RANK, 2 * RANK),
         (received,),
-        cost=pl.CostEstimate(flops=64 * 64 * 64 * 64, bytes_accessed=MIB, transcendentals=0),
-    )
+        cost=pl.CostEstimate(flops=4 * RANK**3, bytes_accessed=20 * MIB, transcendentals=0),
+    )
+    *parts, inverse = lax.optimization_barrier((*parts, inverse))
     parts = parts + [lax.ppermute(part, "ia", CORE_SWAP) for part in parts]
     sent = call(
         finish_kernel,

time: 106 us -> 79.8 us (0.75)
  Pallas kernels: 34 us -> 15.1 us
  local copies, waits for them, and re-layouts: 7.32 us -> 0.01 us
  starting transfers between devices: 25.9 us -> 22.9 us
  waiting for transfers between devices: 8.91 us -> 11.9 us
    pallas_call x9 -> x8, Pallas kernels: 34 us -> 15.1 us  [call(): pl.pallas_call(kernel, out_shape=out_shape, in_specs=[VMEM] * len(operand...]
    unnamed x6 -> x2, local copies, waits for them, and re-layouts: 7.32 us -> 0.01 us
    ppermute x4, starting transfers between devices: 6.67 us -> 3.61 us  [on_device(): parts = parts + [lax.ppermute(part, 'ia', CORE_SWAP) for part in parts]]
    ppermute x1, waiting for transfers between devices: 0.01 us -> 1.91 us  [on_device(): other = lax.ppermute(mine, 'ia', CORE_SWAP)]
    ppermute x4, waiting for transfers between devices: 0.01 us -> 1.08 us  [on_device(): parts = parts + [lax.ppermute(part, 'ia', CORE_SWAP) for part in parts]]
  transfers between devices with their start and end apart: 17 -> 17, of which waited for: 6 -> 11; matrix products, arithmetic and copies ran while one was open for 0% -> 0% of each run, Pallas kernels for 15% -> 7%
where the time goes in v2:
time: 79.8 us; the launch traced here: 79.5 us
  blocking collectives  29 us (36%)
  starting transfers between devices  22.9 us (29%)
  Pallas kernels  15.1 us (19%)
  waiting for transfers between devices  11.9 us (15%)
    all_to_all x2, blocking collectives, on_device(): received = lax.all_to_all(sent, ('ja', 'ka'), 0, 0)  29 us
    ppermute x12, starting transfers between devices, around(): return [value] + [lax.ppermute(value, axis, perm) for perm in perms]  15.1 us
    pallas_call x8, Pallas kernels, call(): pl.pallas_call(kernel, out_shape=out_shape, in_specs=[VMEM] * len(operand...  15.1 us
    ppermute x12, waiting for transfers between devices, around(): return [value] + [lax.ppermute(value, axis, perm) for perm in perms]  8.9 us
    ppermute x1, starting transfers between devices, on_device(): other = lax.ppermute(mine, 'ia', CORE_SWAP)  4.2 us
    ppermute x4, starting transfers between devices, on_device(): parts = parts + [lax.ppermute(part, 'ia', CORE_SWAP) for part in parts]  3.61 us
    ppermute x1, waiting for transfers between devices, on_device(): other = lax.ppermute(mine, 'ia', CORE_SWAP)  1.91 us
  transfers between devices with their start and end apart: 17, of which 11 were waited for; matrix products, arithmetic and copies ran while one was open for 0% of the time, Pallas kernels for 7%

profile of v2, /device:TPU:1, one launch (start us, length us, event | category | flops | bytes accessed | tf_op | source)
XLA Modules:
  0.0 79.5 jit_solution(14237631250172508516)
XLA Ops:
  0.6 1.1 %shard_map.50.m0 = f32[16,8,128]{2,1,0:T(8,128)S(1)} custom-call(f32[32,2,64]{2,1,0:T(2,128)} %bitcast.3, f32[32,4,64]{2,1,0:T(4,128)} %bitcast.2, f32[32,16,64,128]{3,2,1,0:T(8,128)} %tensor.3), custom_call_target="tpu_custom_call" | custom-call | tf_op jit(solution)/shard_map/pallas_call | solution.py:28
  1.8 4.7 %collective-permute-start.2 = (f32[16,8,128]{2,1,0:T(8,128)S(1)}, f32[16,8,128]{2,1,0:T(8,128)S(1)}, u32[]{:S(2)}, u32[]{:S(2)}) collective-permute-start(f32[16,8,128]{2,1,0:T(8,128)S(1)} %shard_map.50.m0), channel_id=1, source_target_pairs={{0,96},{16,112},{32,0},{48,16},{64,32},{80,48},{96,64},{112,80},{1... | collective-permute-start | bytes 196616 | tf_op jit(solution)/shard_map/ppermute | solution.py:221
  6.4 0.7 collective-permute-start
  7.1 0.6 collective-permute-done.2.m3
  7.8 3.4 %collective-permute-done.1.m2 = f32[16,8,128]{2,1,0:T(8,128)S(1)} collective-permute-done((f32[16,8,128]{2,1,0:T(8,128)S(1)}, f32[16,8,128]{2,1,0:T(8,128)S(1)}, u32[]{:S(2)}, u32[]{:S(2)}) %collective-permute-start.1) | collective-permute-done | bytes 65568 | tf_op jit(solution)/shard_map/ppermute | solution.py:221
  11.2 0.3 collective-permute-done.m1
  11.5 2.8 %collective-permute-start.5 = (f32[16,8,128]{2,1,0:T(8,128)S(1)}, f32[16,8,128]{2,1,0:T(8,128)S(1)}, u32[]{:S(2)}, u32[]{:S(2)}) collective-permute-start(f32[16,8,128]{2,1,0:T(8,128)S(1)} %get-tuple-element.9.b0), channel_id=1, source_target_pairs={{0,3},{1,0},{2,1},{3,2},{4,7},{5,4},{6,5},{7,6},{8,11},{9,8},{10,9... | collective-permute-start | bytes 196616 | tf_op jit(solution)/shard_map/ppermute | solution.py:221
  14.3 2.5 %collective-permute-start.8 = (f32[16,16,128]{2,1,0:T(8,128)S(1)}, f32[16,16,128]{2,1,0:T(8,128)S(1)}, u32[]{:S(2)}, u32[]{:S(2)}) collective-permute-start(f32[16,16,128]{2,1,0:T(8,128)S(1)} %get-tuple-element.10.c0), channel_id=1, source_target_pairs={{0,12},{4,0},{8,4},{12,8},{1,13},{5,1},{9,5},{13,9},{2,14},{6,2},{... | collective-permute-start | bytes 393224 | tf_op jit(solution)/shard_map/ppermute | solution.py:221
  16.8 0.5 collective-permute-start.7
  17.3 0.6 collective-permute-start.6
  17.9 0.3 collective-permute-start.4
  18.3 0.7 collective-permute-start.3
  19.0 3.6 %collective-permute-done.4.b2 = f32[16,8,128]{2,1,0:T(8,128)S(1)} collective-permute-done((f32[16,8,128]{2,1,0:T(8,128)S(1)}, f32[16,8,128]{2,1,0:T(8,128)S(1)}, u32[]{:S(2)}, u32[]{:S(2)}) %collective-permute-start.4) | collective-permute-done | bytes 65568 | tf_op jit(solution)/shard_map/ppermute | solution.py:221
  22.6 0.6 collective-permute-done.3.b1
  23.2 0.3 collective-permute-done.6.c1
  23.7 4.2 %collective-permute-start.9 = (f32[16,96,128]{2,1,0:T(8,128)S(1)}, f32[16,96,128]{2,1,0:T(8,128)S(1)}, u32[]{:S(2)}, u32[]{:S(2)}) collective-permute-start(f32[16,96,128]{2,1,0:T(8,128)S(1)} %shard_map.52.mine), channel_id=1, source_target_pairs={{0,16},{16,0},{32,48},{48,32},{64,80},{80,64},{96,112},{112,96},{1... | collective-permute-start | bytes 2359304 | tf_op jit(solution)/shard_map/ppermute | solution.py:242
  27.9 1.9 %collective-permute-done.9.other = f32[16,96,128]{2,1,0:T(8,128)S(1)} collective-permute-done((f32[16,96,128]{2,1,0:T(8,128)S(1)}, f32[16,96,128]{2,1,0:T(8,128)S(1)}, u32[]{:S(2)}, u32[]{:S(2)}) %collective-permute-start.9) | collective-permute-done | bytes 786464 | tf_op jit(solution)/shard_map/ppermute | solution.py:242
  29.8 5.7 %shard_map.53 = f32[16,64,128]{2,1,0:T(8,128)S(1)} custom-call(f32[32,16,64,128]{3,2,1,0:T(8,128)S(1)} %copy-done, f32[16,96,128]{2,1,0:T(8,128)S(1)} %shard_map.52.mine, f32[16,96,128]{2,1,0:T(8,128)S(1)} %collective-permute-done.9.other), custom_call_target="tpu_custom_call" | custom-call | flops 4294967296 | bytes 16777216 | tf_op jit(solution)/shard_map/pallas_call | solution.py:28
  35.5 14.4 %all_to_all.10.received = f32[16,64,128]{2,1,0:T(8,128)S(1)} all-to-all(f32[16,64,128]{2,1,0:T(8,128)S(1)} %shard_map.53), channel_id=1, replica_groups=mesh['ia'=8,'ja'=4,'ka'=4] {'ja','ka'}, dimensions={0} | all-to-all | bytes 1048576 | tf_op jit(solution)/shard_map/all_to_all | solution.py:250
  49.9 0.6 collective-permute-start.12
  50.5 0.9 %collective-permute-start.11 = (f32[16,128]{1,0:T(8,128)S(1)}, f32[16,128]{1,0:T(8,128)S(1)}, u32[]{:S(2)}, u32[]{:S(2)}) collective-permute-start(f32[16,128]{1,0:T(8,128)S(1)} %shard_map.54.w0), channel_id=1, source_target_pairs={{0,64},{16,80},{32,96},{48,112},{64,0},{80,16},{96,32},{112,48},{1... | collective-permute-start | bytes 24584 | tf_op jit(solution)/shard_map/ppermute | solution.py:221
  51.4 0.8 collective-permute-start.10
  52.2 5.9 %shard_map.55.inverse = f32[128,128]{1,0:T(8,128)S(1)} custom-call(f32[16,64,128]{2,1,0:T(8,128)S(1)} %all_to_all.10.received), custom_call_target="tpu_custom_call" | custom-call | flops 1048576 | bytes 20971520 | tf_op jit(solution)/shard_map/pallas_call | solution.py:28
  58.1 3.0 %collective-permute-start.13 = (f32[16,128]{1,0:T(8,128)S(1)}, f32[16,128]{1,0:T(8,128)S(1)}, u32[]{:S(2)}, u32[]{:S(2)}) collective-permute-start(f32[16,128]{1,0:T(8,128)S(1)} %shard_map.54.w0), channel_id=1, source_target_pairs={{0,16},{16,0},{32,48},{48,32},{64,80},{80,64},{96,112},{112,96},{1... | collective-permute-start | bytes 24584 | tf_op jit(solution)/shard_map/ppermute | solution.py:260
  61.2 0.4 collective-permute-start.15
  61.7 0.2 collective-permute-done.13.v0
  62.0 0.3 collective-permute-done.14.v1
  62.3 0.2 collective-permute-done.15.v2
  62.5 0.3 collective-permute-done.16.v3
  62.8 0.9 %shard_map.56 = f32[16,72,128]{2,1,0:T(8,128)S(1)} custom-call(f32[16,128]{1,0:T(8,128)S(1)} %shard_map.54.w0, f32[16,128]{1,0:T(8,128)S(1)} %collective-permute-done.10.w1, f32[16,128]{1,0:T(8,128)S(1)} %collective-permute-done.11.w2, f32[16,128]{1,0:T(8,128)S(1)} %collective-permute-done.12.w3, f32[16,128]{1,0:T(8,128)S(1)} %collective-permute-done.13.v0, ...), custom_call_target="tpu_custom_call" | custom-call | tf_op jit(solution)/shard_map/pallas_call | solution.py:28
  63.7 14.7 %all_to_all.11.received = f32[16,72,128]{2,1,0:T(8,128)S(1)} all-to-all(f32[16,72,128]{2,1,0:T(8,128)S(1)} %shard_map.56), channel_id=1, replica_groups=mesh['ia'=8,'ja'=4,'ka'=4] {'ja','ka'}, dimensions={0} | all-to-all | bytes 1179648 | tf_op jit(solution)/shard_map/all_to_all | solution.py:267
  78.3 1.2 %shard_map.57 = (f32[32,1,1,64]{3,2,1,0:T(1,128)}, f32[32,64,64]{2,1,0:T(8,128)}) custom-call(f32[16,72,128]{2,1,0:T(8,128)S(1)} %all_to_all.11.received), custom_call_target="tpu_custom_call" | custom-call | tf_op jit(solution)/shard_map/pallas_call | solution.py:28
  (14 shorter events, 0.4 us)
Async XLA Ops:
  0.6 29.2 %copy-start = (f32[32,16,64,128]{3,2,1,0:T(8,128)S(1)}, f32[32,16,64,128]{3,2,1,0:T(8,128)}, u32[]{:S(2)}) copy-start(f32[32,16,64,128]{3,2,1,0:T(8,128)} %tensor.3) | copy-start | bytes 50331652
  1.8 6.0 %collective-permute-start.2 = (f32[16,8,128]{2,1,0:T(8,128)S(1)}, f32[16,8,128]{2,1,0:T(8,128)S(1)}, u32[]{:S(2)}, u32[]{:S(2)}) collective-permute-start(f32[16,8,128]{2,1,0:T(8,128)S(1)} %shard_map.50.m0), channel_id=1, source_target_pairs={{0,96},{16,112},{32,0},{48,16},{64,32},{80,48},{96,64},{112,80},{1... | collective-permute-start | bytes 196616 | tf_op jit(solution)/shard_map/ppermute | solution.py:221
  6.4 4.7 %collective-permute-start.1 = (f32[16,8,128]{2,1,0:T(8,128)S(1)}, f32[16,8,128]{2,1,0:T(8,128)S(1)}, u32[]{:S(2)}, u32[]{:S(2)}) collective-permute-start(f32[16,8,128]{2,1,0:T(8,128)S(1)} %shard_map.50.m0), channel_id=1, source_target_pairs={{0,64},{16,80},{32,96},{48,112},{64,0},{80,16},{96,32},{112,48},{1... | collective-permute-start | bytes 196616 | tf_op jit(solution)/shard_map/ppermute | solution.py:221
  6.4 5.0 %collective-permute-start = (f32[16,8,128]{2,1,0:T(8,128)S(1)}, f32[16,8,128]{2,1,0:T(8,128)S(1)}, u32[]{:S(2)}, u32[]{:S(2)}) collective-permute-start(f32[16,8,128]{2,1,0:T(8,128)S(1)} %shard_map.50.m0), channel_id=1, source_target_pairs={{0,32},{16,48},{32,64},{48,80},{64,96},{80,112},{96,0},{112,16},{1... | collective-permute-start | bytes 196616 | tf_op jit(solution)/shard_map/ppermute | solution.py:221
  11.5 6.8 %collective-permute-start.5 = (f32[16,8,128]{2,1,0:T(8,128)S(1)}, f32[16,8,128]{2,1,0:T(8,128)S(1)}, u32[]{:S(2)}, u32[]{:S(2)}) collective-permute-start(f32[16,8,128]{2,1,0:T(8,128)S(1)} %get-tuple-element.9.b0), channel_id=1, source_target_pairs={{0,3},{1,0},{2,1},{3,2},{4,7},{5,4},{6,5},{7,6},{8,11},{9,8},{10,9... | collective-permute-start | bytes 196616 | tf_op jit(solution)/shard_map/ppermute | solution.py:221
  14.3 8.9 %collective-permute-start.8 = (f32[16,16,128]{2,1,0:T(8,128)S(1)}, f32[16,16,128]{2,1,0:T(8,128)S(1)}, u32[]{:S(2)}, u32[]{:S(2)}) collective-permute-start(f32[16,16,128]{2,1,0:T(8,128)S(1)} %get-tuple-element.10.c0), channel_id=1, source_target_pairs={{0,12},{4,0},{8,4},{12,8},{1,13},{5,1},{9,5},{13,9},{2,14},{6,2},{... | collective-permute-start | bytes 393224 | tf_op jit(solution)/shard_map/ppermute | solution.py:221
  16.8 6.5 %collective-permute-start.7 = (f32[16,16,128]{2,1,0:T(8,128)S(1)}, f32[16,16,128]{2,1,0:T(8,128)S(1)}, u32[]{:S(2)}, u32[]{:S(2)}) collective-permute-start(f32[16,16,128]{2,1,0:T(8,128)S(1)} %get-tuple-element.10.c0), channel_id=1, source_target_pairs={{0,8},{4,12},{8,0},{12,4},{1,9},{5,13},{9,1},{13,5},{2,10},{6,14},... | collective-permute-start | bytes 393224 | tf_op jit(solution)/shard_map/ppermute | solution.py:221
  17.3 6.2 %collective-permute-start.6 = (f32[16,16,128]{2,1,0:T(8,128)S(1)}, f32[16,16,128]{2,1,0:T(8,128)S(1)}, u32[]{:S(2)}, u32[]{:S(2)}) collective-permute-start(f32[16,16,128]{2,1,0:T(8,128)S(1)} %get-tuple-element.10.c0), channel_id=1, source_target_pairs={{0,4},{4,8},{8,12},{12,0},{1,5},{5,9},{9,13},{13,1},{2,6},{6,10},{... | collective-permute-start | bytes 393224 | tf_op jit(solution)/shard_map/ppermute | solution.py:221
  17.9 4.7 %collective-permute-start.4 = (f32[16,8,128]{2,1,0:T(8,128)S(1)}, f32[16,8,128]{2,1,0:T(8,128)S(1)}, u32[]{:S(2)}, u32[]{:S(2)}) collective-permute-start(f32[16,8,128]{2,1,0:T(8,128)S(1)} %get-tuple-element.9.b0), channel_id=1, source_target_pairs={{0,2},{1,3},{2,0},{3,1},{4,6},{5,7},{6,4},{7,5},{8,10},{9,11},{10,... | collective-permute-start | bytes 196616 | tf_op jit(solution)/shard_map/ppermute | solution.py:221
  18.3 5.0 %collective-permute-start.3 = (f32[16,8,128]{2,1,0:T(8,128)S(1)}, f32[16,8,128]{2,1,0:T(8,128)S(1)}, u32[]{:S(2)}, u32[]{:S(2)}) collective-permute-start(f32[16,8,128]{2,1,0:T(8,128)S(1)} %get-tuple-element.9.b0), channel_id=1, source_target_pairs={{0,1},{1,2},{2,3},{3,0},{4,5},{5,6},{6,7},{7,4},{8,9},{9,10},{10,1... | collective-permute-start | bytes 196616 | tf_op jit(solution)/shard_map/ppermute | solution.py:221
  23.7 6.1 %collective-permute-start.9 = (f32[16,96,128]{2,1,0:T(8,128)S(1)}, f32[16,96,128]{2,1,0:T(8,128)S(1)}, u32[]{:S(2)}, u32[]{:S(2)}) collective-permute-start(f32[16,96,128]{2,1,0:T(8,128)S(1)} %shard_map.52.mine), channel_id=1, source_target_pairs={{0,16},{16,0},{32,48},{48,32},{64,80},{80,64},{96,112},{112,96},{1... | collective-permute-start | bytes 2359304 | tf_op jit(solution)/shard_map/ppermute | solution.py:242
  49.9 8.2 %collective-permute-start.12 = (f32[16,128]{1,0:T(8,128)S(1)}, f32[16,128]{1,0:T(8,128)S(1)}, u32[]{:S(2)}, u32[]{:S(2)}) collective-permute-start(f32[16,128]{1,0:T(8,128)S(1)} %shard_map.54.w0), channel_id=1, source_target_pairs={{0,96},{16,112},{32,0},{48,16},{64,32},{80,48},{96,64},{112,80},{1... | collective-permute-start | bytes 24584 | tf_op jit(solution)/shard_map/ppermute | solution.py:221
  50.5 7.6 %collective-permute-start.11 = (f32[16,128]{1,0:T(8,128)S(1)}, f32[16,128]{1,0:T(8,128)S(1)}, u32[]{:S(2)}, u32[]{:S(2)}) collective-permute-start(f32[16,128]{1,0:T(8,128)S(1)} %shard_map.54.w0), channel_id=1, source_target_pairs={{0,64},{16,80},{32,96},{48,112},{64,0},{80,16},{96,32},{112,48},{1... | collective-permute-start | bytes 24584 | tf_op jit(solution)/shard_map/ppermute | solution.py:221
  51.4 6.7 %collective-permute-start.10 = (f32[16,128]{1,0:T(8,128)S(1)}, f32[16,128]{1,0:T(8,128)S(1)}, u32[]{:S(2)}, u32[]{:S(2)}) collective-permute-start(f32[16,128]{1,0:T(8,128)S(1)} %shard_map.54.w0), channel_id=1, source_target_pairs={{0,32},{16,48},{32,64},{48,80},{64,96},{80,112},{96,0},{112,16},{1... | collective-permute-start | bytes 24584 | tf_op jit(solution)/shard_map/ppermute | solution.py:221
  58.1 3.8 %collective-permute-start.13 = (f32[16,128]{1,0:T(8,128)S(1)}, f32[16,128]{1,0:T(8,128)S(1)}, u32[]{:S(2)}, u32[]{:S(2)}) collective-permute-start(f32[16,128]{1,0:T(8,128)S(1)} %shard_map.54.w0), channel_id=1, source_target_pairs={{0,16},{16,0},{32,48},{48,32},{64,80},{80,64},{96,112},{112,96},{1... | collective-permute-start | bytes 24584 | tf_op jit(solution)/shard_map/ppermute | solution.py:260
  61.1 1.2 %collective-permute-start.14 = (f32[16,128]{1,0:T(8,128)S(1)}, f32[16,128]{1,0:T(8,128)S(1)}, u32[]{:S(2)}, u32[]{:S(2)}) collective-permute-start(f32[16,128]{1,0:T(8,128)S(1)} %collective-permute-done.10.w1), channel_id=1, source_target_pairs={{0,16},{16,0},{32,48},{48,32},{64,80},{80,64},{96,112},{112,96},{1... | collective-permute-start | bytes 24584 | tf_op jit(solution)/shard_map/ppermute | solution.py:260
  61.2 1.2 %collective-permute-start.15 = (f32[16,128]{1,0:T(8,128)S(1)}, f32[16,128]{1,0:T(8,128)S(1)}, u32[]{:S(2)}, u32[]{:S(2)}) collective-permute-start(f32[16,128]{1,0:T(8,128)S(1)} %collective-permute-done.11.w2), channel_id=1, source_target_pairs={{0,16},{16,0},{32,48},{48,32},{64,80},{80,64},{96,112},{112,96},{1... | collective-permute-start | bytes 24584 | tf_op jit(solution)/shard_map/ppermute | solution.py:260
  61.7 1.2 %collective-permute-start.16 = (f32[16,128]{1,0:T(8,128)S(1)}, f32[16,128]{1,0:T(8,128)S(1)}, u32[]{:S(2)}, u32[]{:S(2)}) collective-permute-start(f32[16,128]{1,0:T(8,128)S(1)} %collective-permute-done.12.w3), channel_id=1, source_target_pairs={{0,16},{16,0},{32,48},{48,32},{64,80},{80,64},{96,112},{112,96},{1... | collective-permute-start | bytes 24584 | tf_op jit(solution)/shard_map/ppermute | solution.py:260

commit v3 on v2

v3 whole, which is shorter than its diff:
```python
import jax
import jax.numpy as jnp
from jax import lax
from jax.experimental import pallas as pl
from jax.experimental.pallas import tpu as pltpu
from jax.sharding import Mesh
from jax.sharding import PartitionSpec as P

FIELDS, RANK = 32, 64
PAIRS = FIELDS // 2
ID, JD, KD = 16, 64, 128
N_IA, N_JA, N_KA = 8, 4, 4
N_Z = N_IA // 2
B_OWN = JD // (N_IA * N_KA)
C_OWN = KD // (N_IA * N_JA)
I_ALL = N_IA * ID
OWNERS = PAIRS * 2
HIGH = lax.Precision.HIGHEST
MIB = 1024 * 1024
VMEM = pl.BlockSpec(memory_space=pltpu.VMEM)
ANY = pl.BlockSpec(memory_space=pl.ANY)
PANEL = 16
UNROLL = 4


def call(kernel, out_shape, operands, *, specs=None, scratch=(), vmem=16, cost=None):
    return pl.pallas_call(
        kernel,
        out_shape=out_shape,
        in_specs=[VMEM] * len(operands) if specs is None else specs,
        out_specs=jax.tree.map(lambda _: VMEM, out_shape),
        scratch_shapes=list(scratch),
        cost_estimate=cost,
        compiler_params=pltpu.CompilerParams(vmem_limit_bytes=vmem * MIB),
    )(*operands)


def f32(*shape):
    return jax.ShapeDtypeStruct(shape, jnp.float32)


def place():
    return tuple(lax.axis_index(axis) for axis in ("z", "core", "ja", "ka"))


def pack_kernel(b_hbm, c_hbm, tensor, out, b, c, sems):
    copies = [pltpu.make_async_copy(b_hbm, b, sems.at[0]), pltpu.make_async_copy(c_hbm, c, sems.at[1])]
    for copy in copies:
        copy.start()
    for copy in copies:
        copy.wait()
    for p in range(PAIRS):
        for side in range(2):
            lanes = slice(side * RANK, (side + 1) * RANK)
            out[p, 0:B_OWN, lanes] = b[2 * p + side]
            out[p, B_OWN : B_OWN + C_OWN, lanes] = c[2 * p + side]
        out[p, B_OWN + C_OWN :, :] = jnp.zeros((8 - B_OWN - C_OWN, 2 * RANK), jnp.float32)


def in_order(pieces, first, rows):
    n = len(pieces)
    rising = jnp.concatenate([pieces[-t % n] for t in range(n)], axis=0)
    return pltpu.roll(rising, first * rows, 0)


def swap_halves(v):
    return pltpu.roll(v, RANK, 1)


def fold(v):
    half = v.shape[0] // 2
    lane = lax.broadcasted_iota(jnp.int32, (1, 2 * RANK), 1)
    return jnp.where(lane < RANK, v[:half], swap_halves(v[half:]))


def along_z_kernel(m0, m1, m2, m3, b, c):
    z, _, _, _ = place()
    parts = (m0, m1, m2, m3)
    for p in range(PAIRS):
        b[p] = in_order([m[p, :B_OWN, :] for m in parts], z, B_OWN)
        c[p] = in_order([m[p, B_OWN : B_OWN + C_OWN, :] for m in parts], z, C_OWN)


def along_xy_kernel(b0, b1, b2, b3, c0, c1, c2, c3, out):
    _, _, x, y = place()
    for p in range(PAIRS):
        for z in range(N_Z):
            rows = slice(z * B_OWN, (z + 1) * B_OWN)
            n = B_OWN * N_KA
            out[p, z * n : (z + 1) * n, :] = in_order([b[p, rows, :] for b in (b0, b1, b2, b3)], y, B_OWN)
        for z in range(N_Z):
            rows = slice(z * C_OWN, (z + 1) * C_OWN)
            n = C_OWN * N_JA
            at = JD // 2 + z * n
            out[p, at : at + n, :] = in_order([c[p, rows, :] for c in (c0, c1, c2, c3)], x, C_OWN)


def mttkrp_kernel(tensor, mine, other, out):
    _, core, x, y = place()
    lane = lax.broadcasted_iota(jnp.int32, (1, 2 * RANK), 1)
    left = lane < RANK
    first_core = core == 0
    nb, nc = B_OWN * N_KA, C_OWN * N_JA

    def both(p, at, rows):
        here, there = mine[p, pl.ds(at, rows), :], other[p, pl.ds(at, rows), :]
        return [jnp.where(first_core, here, there), jnp.where(first_core, there, here)]

    def pair(p):
        b = jnp.concatenate([part for z in range(N_Z) for part in both(p, z * nb, nb)], axis=0)
        c = jnp.concatenate([part for z in range(N_Z) for part in both(p, JD // 2 + z * nc, nc)], axis=0)
        part_b = mine[p, pl.ds(pl.multiple_of(y * nb, nb), nb), :]
        part_c = mine[p, pl.ds(pl.multiple_of(JD // 2 + x * nc, nc), nc), :]
        for side in range(2):
            d = side * PAIRS + p
            out[d, 8:16, :] = fold(swap_halves(part_c) if side else part_c)
            part = fold(swap_halves(part_b) if side else part_b)
            out[d, 16:24, :] = jnp.concatenate([part, jnp.zeros_like(part)], axis=0)
        c1 = c.astype(jnp.bfloat16).astype(jnp.float32)
        c2 = (c - c1).astype(jnp.bfloat16).astype(jnp.float32)
        c3 = c - c1 - c2
        for side in range(2):
            if side == 0:
                first = jnp.where(left, c1, swap_halves(c2))
                second = jnp.where(left, c3, 0.0)
                weight = jnp.where(left, b, swap_halves(b))
            else:
                first = jnp.where(left, swap_halves(c1), c2)
                second = jnp.where(left, swap_halves(c3), 0.0)
                weight = jnp.where(left, swap_halves(b), b)
            pieces = jnp.concatenate([first.astype(jnp.bfloat16), second.astype(jnp.bfloat16)], axis=1)
            block = tensor[2 * p + side].reshape(ID * JD, KD)
            high = block.astype(jnp.bfloat16)
            low = (block - high.astype(jnp.float32)).astype(jnp.bfloat16)
            product = jnp.dot(
                jnp.concatenate([high, low], axis=1),
                jnp.concatenate([pieces, pieces], axis=0),
                preferred_element_type=jnp.float32,
            )
            product = (product[:, :KD] + product[:, KD:]).reshape(ID, JD, KD) * weight
            total = jnp.sum(product.reshape(ID, JD // 8, 8, KD).sum(axis=1), axis=1)
            out[side * PAIRS + p, :8, :] = fold(total + swap_halves(total))

    def step(n, carry):
        for u in range(UNROLL):
            pair(n * UNROLL + u)
        return carry

    lax.fori_loop(0, PAIRS // UNROLL, step, 0)


def total_kernel(received, out):
    for core in range(2):
        total = received[core * PAIRS, :8, :]
        for s in range(1, PAIRS):
            total = total + received[core * PAIRS + s, :8, :]
        out[8 * core : 8 * core + 8, :] = total


def rows_gram(rows):
    both = lax.dot_general(rows, rows, (((0,), (0,)), ((), ())), precision=HIGH, preferred_element_type=jnp.float32)
    return both[:RANK] + swap_halves(both[RANK:])


def factor_kernel(received, out):
    gram = rows_gram(received[:, 16:20, :].reshape(OWNERS * 4, 2 * RANK))
    gram = gram * rows_gram(received[:, 8:16, :].reshape(OWNERS * 8, 2 * RANK))
    lane = lax.broadcasted_iota(jnp.int32, (RANK, 2 * RANK), 1)
    row = lax.broadcasted_iota(jnp.int32, (RANK, 2 * RANK), 0)
    whole = jnp.where(lane < RANK, gram, jnp.where(lane == row + RANK, 1.0, 0.0))
    n = RANK // PANEL
    panels = [whole[PANEL * t : PANEL * (t + 1)] for t in range(n)]
    sub = lax.broadcasted_iota(jnp.int32, (PANEL, 2 * RANK), 0)
    for t in range(n):
        panel = panels[t]
        columns = [
            jnp.broadcast_to(panel[:, PANEL * t + j : PANEL * t + j + 1], panel.shape) for j in range(PANEL)
        ]
        inverses = []
        for k in range(PANEL):
            inverses.append(1.0 / columns[k][k : k + 1, :])
            if k == PANEL - 1:
                break
            first = (k + 1) // 8 * 8
            factor = jnp.where(sub[first:] > k, columns[k][first:], 0.0) * inverses[k]

            def eliminate(v):
                low = v[first:] - factor * v[k : k + 1, :]
                return jnp.concatenate([v[:first], low], axis=0) if first else low

            for j in range(k + 1, PANEL):
                columns[j] = eliminate(columns[j])
            panel = eliminate(panel)
        panels[t] = panel
        if t < n - 1:
            factors = jnp.transpose(panel * jnp.concatenate(inverses, axis=0))
            for u in range(t + 1, n):
                rest = panels[u]
                for k in range(PANEL):
                    rest = rest - factors[PANEL * u : PANEL * (u + 1), k : k + 1] * panel[k : k + 1, :]
                panels[u] = rest
    whole = jnp.concatenate(panels, axis=0)
    pivots = jnp.sum(jnp.where(lane == row, whole, 0.0), axis=1, keepdims=True)
    inverse = jnp.where(lane >= RANK, whole * lax.rsqrt(pivots), 0.0)
    out[:RANK, :] = swap_halves(inverse)
    out[RANK:, :] = inverse


def finish_kernel(w0, w1, w2, w3, inverse, out, every, rows):
    z, _, _, _ = place()
    for s, part in enumerate((w0, w1, w2, w3)):
        at = lax.rem(z - s + N_Z, N_Z) * 16
        every[pl.ds(pl.multiple_of(at, 16), 16), :] = part[...]
    inv = inverse[...]
    half = lax.dot_general(every[...], inv, (((1,), (1,)), ((), ())), precision=HIGH, preferred_element_type=jnp.float32)
    solved = jnp.dot(half, inv, precision=HIGH, preferred_element_type=jnp.float32)
    rows[...] = solved
    gram = fold(rows_gram(solved) * (1.0 / I_ALL))
    own = rows[pl.ds(pl.multiple_of(z * 16, 16), 16), :]
    for core in range(2):
        for q in range(ID):
            out[core * PAIRS + q, : RANK // 2, :] = gram
            row = core * 8 + q % 8
            out[core * PAIRS + q, RANK // 2 :, :] = jnp.broadcast_to(own[row : row + 1], (8, 2 * RANK))


def unpack_kernel(received, rows, gram):
    _, _, x, y = place()
    upper = x * N_KA + y >= 8
    half = RANK // 2
    for p in range(PAIRS):
        for side in range(2):
            source = side * PAIRS + p
            gram[2 * p + side, :half] = received[source, :half, :RANK]
            gram[2 * p + side, half:] = received[source, :half, RANK:]
            row = received[source, half : half + 1, :]
            rows[2 * p + side, 0] = jnp.where(upper, row[:, RANK:], row[:, :RANK])


LINE = [[(i, (i + s) % 4) for i in range(4)] for s in range(1, 4)]


def around(value, axis):
    return [value] + [lax.ppermute(value, axis, perm) for perm in LINE]


def on_device(tensor, factor_b, factor_c):
    packed = call(
        pack_kernel,
        f32(PAIRS, 8, 2 * RANK),
        [pltpu.with_memory_space_constraint(f, pltpu.HBM) for f in (factor_b[:, 0], factor_c[:, 0], tensor)],
        specs=[ANY, ANY, ANY],
        scratch=[
            pltpu.VMEM((FIELDS, B_OWN, RANK), jnp.float32),
            pltpu.VMEM((FIELDS, C_OWN, RANK), jnp.float32),
            pltpu.SemaphoreType.DMA((2,)),
        ],
    )
    parts = around(packed, "z")
    near = pltpu.with_memory_space_constraint(tensor, pltpu.VMEM)
    b, c = call(along_z_kernel, (f32(PAIRS, 8, 2 * RANK), f32(PAIRS, 16, 2 * RANK)), parts)
    parts = around(b, "ka") + around(c, "ja")
    mine = call(along_xy_kernel, f32(PAIRS, 96, 2 * RANK), parts)
    other = lax.ppermute(mine, "core", [(0, 1), (1, 0)])
    sent = call(
        mttkrp_kernel,
        f32(OWNERS, 24, 2 * RANK),
        (near, mine, other),
        vmem=28,
        cost=pl.CostEstimate(flops=8 * 2 * tensor.size * RANK, bytes_accessed=4 * tensor.size, transcendentals=0),
    )
    received = lax.all_to_all(sent, ("core", "ja", "ka"), 0, 0)
    owned = call(total_kernel, f32(16, 2 * RANK), (received,))
    parts = around(owned, "z")
    inverse = call(
        factor_kernel,
        f32(2 * RANK, 2 * RANK),
        (received,),
        cost=pl.CostEstimate(flops=4 * RANK**3, bytes_accessed=10 * MIB, transcendentals=0),
    )
    sent = call(
        finish_kernel,
        f32(OWNERS, RANK // 2 + 8, 2 * RANK),
        (*parts, inverse),
        scratch=[pltpu.VMEM((I_ALL // 2, 2 * RANK), jnp.float32)] * 2,
    )
    received = lax.all_to_all(sent, ("core", "ja", "ka"), 0, 0)
    rows, gram = call(unpack_kernel, (f32(FIELDS, 1, 1, RANK), f32(FIELDS, RANK, RANK)), (received,))
    return rows, gram


def solution(mesh):
    return jax.shard_map(
        on_device,
        mesh=Mesh(mesh.devices.reshape(N_Z, 2, N_JA, N_KA), ("z", "core", "ja", "ka")),
        in_specs=(
            P(None, ("z", "core"), "ja", "ka"),
            P(None, "ja", ("z", "core", "ka"), None),
            P(None, "ka", ("z", "core", "ja"), None),
        ),
        out_specs=(P(None, ("z", "core"), ("ja", "ka"), None), P()),
        check_vma=False,
    )
```

time: 79.8 us -> 76 us (0.952)
  starting transfers between devices: 22.9 us -> 19.3 us
  blocking collectives: 29 us -> 32.4 us
  Pallas kernels: 15.1 us -> 12 us
    ppermute x17 -> x13, starting transfers between devices: 22.9 us -> 19.3 us  [the longest x12 15.1 us: around(): return [value] + [lax.ppermute(value, axis, perm) for perm in LINE]]
    all_to_all x2, blocking collectives: 29 us -> 32.4 us  [on_device(): received = lax.all_to_all(sent, ('core', 'ja', 'ka'), 0, 0)]
    pallas_call x8, Pallas kernels: 15.1 us -> 12 us  [call(): pl.pallas_call(kernel, out_shape=out_shape, in_specs=[VMEM] * len(operand...]
    ppermute x17 -> x13, waiting for transfers between devices: 11.9 us -> 11.4 us  [the longest x12 9.54 us: around(): return [value] + [lax.ppermute(value, axis, perm) for perm in LINE]]
  transfers between devices with their start and end apart: 17 -> 13, of which waited for: 11 -> 9; matrix products, arithmetic and copies ran while one was open for 0% -> 0% of each run, Pallas kernels for 7% -> 3%
where the time goes in v3:
time: 76 us; the launch traced here: 75.8 us
  blocking collectives  32.4 us (43%)
  starting transfers between devices  19.3 us (25%)
  Pallas kernels  12 us (16%)
  waiting for transfers between devices  11.4 us (15%)
    all_to_all x2, blocking collectives, on_device(): received = lax.all_to_all(sent, ('core', 'ja', 'ka'), 0, 0)  32.4 us
    ppermute x12, starting transfers between devices, around(): return [value] + [lax.ppermute(value, axis, perm) for perm in LINE]  15.1 us
    pallas_call x8, Pallas kernels, call(): pl.pallas_call(kernel, out_shape=out_shape, in_specs=[VMEM] * len(operand...  12 us
    ppermute x12, waiting for transfers between devices, around(): return [value] + [lax.ppermute(value, axis, perm) for perm in LINE]  9.54 us
    ppermute x1, starting transfers between devices, on_device(): other = lax.ppermute(mine, 'core', [(0, 1), (1, 0)])  4.2 us
    ppermute x1, waiting for transfers between devices, on_device(): other = lax.ppermute(mine, 'core', [(0, 1), (1, 0)])  1.91 us
  transfers between devices with their start and end apart: 13, of which 9 were waited for; matrix products, arithmetic and copies ran while one was open for 0% of the time, Pallas kernels for 3%

profile of v3, /device:TPU:1, one launch (start us, length us, event | category | flops | bytes accessed | tf_op | source)
XLA Modules:
  0.0 75.8 jit_solution(10334696768669461419)
XLA Ops:
  0.6 1.1 %shard_map.50.m0 = f32[16,8,128]{2,1,0:T(8,128)S(1)} custom-call(f32[32,2,64]{2,1,0:T(2,128)} %bitcast.3, f32[32,4,64]{2,1,0:T(4,128)} %bitcast.2, f32[32,16,64,128]{3,2,1,0:T(8,128)} %tensor.3), custom_call_target="tpu_custom_call" | custom-call | tf_op jit(solution)/shard_map/pallas_call | solution.py:27
  1.8 4.7 %collective-permute-start.2 = (f32[16,8,128]{2,1,0:T(8,128)S(1)}, f32[16,8,128]{2,1,0:T(8,128)S(1)}, u32[]{:S(2)}, u32[]{:S(2)}) collective-permute-start(f32[16,8,128]{2,1,0:T(8,128)S(1)} %shard_map.50.m0), channel_id=1, source_target_pairs={{0,96},{32,0},{64,32},{96,64},{1,97},{33,1},{65,33},{97,65},{2,98}... | collective-permute-start | bytes 196616 | tf_op jit(solution)/shard_map/ppermute | solution.py:244
  6.4 0.0 collective-permute-start.1
  6.4 0.7 collective-permute-start
  7.1 0.6 collective-permute-done.2.m3
  7.8 3.4 %collective-permute-done.1.m2 = f32[16,8,128]{2,1,0:T(8,128)S(1)} collective-permute-done((f32[16,8,128]{2,1,0:T(8,128)S(1)}, f32[16,8,128]{2,1,0:T(8,128)S(1)}, u32[]{:S(2)}, u32[]{:S(2)}) %collective-permute-start.1) | collective-permute-done | bytes 65568 | tf_op jit(solution)/shard_map/ppermute | solution.py:244
  11.2 0.3 collective-permute-done.m1
  11.5 2.8 %collective-permute-start.5 = (f32[16,8,128]{2,1,0:T(8,128)S(1)}, f32[16,8,128]{2,1,0:T(8,128)S(1)}, u32[]{:S(2)}, u32[]{:S(2)}) collective-permute-start(f32[16,8,128]{2,1,0:T(8,128)S(1)} %get-tuple-element.4.b0), channel_id=1, source_target_pairs={{0,3},{1,0},{2,1},{3,2},{4,7},{5,4},{6,5},{7,6},{8,11},{9,8},{10,9... | collective-permute-start | bytes 196616 | tf_op jit(solution)/shard_map/ppermute | solution.py:244
  14.3 2.5 %collective-permute-start.8 = (f32[16,16,128]{2,1,0:T(8,128)S(1)}, f32[16,16,128]{2,1,0:T(8,128)S(1)}, u32[]{:S(2)}, u32[]{:S(2)}) collective-permute-start(f32[16,16,128]{2,1,0:T(8,128)S(1)} %get-tuple-element.5.c0), channel_id=1, source_target_pairs={{0,12},{4,0},{8,4},{12,8},{1,13},{5,1},{9,5},{13,9},{2,14},{6,2},{... | collective-permute-start | bytes 393224 | tf_op jit(solution)/shard_map/ppermute | solution.py:244
  16.8 0.5 collective-permute-start.7
  17.3 0.6 collective-permute-start.6
  17.9 0.3 collective-permute-start.4
  18.3 0.0 collective-permute-done.5.b3
  18.3 0.7 collective-permute-start.3
  19.0 3.6 %collective-permute-done.4.b2 = f32[16,8,128]{2,1,0:T(8,128)S(1)} collective-permute-done((f32[16,8,128]{2,1,0:T(8,128)S(1)}, f32[16,8,128]{2,1,0:T(8,128)S(1)}, u32[]{:S(2)}, u32[]{:S(2)}) %collective-permute-start.4) | collective-permute-done | bytes 65568 | tf_op jit(solution)/shard_map/ppermute | solution.py:244
  22.6 0.6 collective-permute-done.3.b1
  23.2 0.0 collective-permute-done.8.c3
  23.2 0.3 collective-permute-done.6.c1
  23.5 0.2 shard_map.52.mine
  23.7 4.2 %collective-permute-start.9 = (f32[16,96,128]{2,1,0:T(8,128)S(1)}, f32[16,96,128]{2,1,0:T(8,128)S(1)}, u32[]{:S(2)}, u32[]{:S(2)}) collective-permute-start(f32[16,96,128]{2,1,0:T(8,128)S(1)} %shard_map.52.mine), channel_id=1, source_target_pairs={{0,16},{16,0},{1,17},{17,1},{2,18},{18,2},{3,19},{19,3},{4,20},{20... | collective-permute-start | bytes 2359304 | tf_op jit(solution)/shard_map/ppermute | solution.py:264
  27.9 1.9 %collective-permute-done.9.other = f32[16,96,128]{2,1,0:T(8,128)S(1)} collective-permute-done((f32[16,96,128]{2,1,0:T(8,128)S(1)}, f32[16,96,128]{2,1,0:T(8,128)S(1)}, u32[]{:S(2)}, u32[]{:S(2)}) %collective-permute-start.9) | collective-permute-done | bytes 786464 | tf_op jit(solution)/shard_map/ppermute | solution.py:264
  29.8 6.0 %shard_map.53 = f32[32,24,128]{2,1,0:T(8,128)S(1)} custom-call(f32[32,16,64,128]{3,2,1,0:T(8,128)S(1)} %copy-done, f32[16,96,128]{2,1,0:T(8,128)S(1)} %shard_map.52.mine, f32[16,96,128]{2,1,0:T(8,128)S(1)} %collective-permute-done.9.other), custom_call_target="tpu_custom_call" | custom-call | flops 4294967296 | bytes 16777216 | tf_op jit(solution)/shard_map/pallas_call | solution.py:27
  35.8 14.7 %all_to_all.10.received = f32[32,24,128]{2,1,0:T(8,128)S(1)} all-to-all(f32[32,24,128]{2,1,0:T(8,128)S(1)} %shard_map.53), channel_id=1, replica_groups=mesh['z'=4,'core'=2,'ja'=4,'ka'=4] {'core','ja','ka'}, dimensions={0} | all-to-all | bytes 786432 | tf_op jit(solution)/shard_map/all_to_all | solution.py:272
  50.5 0.6 collective-permute-start.12
  51.2 0.9 %collective-permute-start.11 = (f32[16,128]{1,0:T(8,128)S(1)}, f32[16,128]{1,0:T(8,128)S(1)}, u32[]{:S(2)}, u32[]{:S(2)}) collective-permute-start(f32[16,128]{1,0:T(8,128)S(1)} %shard_map.54.w0), channel_id=1, source_target_pairs={{0,64},{32,96},{64,0},{96,32},{1,65},{33,97},{65,1},{97,33},{2,66}... | collective-permute-start | bytes 24584 | tf_op jit(solution)/shard_map/ppermute | solution.py:244
  52.0 0.8 %collective-permute-start.10 = (f32[16,128]{1,0:T(8,128)S(1)}, f32[16,128]{1,0:T(8,128)S(1)}, u32[]{:S(2)}, u32[]{:S(2)}) collective-permute-start(f32[16,128]{1,0:T(8,128)S(1)} %shard_map.54.w0), channel_id=1, source_target_pairs={{0,32},{32,64},{64,96},{96,0},{1,33},{33,65},{65,97},{97,1},{2,34}... | collective-permute-start | bytes 24584 | tf_op jit(solution)/shard_map/ppermute | solution.py:244
  52.8 2.3 %shard_map.55.inverse = f32[128,128]{1,0:T(8,128)S(1)} custom-call(f32[32,24,128]{2,1,0:T(8,128)S(1)} %all_to_all.10.received), custom_call_target="tpu_custom_call" | custom-call | flops 1048576 | bytes 10485760 | tf_op jit(solution)/shard_map/pallas_call | solution.py:27
  55.1 0.1 collective-permute-done.11.w2
  55.2 0.6 collective-permute-done.10.w1
  55.7 1.0 %shard_map.56 = f32[32,40,128]{2,1,0:T(8,128)S(1)} custom-call(f32[16,128]{1,0:T(8,128)S(1)} %shard_map.54.w0, f32[16,128]{1,0:T(8,128)S(1)} %collective-permute-done.10.w1, f32[16,128]{1,0:T(8,128)S(1)} %collective-permute-done.11.w2, f32[16,128]{1,0:T(8,128)S(1)} %collective-permute-done.12.w3, f32[128,128]{1,0:T(8,128)S(1)} %shard_map.55.inverse), custom_call_target="tpu_custom_call" | custom-call | tf_op jit(solution)/shard_map/pallas_call | solution.py:27
  56.7 17.7 %all_to_all.11.received = f32[32,40,128]{2,1,0:T(8,128)S(1)} all-to-all(f32[32,40,128]{2,1,0:T(8,128)S(1)} %shard_map.56), channel_id=1, replica_groups=mesh['z'=4,'core'=2,'ja'=4,'ka'=4] {'core','ja','ka'}, dimensions={0} | all-to-all | bytes 1310720 | tf_op jit(solution)/shard_map/all_to_all | solution.py:287
  74.4 1.4 %shard_map.57 = (f32[32,1,1,64]{3,2,1,0:T(1,128)}, f32[32,64,64]{2,1,0:T(8,128)}) custom-call(f32[32,40,128]{2,1,0:T(8,128)S(1)} %all_to_all.11.received), custom_call_target="tpu_custom_call" | custom-call | tf_op jit(solution)/shard_map/pallas_call | solution.py:27
  (6 shorter events, 0.1 us)
Async XLA Ops:
  0.6 29.2 %copy-start = (f32[32,16,64,128]{3,2,1,0:T(8,128)S(1)}, f32[32,16,64,128]{3,2,1,0:T(8,128)}, u32[]{:S(2)}) copy-start(f32[32,16,64,128]{3,2,1,0:T(8,128)} %tensor.3) | copy-start | bytes 50331652
  1.8 6.0 %collective-permute-start.2 = (f32[16,8,128]{2,1,0:T(8,128)S(1)}, f32[16,8,128]{2,1,0:T(8,128)S(1)}, u32[]{:S(2)}, u32[]{:S(2)}) collective-permute-start(f32[16,8,128]{2,1,0:T(8,128)S(1)} %shard_map.50.m0), channel_id=1, source_target_pairs={{0,96},{32,0},{64,32},{96,64},{1,97},{33,1},{65,33},{97,65},{2,98}... | collective-permute-start | bytes 196616 | tf_op jit(solution)/shard_map/ppermute | solution.py:244
  6.4 4.7 %collective-permute-start.1 = (f32[16,8,128]{2,1,0:T(8,128)S(1)}, f32[16,8,128]{2,1,0:T(8,128)S(1)}, u32[]{:S(2)}, u32[]{:S(2)}) collective-permute-start(f32[16,8,128]{2,1,0:T(8,128)S(1)} %shard_map.50.m0), channel_id=1, source_target_pairs={{0,64},{32,96},{64,0},{96,32},{1,65},{33,97},{65,1},{97,33},{2,66}... | collective-permute-start | bytes 196616 | tf_op jit(solution)/shard_map/ppermute | solution.py:244
  6.4 5.0 %collective-permute-start = (f32[16,8,128]{2,1,0:T(8,128)S(1)}, f32[16,8,128]{2,1,0:T(8,128)S(1)}, u32[]{:S(2)}, u32[]{:S(2)}) collective-permute-start(f32[16,8,128]{2,1,0:T(8,128)S(1)} %shard_map.50.m0), channel_id=1, source_target_pairs={{0,32},{32,64},{64,96},{96,0},{1,33},{33,65},{65,97},{97,1},{2,34}... | collective-permute-start | bytes 196616 | tf_op jit(solution)/shard_map/ppermute | solution.py:244
  11.5 6.8 %collective-permute-start.5 = (f32[16,8,128]{2,1,0:T(8,128)S(1)}, f32[16,8,128]{2,1,0:T(8,128)S(1)}, u32[]{:S(2)}, u32[]{:S(2)}) collective-permute-start(f32[16,8,128]{2,1,0:T(8,128)S(1)} %get-tuple-element.4.b0), channel_id=1, source_target_pairs={{0,3},{1,0},{2,1},{3,2},{4,7},{5,4},{6,5},{7,6},{8,11},{9,8},{10,9... | collective-permute-start | bytes 196616 | tf_op jit(solution)/shard_map/ppermute | solution.py:244
  14.3 8.9 %collective-permute-start.8 = (f32[16,16,128]{2,1,0:T(8,128)S(1)}, f32[16,16,128]{2,1,0:T(8,128)S(1)}, u32[]{:S(2)}, u32[]{:S(2)}) collective-permute-start(f32[16,16,128]{2,1,0:T(8,128)S(1)} %get-tuple-element.5.c0), channel_id=1, source_target_pairs={{0,12},{4,0},{8,4},{12,8},{1,13},{5,1},{9,5},{13,9},{2,14},{6,2},{... | collective-permute-start | bytes 393224 | tf_op jit(solution)/shard_map/ppermute | solution.py:244
  16.8 6.5 %collective-permute-start.7 = (f32[16,16,128]{2,1,0:T(8,128)S(1)}, f32[16,16,128]{2,1,0:T(8,128)S(1)}, u32[]{:S(2)}, u32[]{:S(2)}) collective-permute-start(f32[16,16,128]{2,1,0:T(8,128)S(1)} %get-tuple-element.5.c0), channel_id=1, source_target_pairs={{0,8},{4,12},{8,0},{12,4},{1,9},{5,13},{9,1},{13,5},{2,10},{6,14},... | collective-permute-start | bytes 393224 | tf_op jit(solution)/shard_map/ppermute | solution.py:244
  17.3 6.2 %collective-permute-start.6 = (f32[16,16,128]{2,1,0:T(8,128)S(1)}, f32[16,16,128]{2,1,0:T(8,128)S(1)}, u32[]{:S(2)}, u32[]{:S(2)}) collective-permute-start(f32[16,16,128]{2,1,0:T(8,128)S(1)} %get-tuple-element.5.c0), channel_id=1, source_target_pairs={{0,4},{4,8},{8,12},{12,0},{1,5},{5,9},{9,13},{13,1},{2,6},{6,10},{... | collective-permute-start | bytes 393224 | tf_op jit(solution)/shard_map/ppermute | solution.py:244
  17.9 4.7 %collective-permute-start.4 = (f32[16,8,128]{2,1,0:T(8,128)S(1)}, f32[16,8,128]{2,1,0:T(8,128)S(1)}, u32[]{:S(2)}, u32[]{:S(2)}) collective-permute-start(f32[16,8,128]{2,1,0:T(8,128)S(1)} %get-tuple-element.4.b0), channel_id=1, source_target_pairs={{0,2},{1,3},{2,0},{3,1},{4,6},{5,7},{6,4},{7,5},{8,10},{9,11},{10,... | collective-permute-start | bytes 196616 | tf_op jit(solution)/shard_map/ppermute | solution.py:244
  18.3 5.0 %collective-permute-start.3 = (f32[16,8,128]{2,1,0:T(8,128)S(1)}, f32[16,8,128]{2,1,0:T(8,128)S(1)}, u32[]{:S(2)}, u32[]{:S(2)}) collective-permute-start(f32[16,8,128]{2,1,0:T(8,128)S(1)} %get-tuple-element.4.b0), channel_id=1, source_target_pairs={{0,1},{1,2},{2,3},{3,0},{4,5},{5,6},{6,7},{7,4},{8,9},{9,10},{10,1... | collective-permute-start | bytes 196616 | tf_op jit(solution)/shard_map/ppermute | solution.py:244
  23.7 6.1 %collective-permute-start.9 = (f32[16,96,128]{2,1,0:T(8,128)S(1)}, f32[16,96,128]{2,1,0:T(8,128)S(1)}, u32[]{:S(2)}, u32[]{:S(2)}) collective-permute-start(f32[16,96,128]{2,1,0:T(8,128)S(1)} %shard_map.52.mine), channel_id=1, source_target_pairs={{0,16},{16,0},{1,17},{17,1},{2,18},{18,2},{3,19},{19,3},{4,20},{20... | collective-permute-start | bytes 2359304 | tf_op jit(solution)/shard_map/ppermute | solution.py:264
  50.5 4.6 %collective-permute-start.12 = (f32[16,128]{1,0:T(8,128)S(1)}, f32[16,128]{1,0:T(8,128)S(1)}, u32[]{:S(2)}, u32[]{:S(2)}) collective-permute-start(f32[16,128]{1,0:T(8,128)S(1)} %shard_map.54.w0), channel_id=1, source_target_pairs={{0,96},{32,0},{64,32},{96,64},{1,97},{33,1},{65,33},{97,65},{2,98}... | collective-permute-start | bytes 24584 | tf_op jit(solution)/shard_map/ppermute | solution.py:244
  51.2 4.0 %collective-permute-start.11 = (f32[16,128]{1,0:T(8,128)S(1)}, f32[16,128]{1,0:T(8,128)S(1)}, u32[]{:S(2)}, u32[]{:S(2)}) collective-permute-start(f32[16,128]{1,0:T(8,128)S(1)} %shard_map.54.w0), channel_id=1, source_target_pairs={{0,64},{32,96},{64,0},{96,32},{1,65},{33,97},{65,1},{97,33},{2,66}... | collective-permute-start | bytes 24584 | tf_op jit(solution)/shard_map/ppermute | solution.py:244
  52.0 3.7 %collective-permute-start.10 = (f32[16,128]{1,0:T(8,128)S(1)}, f32[16,128]{1,0:T(8,128)S(1)}, u32[]{:S(2)}, u32[]{:S(2)}) collective-permute-start(f32[16,128]{1,0:T(8,128)S(1)} %shard_map.54.w0), channel_id=1, source_target_pairs={{0,32},{32,64},{64,96},{96,0},{1,33},{33,65},{65,97},{97,1},{2,34}... | collective-permute-start | bytes 24584 | tf_op jit(solution)/shard_map/ppermute | solution.py:244

commit v4 on v3

--- a/solution.py
+++ b/solution.py
@@ -14,13 +14,12 @@
 B_OWN = JD // (N_IA * N_KA)
 C_OWN = KD // (N_IA * N_JA)
 I_ALL = N_IA * ID
-OWNERS = PAIRS * 2
 HIGH = lax.Precision.HIGHEST
 MIB = 1024 * 1024
 VMEM = pl.BlockSpec(memory_space=pltpu.VMEM)
 ANY = pl.BlockSpec(memory_space=pl.ANY)
 PANEL = 16
-UNROLL = 4
+UNROLL = 8
 
 
 def call(kernel, out_shape, operands, *, specs=None, scratch=(), vmem=16, cost=None):
@@ -95,66 +94,89 @@
             out[p, at : at + n, :] = in_order([c[p, rows, :] for c in (c0, c1, c2, c3)], x, C_OWN)
 
 
-def mttkrp_kernel(tensor, mine, other, out):
+def contract(p, side, tensor, mine, other):
+    first_core = lax.axis_index("core") == 0
+    left = lax.broadcasted_iota(jnp.int32, (1, 2 * RANK), 1) < RANK
+    nb, nc = B_OWN * N_KA, C_OWN * N_JA
+
+    def both(at, rows):
+        here, there = mine[p, at : at + rows, :], other[p, at : at + rows, :]
+        return [jnp.where(first_core, here, there), jnp.where(first_core, there, here)]
+
+    def chosen(v):
+        return jnp.where(side == 0, v, swap_halves(v))
+
+    b = chosen(jnp.concatenate([part for z in range(N_Z) for part in both(z * nb, nb)], axis=0))
+    c = chosen(jnp.concatenate([part for z in range(N_Z) for part in both(JD // 2 + z * nc, nc)], axis=0))
+    c1 = c.astype(jnp.bfloat16).astype(jnp.float32)
+    c2 = (c - c1).astype(jnp.bfloat16).astype(jnp.float32)
+    c3 = c - c1 - c2
+    first = jnp.where(left, c1, swap_halves(c2))
+    second = jnp.where(left, c3, 0.0)
+    weight = jnp.where(left, b, swap_halves(b))
+    pieces = jnp.concatenate([first.astype(jnp.bfloat16), second.astype(jnp.bfloat16)], axis=1)
+    block = tensor[2 * p + side].reshape(ID * JD, KD)
+    high = block.astype(jnp.bfloat16)
+    low = (block - high.astype(jnp.float32)).astype(jnp.bfloat16)
+    product = jnp.dot(
+        jnp.concatenate([high, low], axis=1),
+        jnp.concatenate([pieces, pieces], axis=0),
+        preferred_element_type=jnp.float32,
+    )
+    product = (product[:, :KD] + product[:, KD:]).reshape(ID, JD, KD) * weight
+    total = jnp.sum(product.reshape(ID, JD // 8, 8, KD).sum(axis=1), axis=1)
+    return fold(total + swap_halves(total))
+
+
+def by_pairs(body):
+    def step(n, carry):
+        for u in range(UNROLL):
+            body(n * UNROLL + u)
+        return carry
+
+    lax.fori_loop(0, PAIRS // UNROLL, step, 0)
+
+
+def other_fields_kernel(tensor, mine, other, out):
+    side = 1 - lax.axis_index("core")
+
+    def pair(p):
+        out[p] = contract(p, side, tensor, mine, other)
+
+    by_pairs(pair)
+
+
+def own_fields_kernel(tensor, mine, other, out):
     _, core, x, y = place()
-    lane = lax.broadcasted_iota(jnp.int32, (1, 2 * RANK), 1)
-    left = lane < RANK
     first_core = core == 0
     nb, nc = B_OWN * N_KA, C_OWN * N_JA
 
-    def both(p, at, rows):
+    def share(p, at, rows):
         here, there = mine[p, pl.ds(at, rows), :], other[p, pl.ds(at, rows), :]
-        return [jnp.where(first_core, here, there), jnp.where(first_core, there, here)]
+        parts = [jnp.where(first_core, here, there), jnp.where(first_core, there, here)]
+        part = jnp.concatenate(parts, axis=0)
+        return fold(jnp.where(first_core, part, swap_halves(part)))
 
     def pair(p):
-        b = jnp.concatenate([part for z in range(N_Z) for part in both(p, z * nb, nb)], axis=0)
-        c = jnp.concatenate([part for z in range(N_Z) for part in both(p, JD // 2 + z * nc, nc)], axis=0)
-        part_b = mine[p, pl.ds(pl.multiple_of(y * nb, nb), nb), :]
-        part_c = mine[p, pl.ds(pl.multiple_of(JD // 2 + x * nc, nc), nc), :]
-        for side in range(2):
-            d = side * PAIRS + p
-            out[d, 8:16, :] = fold(swap_halves(part_c) if side else part_c)
-            part = fold(swap_halves(part_b) if side else part_b)
-            out[d, 16:24, :] = jnp.concatenate([part, jnp.zeros_like(part)], axis=0)
-        c1 = c.astype(jnp.bfloat16).astype(jnp.float32)
-        c2 = (c - c1).astype(jnp.bfloat16).astype(jnp.float32)
-        c3 = c - c1 - c2
-        for side in range(2):
-            if side == 0:
-                first = jnp.where(left, c1, swap_halves(c2))
-                second = jnp.where(left, c3, 0.0)
-                weight = jnp.where(left, b, swap_halves(b))
-            else:
-                first = jnp.where(left, swap_halves(c1), c2)
-                second = jnp.where(left, swap_halves(c3), 0.0)
-                weight = jnp.where(left, swap_halves(b), b)
-            pieces = jnp.concatenate([first.astype(jnp.bfloat16), second.astype(jnp.bfloat16)], axis=1)
-            block = tensor[2 * p + side].reshape(ID * JD, KD)
-            high = block.astype(jnp.bfloat16)
-            low = (block - high.astype(jnp.float32)).astype(jnp.bfloat16)
-            product = jnp.dot(
-                jnp.concatenate([high, low], axis=1),
-                jnp.concatenate([pieces, pieces], axis=0),
-                preferred_element_type=jnp.float32,
-            )
-            product = (product[:, :KD] + product[:, KD:]).reshape(ID, JD, KD) * weight
-            total = jnp.sum(product.reshape(ID, JD // 8, 8, KD).sum(axis=1), axis=1)
-            out[side * PAIRS + p, :8, :] = fold(total + swap_halves(total))
-
-    def step(n, carry):
-        for u in range(UNROLL):
-            pair(n * UNROLL + u)
-        return carry
-
-    lax.fori_loop(0, PAIRS // UNROLL, step, 0)
+        out[p, pl.ds(pl.multiple_of(8 * (1 - core), 8), 8), :] = jnp.zeros((8, 2 * RANK), jnp.float32)
+        out[p, pl.ds(pl.multiple_of(8 * core, 8), 8), :] = contract(p, core, tensor, mine, other)
+        out[p, 16:24, :] = share(p, pl.multiple_of(y * nb, nb), nb)
+        out[p, 24:40, :] = share(p, pl.multiple_of(JD // 2 + x * nc, nc), nc)
+
+    by_pairs(pair)
+
+
+def join_kernel(sums, swapped, out):
+    at = pl.multiple_of(8 * (1 - lax.axis_index("core")), 8)
+    out[...] = sums[...]
+    out[:, pl.ds(at, 8), :] = swapped[...]
 
 
 def total_kernel(received, out):
-    for core in range(2):
-        total = received[core * PAIRS, :8, :]
-        for s in range(1, PAIRS):
-            total = total + received[core * PAIRS + s, :8, :]
-        out[8 * core : 8 * core + 8, :] = total
+    total = received[0, :16, :]
+    for s in range(1, PAIRS):
+        total = total + received[s, :16, :]
+    out[...] = total
 
 
 def rows_gram(rows):
@@ -163,8 +185,8 @@
 
 
 def factor_kernel(received, out):
-    gram = rows_gram(received[:, 16:20, :].reshape(OWNERS * 4, 2 * RANK))
-    gram = gram * rows_gram(received[:, 8:16, :].reshape(OWNERS * 8, 2 * RANK))
+    gram = rows_gram(received[:, 16:24, :].reshape(PAIRS * 8, 2 * RANK))
+    gram = gram * rows_gram(received[:, 24:40, :].reshape(PAIRS * 16, 2 * RANK))
     lane = lax.broadcasted_iota(jnp.int32, (RANK, 2 * RANK), 1)
     row = lax.broadcasted_iota(jnp.int32, (RANK, 2 * RANK), 0)
     whole = jnp.where(lane < RANK, gram, jnp.where(lane == row + RANK, 1.0, 0.0))
@@ -217,24 +239,29 @@
     rows[...] = solved
     gram = fold(rows_gram(solved) * (1.0 / I_ALL))
     own = rows[pl.ds(pl.multiple_of(z * 16, 16), 16), :]
-    for core in range(2):
-        for q in range(ID):
-            out[core * PAIRS + q, : RANK // 2, :] = gram
-            row = core * 8 + q % 8
-            out[core * PAIRS + q, RANK // 2 :, :] = jnp.broadcast_to(own[row : row + 1], (8, 2 * RANK))
-
-
-def unpack_kernel(received, rows, gram):
-    _, _, x, y = place()
+    for q in range(ID):
+        out[q, : RANK // 2, :] = gram
+        for core in range(2):
+            row, at = core * 8 + q % 8, RANK // 2 + core * 4
+            out[q, at : at + 4, :] = jnp.broadcast_to(own[row : row + 1], (4, 2 * RANK))
+
+
+def unpack_kernel(received, swapped, rows, gram):
+    _, core, x, y = place()
     upper = x * N_KA + y >= 8
     half = RANK // 2
-    for p in range(PAIRS):
-        for side in range(2):
-            source = side * PAIRS + p
-            gram[2 * p + side, :half] = received[source, :half, :RANK]
-            gram[2 * p + side, half:] = received[source, :half, RANK:]
-            row = received[source, half : half + 1, :]
-            rows[2 * p + side, 0] = jnp.where(upper, row[:, RANK:], row[:, :RANK])
+
+    def unpack(here):
+        for p in range(PAIRS):
+            for side in range(2):
+                source = received if side == here else swapped
+                gram[2 * p + side, :half] = source[p, :half, :RANK]
+                gram[2 * p + side, half:] = source[p, :half, RANK:]
+                row = source[p, half + 4 * here : half + 4 * here + 1, :]
+                rows[2 * p + side, 0] = jnp.where(upper, row[:, RANK:], row[:, :RANK])
+
+    for here in range(2):
+        pl.when(core == here)(lambda here=here: unpack(here))
 
 
 LINE = [[(i, (i + s) % 4) for i in range(4)] for s in range(1, 4)]
@@ -242,6 +269,10 @@
 
 def around(value, axis):
     return [value] + [lax.ppermute(value, axis, perm) for perm in LINE]
+
+
+def swap_cores(value):
+    return lax.ppermute(value, "core", [(0, 1), (1, 0)])
 
 
 def on_device(tensor, factor_b, factor_c):
@@ -261,15 +292,13 @@
     b, c = call(along_z_kernel, (f32(PAIRS, 8, 2 * RANK), f32(PAIRS, 16, 2 * RANK)), parts)
     parts = around(b, "ka") + around(c, "ja")
     mine = call(along_xy_kernel, f32(PAIRS, 96, 2 * RANK), parts)
-    other = lax.ppermute(mine, "core", [(0, 1), (1, 0)])
-    sent = call(
-        mttkrp_kernel,
-        f32(OWNERS, 24, 2 * RANK),
-        (near, mine, other),
-        vmem=28,
-        cost=pl.CostEstimate(flops=8 * 2 * tensor.size * RANK, bytes_accessed=4 * tensor.size, transcendentals=0),
-    )
-    received = lax.all_to_all(sent, ("core", "ja", "ka"), 0, 0)
+    other = swap_cores(mine)
+    half = pl.CostEstimate(flops=8 * tensor.size * RANK, bytes_accessed=2 * tensor.size, transcendentals=0)
+    theirs = call(other_fields_kernel, f32(PAIRS, 8, 2 * RANK), (near, mine, other), vmem=28, cost=half)
+    swapped = swap_cores(theirs)
+    sums = call(own_fields_kernel, f32(PAIRS, 40, 2 * RANK), (near, mine, other), vmem=28, cost=half)
+    sent = call(join_kernel, f32(PAIRS, 40, 2 * RANK), (sums, swapped))
+    received = lax.all_to_all(sent, ("ja", "ka"), 0, 0)
     owned = call(total_kernel, f32(16, 2 * RANK), (received,))
     parts = around(owned, "z")
     inverse = call(
@@ -280,12 +309,13 @@
     )
     sent = call(
         finish_kernel,
-        f32(OWNERS, RANK // 2 + 8, 2 * RANK),
+        f32(PAIRS, RANK // 2 + 8, 2 * RANK),
         (*parts, inverse),
         scratch=[pltpu.VMEM((I_ALL // 2, 2 * RANK), jnp.float32)] * 2,
     )
-    received = lax.all_to_all(sent, ("core", "ja", "ka"), 0, 0)
-    rows, gram = call(unpack_kernel, (f32(FIELDS, 1, 1, RANK), f32(FIELDS, RANK, RANK)), (received,))
+    received = lax.all_to_all(sent, ("ja", "ka"), 0, 0)
+    swapped = swap_cores(received)
+    rows, gram = call(unpack_kernel, (f32(FIELDS, 1, 1, RANK), f32(FIELDS, RANK, RANK)), (received, swapped))
     return rows, gram
 
 

time: 76 us -> 73.7 us (0.970)
  blocking collectives: 32.4 us -> 23.8 us
  starting transfers between devices: 19.3 us -> 23.7 us
  waiting for transfers between devices: 11.4 us -> 12.7 us
    all_to_all x2, blocking collectives: 32.4 us -> 23.8 us  [on_device(): received = lax.all_to_all(sent, ('ja', 'ka'), 0, 0)]
    ppermute x1 -> x3, starting transfers between devices: 4.2 us -> 8.64 us  [swap_cores(): return lax.ppermute(value, 'core', [(0, 1), (1, 0)])]
    ppermute x1 -> x3, waiting for transfers between devices: 1.91 us -> 3.17 us  [swap_cores(): return lax.ppermute(value, 'core', [(0, 1), (1, 0)])]
    pallas_call x8 -> x10, Pallas kernels: 12 us -> 12.6 us  [call(): pl.pallas_call(kernel, out_shape=out_shape, in_specs=[VMEM] * len(operand...]
  transfers between devices with their start and end apart: 13 -> 15, of which waited for: 9 -> 10; matrix products, arithmetic and copies ran while one was open for 0% -> 0% of each run, Pallas kernels for 3% -> 8%
where the time goes in v4:
time: 73.7 us; the launch traced here: 73.6 us
  blocking collectives  23.8 us (32%)
  starting transfers between devices  23.7 us (32%)
  waiting for transfers between devices  12.7 us (17%)
  Pallas kernels  12.6 us (17%)
    all_to_all x2, blocking collectives, on_device(): received = lax.all_to_all(sent, ('ja', 'ka'), 0, 0)  23.8 us
    ppermute x12, starting transfers between devices, around(): return [value] + [lax.ppermute(value, axis, perm) for perm in LINE]  15.1 us
    pallas_call x10, Pallas kernels, call(): pl.pallas_call(kernel, out_shape=out_shape, in_specs=[VMEM] * len(operand...  12.6 us
    ppermute x12, waiting for transfers between devices, around(): return [value] + [lax.ppermute(value, axis, perm) for perm in LINE]  9.54 us
    ppermute x3, starting transfers between devices, swap_cores(): return lax.ppermute(value, 'core', [(0, 1), (1, 0)])  8.64 us
    ppermute x3, waiting for transfers between devices, swap_cores(): return lax.ppermute(value, 'core', [(0, 1), (1, 0)])  3.17 us
  transfers between devices with their start and end apart: 15, of which 10 were waited for; matrix products, arithmetic and copies ran while one was open for 0% of the time, Pallas kernels for 8%

profile of v4, /device:TPU:1, one launch (start us, length us, event | category | flops | bytes accessed | tf_op | source)
XLA Modules:
  0.0 73.6 jit_solution(4247880403237143094)
XLA Ops:
  0.6 1.1 %shard_map.50.m0 = f32[16,8,128]{2,1,0:T(8,128)S(1)} custom-call(f32[32,2,64]{2,1,0:T(2,128)} %bitcast.3, f32[32,4,64]{2,1,0:T(4,128)} %bitcast.2, f32[32,16,64,128]{3,2,1,0:T(8,128)} %tensor.5), custom_call_target="tpu_custom_call" | custom-call | tf_op jit(solution)/shard_map/pallas_call | solution.py:26
  1.8 4.7 %collective-permute-start.2 = (f32[16,8,128]{2,1,0:T(8,128)S(1)}, f32[16,8,128]{2,1,0:T(8,128)S(1)}, u32[]{:S(2)}, u32[]{:S(2)}) collective-permute-start(f32[16,8,128]{2,1,0:T(8,128)S(1)} %shard_map.50.m0), channel_id=1, source_target_pairs={{0,96},{32,0},{64,32},{96,64},{1,97},{33,1},{65,33},{97,65},{2,98}... | collective-permute-start | bytes 196616 | tf_op jit(solution)/shard_map/ppermute | solution.py:271
  6.4 0.7 collective-permute-start
  7.1 0.6 collective-permute-done.2.m3
  7.8 3.4 %collective-permute-done.1.m2 = f32[16,8,128]{2,1,0:T(8,128)S(1)} collective-permute-done((f32[16,8,128]{2,1,0:T(8,128)S(1)}, f32[16,8,128]{2,1,0:T(8,128)S(1)}, u32[]{:S(2)}, u32[]{:S(2)}) %collective-permute-start.1) | collective-permute-done | bytes 65568 | tf_op jit(solution)/shard_map/ppermute | solution.py:271
  11.2 0.3 collective-permute-done.m1
  11.5 2.8 %collective-permute-start.5 = (f32[16,8,128]{2,1,0:T(8,128)S(1)}, f32[16,8,128]{2,1,0:T(8,128)S(1)}, u32[]{:S(2)}, u32[]{:S(2)}) collective-permute-start(f32[16,8,128]{2,1,0:T(8,128)S(1)} %get-tuple-element.4.b0), channel_id=1, source_target_pairs={{0,3},{1,0},{2,1},{3,2},{4,7},{5,4},{6,5},{7,6},{8,11},{9,8},{10,9... | collective-permute-start | bytes 196616 | tf_op jit(solution)/shard_map/ppermute | solution.py:271
  14.3 2.5 %collective-permute-start.8 = (f32[16,16,128]{2,1,0:T(8,128)S(1)}, f32[16,16,128]{2,1,0:T(8,128)S(1)}, u32[]{:S(2)}, u32[]{:S(2)}) collective-permute-start(f32[16,16,128]{2,1,0:T(8,128)S(1)} %get-tuple-element.5.c0), channel_id=1, source_target_pairs={{0,12},{4,0},{8,4},{12,8},{1,13},{5,1},{9,5},{13,9},{2,14},{6,2},{... | collective-permute-start | bytes 393224 | tf_op jit(solution)/shard_map/ppermute | solution.py:271
  16.8 0.5 collective-permute-start.7
  17.3 0.6 collective-permute-start.6
  17.9 0.3 collective-permute-start.4
  18.3 0.7 collective-permute-start.3
  19.0 3.6 %collective-permute-done.4.b2 = f32[16,8,128]{2,1,0:T(8,128)S(1)} collective-permute-done((f32[16,8,128]{2,1,0:T(8,128)S(1)}, f32[16,8,128]{2,1,0:T(8,128)S(1)}, u32[]{:S(2)}, u32[]{:S(2)}) %collective-permute-start.4) | collective-permute-done | bytes 65568 | tf_op jit(solution)/shard_map/ppermute | solution.py:271
  22.6 0.6 collective-permute-done.3.b1
  23.2 0.3 collective-permute-done.6.c1
  23.5 0.2 shard_map.52.mine
  23.7 4.2 %collective-permute-start.9 = (f32[16,96,128]{2,1,0:T(8,128)S(1)}, f32[16,96,128]{2,1,0:T(8,128)S(1)}, u32[]{:S(2)}, u32[]{:S(2)}) collective-permute-start(f32[16,96,128]{2,1,0:T(8,128)S(1)} %shard_map.52.mine), channel_id=1, source_target_pairs={{0,16},{16,0},{1,17},{17,1},{2,18},{18,2},{3,19},{19,3},{4,20},{20... | collective-permute-start | bytes 2359304 | tf_op jit(solution)/shard_map/ppermute | solution.py:275
  27.9 1.9 %collective-permute-done.9.other = f32[16,96,128]{2,1,0:T(8,128)S(1)} collective-permute-done((f32[16,96,128]{2,1,0:T(8,128)S(1)}, f32[16,96,128]{2,1,0:T(8,128)S(1)}, u32[]{:S(2)}, u32[]{:S(2)}) %collective-permute-start.9) | collective-permute-done | bytes 786464 | tf_op jit(solution)/shard_map/ppermute | solution.py:275
  29.8 3.2 %shard_map.54 = f32[16,8,128]{2,1,0:T(8,128)S(1)} custom-call(f32[32,16,64,128]{3,2,1,0:T(8,128)S(1)} %copy-done, f32[16,96,128]{2,1,0:T(8,128)S(1)} %shard_map.52.mine, f32[16,96,128]{2,1,0:T(8,128)S(1)} %collective-permute-done.9.other), custom_call_target="tpu_custom_call" | custom-call | flops 2147483648 | bytes 8388608 | tf_op jit(solution)/shard_map/pallas_call | solution.py:26
  33.0 0.4 collective-permute-start.10
  33.4 3.3 %shard_map.53.sums = f32[16,40,128]{2,1,0:T(8,128)S(1)} custom-call(f32[32,16,64,128]{3,2,1,0:T(8,128)S(1)} %copy-done, f32[16,96,128]{2,1,0:T(8,128)S(1)} %shard_map.52.mine, f32[16,96,128]{2,1,0:T(8,128)S(1)} %collective-permute-done.9.other), custom_call_target="tpu_custom_call" | custom-call | flops 2147483648 | bytes 8388608 | tf_op jit(solution)/shard_map/pallas_call | solution.py:26
  36.8 12.2 %all_to_all.10.received = f32[16,40,128]{2,1,0:T(8,128)S(1)} all-to-all(f32[16,40,128]{2,1,0:T(8,128)S(1)} %shard_map.55), channel_id=1, replica_groups=mesh['z'=4,'core'=2,'ja'=4,'ka'=4] {'ja','ka'}, dimensions={0} | all-to-all | bytes 655360 | tf_op jit(solution)/shard_map/all_to_all | solution.py:301
  49.1 0.6 collective-permute-start.13
  49.7 0.9 %collective-permute-start.12 = (f32[16,128]{1,0:T(8,128)S(1)}, f32[16,128]{1,0:T(8,128)S(1)}, u32[]{:S(2)}, u32[]{:S(2)}) collective-permute-start(f32[16,128]{1,0:T(8,128)S(1)} %shard_map.56.w0), channel_id=1, source_target_pairs={{0,64},{32,96},{64,0},{96,32},{1,65},{33,97},{65,1},{97,33},{2,66}... | collective-permute-start | bytes 24584 | tf_op jit(solution)/shard_map/ppermute | solution.py:271
  50.6 0.8 %collective-permute-start.11 = (f32[16,128]{1,0:T(8,128)S(1)}, f32[16,128]{1,0:T(8,128)S(1)}, u32[]{:S(2)}, u32[]{:S(2)}) collective-permute-start(f32[16,128]{1,0:T(8,128)S(1)} %shard_map.56.w0), channel_id=1, source_target_pairs={{0,32},{32,64},{64,96},{96,0},{1,33},{33,65},{65,97},{97,1},{2,34}... | collective-permute-start | bytes 24584 | tf_op jit(solution)/shard_map/ppermute | solution.py:271
  51.4 2.3 %shard_map.57.inverse = f32[128,128]{1,0:T(8,128)S(1)} custom-call(f32[16,40,128]{2,1,0:T(8,128)S(1)} %all_to_all.10.received), custom_call_target="tpu_custom_call" | custom-call | flops 1048576 | bytes 10485760 | tf_op jit(solution)/shard_map/pallas_call | solution.py:26
  53.7 0.6 collective-permute-done.11.w1
  54.3 1.0 %shard_map.58 = f32[16,40,128]{2,1,0:T(8,128)S(1)} custom-call(f32[16,128]{1,0:T(8,128)S(1)} %shard_map.56.w0, f32[16,128]{1,0:T(8,128)S(1)} %collective-permute-done.11.w1, f32[16,128]{1,0:T(8,128)S(1)} %collective-permute-done.12.w2, f32[16,128]{1,0:T(8,128)S(1)} %collective-permute-done.13.w3, f32[128,128]{1,0:T(8,128)S(1)} %shard_map.57.inverse), custom_call_target="tpu_custom_call" | custom-call | tf_op jit(solution)/shard_map/pallas_call | solution.py:26
  55.3 11.6 %all_to_all.11.received = f32[16,40,128]{2,1,0:T(8,128)S(1)} all-to-all(f32[16,40,128]{2,1,0:T(8,128)S(1)} %shard_map.58), channel_id=1, replica_groups=mesh['z'=4,'core'=2,'ja'=4,'ka'=4] {'ja','ka'}, dimensions={0} | all-to-all | bytes 655360 | tf_op jit(solution)/shard_map/all_to_all | solution.py:316
  66.9 4.0 %collective-permute-start.14 = (f32[16,40,128]{2,1,0:T(8,128)S(1)}, f32[16,40,128]{2,1,0:T(8,128)S(1)}, u32[]{:S(2)}, u32[]{:S(2)}) collective-permute-start(f32[16,40,128]{2,1,0:T(8,128)S(1)} %all_to_all.11.received), channel_id=1, source_target_pairs={{0,16},{16,0},{1,17},{17,1},{2,18},{18,2},{3,19},{19,3},{4,20},{20... | collective-permute-start | bytes 983048 | tf_op jit(solution)/shard_map/ppermute | solution.py:275
  70.9 1.3 %collective-permute-done.14.swapped = f32[16,40,128]{2,1,0:T(8,128)S(1)} collective-permute-done((f32[16,40,128]{2,1,0:T(8,128)S(1)}, f32[16,40,128]{2,1,0:T(8,128)S(1)}, u32[]{:S(2)}, u32[]{:S(2)}) %collective-permute-start.14) | collective-permute-done | bytes 327712 | tf_op jit(solution)/shard_map/ppermute | solution.py:275
  72.2 1.4 %shard_map.59 = (f32[32,1,1,64]{3,2,1,0:T(1,128)}, f32[32,64,64]{2,1,0:T(8,128)}) custom-call(f32[16,40,128]{2,1,0:T(8,128)S(1)} %all_to_all.11.received, f32[16,40,128]{2,1,0:T(8,128)S(1)} %collective-permute-done.14.swapped), custom_call_target="tpu_custom_call" | custom-call | tf_op jit(solution)/shard_map/pallas_call | solution.py:26
  (12 shorter events, 0.2 us)
Async XLA Ops:
  0.6 29.2 %copy-start = (f32[32,16,64,128]{3,2,1,0:T(8,128)S(1)}, f32[32,16,64,128]{3,2,1,0:T(8,128)}, u32[]{:S(2)}) copy-start(f32[32,16,64,128]{3,2,1,0:T(8,128)} %tensor.5) | copy-start | bytes 50331652
  1.8 6.0 %collective-permute-start.2 = (f32[16,8,128]{2,1,0:T(8,128)S(1)}, f32[16,8,128]{2,1,0:T(8,128)S(1)}, u32[]{:S(2)}, u32[]{:S(2)}) collective-permute-start(f32[16,8,128]{2,1,0:T(8,128)S(1)} %shard_map.50.m0), channel_id=1, source_target_pairs={{0,96},{32,0},{64,32},{96,64},{1,97},{33,1},{65,33},{97,65},{2,98}... | collective-permute-start | bytes 196616 | tf_op jit(solution)/shard_map/ppermute | solution.py:271
  6.4 4.7 %collective-permute-start.1 = (f32[16,8,128]{2,1,0:T(8,128)S(1)}, f32[16,8,128]{2,1,0:T(8,128)S(1)}, u32[]{:S(2)}, u32[]{:S(2)}) collective-permute-start(f32[16,8,128]{2,1,0:T(8,128)S(1)} %shard_map.50.m0), channel_id=1, source_target_pairs={{0,64},{32,96},{64,0},{96,32},{1,65},{33,97},{65,1},{97,33},{2,66}... | collective-permute-start | bytes 196616 | tf_op jit(solution)/shard_map/ppermute | solution.py:271
  6.4 5.0 %collective-permute-start = (f32[16,8,128]{2,1,0:T(8,128)S(1)}, f32[16,8,128]{2,1,0:T(8,128)S(1)}, u32[]{:S(2)}, u32[]{:S(2)}) collective-permute-start(f32[16,8,128]{2,1,0:T(8,128)S(1)} %shard_map.50.m0), channel_id=1, source_target_pairs={{0,32},{32,64},{64,96},{96,0},{1,33},{33,65},{65,97},{97,1},{2,34}... | collective-permute-start | bytes 196616 | tf_op jit(solution)/shard_map/ppermute | solution.py:271
  11.5 6.8 %collective-permute-start.5 = (f32[16,8,128]{2,1,0:T(8,128)S(1)}, f32[16,8,128]{2,1,0:T(8,128)S(1)}, u32[]{:S(2)}, u32[]{:S(2)}) collective-permute-start(f32[16,8,128]{2,1,0:T(8,128)S(1)} %get-tuple-element.4.b0), channel_id=1, source_target_pairs={{0,3},{1,0},{2,1},{3,2},{4,7},{5,4},{6,5},{7,6},{8,11},{9,8},{10,9... | collective-permute-start | bytes 196616 | tf_op jit(solution)/shard_map/ppermute | solution.py:271
  14.3 8.9 %collective-permute-start.8 = (f32[16,16,128]{2,1,0:T(8,128)S(1)}, f32[16,16,128]{2,1,0:T(8,128)S(1)}, u32[]{:S(2)}, u32[]{:S(2)}) collective-permute-start(f32[16,16,128]{2,1,0:T(8,128)S(1)} %get-tuple-element.5.c0), channel_id=1, source_target_pairs={{0,12},{4,0},{8,4},{12,8},{1,13},{5,1},{9,5},{13,9},{2,14},{6,2},{... | collective-permute-start | bytes 393224 | tf_op jit(solution)/shard_map/ppermute | solution.py:271
  16.8 6.5 %collective-permute-start.7 = (f32[16,16,128]{2,1,0:T(8,128)S(1)}, f32[16,16,128]{2,1,0:T(8,128)S(1)}, u32[]{:S(2)}, u32[]{:S(2)}) collective-permute-start(f32[16,16,128]{2,1,0:T(8,128)S(1)} %get-tuple-element.5.c0), channel_id=1, source_target_pairs={{0,8},{4,12},{8,0},{12,4},{1,9},{5,13},{9,1},{13,5},{2,10},{6,14},... | collective-permute-start | bytes 393224 | tf_op jit(solution)/shard_map/ppermute | solution.py:271
  17.3 6.2 %collective-permute-start.6 = (f32[16,16,128]{2,1,0:T(8,128)S(1)}, f32[16,16,128]{2,1,0:T(8,128)S(1)}, u32[]{:S(2)}, u32[]{:S(2)}) collective-permute-start(f32[16,16,128]{2,1,0:T(8,128)S(1)} %get-tuple-element.5.c0), channel_id=1, source_target_pairs={{0,4},{4,8},{8,12},{12,0},{1,5},{5,9},{9,13},{13,1},{2,6},{6,10},{... | collective-permute-start | bytes 393224 | tf_op jit(solution)/shard_map/ppermute | solution.py:271
  17.9 4.7 %collective-permute-start.4 = (f32[16,8,128]{2,1,0:T(8,128)S(1)}, f32[16,8,128]{2,1,0:T(8,128)S(1)}, u32[]{:S(2)}, u32[]{:S(2)}) collective-permute-start(f32[16,8,128]{2,1,0:T(8,128)S(1)} %get-tuple-element.4.b0), channel_id=1, source_target_pairs={{0,2},{1,3},{2,0},{3,1},{4,6},{5,7},{6,4},{7,5},{8,10},{9,11},{10,... | collective-permute-start | bytes 196616 | tf_op jit(solution)/shard_map/ppermute | solution.py:271
  18.3 5.0 %collective-permute-start.3 = (f32[16,8,128]{2,1,0:T(8,128)S(1)}, f32[16,8,128]{2,1,0:T(8,128)S(1)}, u32[]{:S(2)}, u32[]{:S(2)}) collective-permute-start(f32[16,8,128]{2,1,0:T(8,128)S(1)} %get-tuple-element.4.b0), channel_id=1, source_target_pairs={{0,1},{1,2},{2,3},{3,0},{4,5},{5,6},{6,7},{7,4},{8,9},{9,10},{10,1... | collective-permute-start | bytes 196616 | tf_op jit(solution)/shard_map/ppermute | solution.py:271
  23.7 6.1 %collective-permute-start.9 = (f32[16,96,128]{2,1,0:T(8,128)S(1)}, f32[16,96,128]{2,1,0:T(8,128)S(1)}, u32[]{:S(2)}, u32[]{:S(2)}) collective-permute-start(f32[16,96,128]{2,1,0:T(8,128)S(1)} %shard_map.52.mine), channel_id=1, source_target_pairs={{0,16},{16,0},{1,17},{17,1},{2,18},{18,2},{3,19},{19,3},{4,20},{20... | collective-permute-start | bytes 2359304 | tf_op jit(solution)/shard_map/ppermute | solution.py:275
  33.0 3.8 %collective-permute-start.10 = (f32[16,8,128]{2,1,0:T(8,128)S(1)}, f32[16,8,128]{2,1,0:T(8,128)S(1)}, u32[]{:S(2)}, u32[]{:S(2)}) collective-permute-start(f32[16,8,128]{2,1,0:T(8,128)S(1)} %shard_map.54), channel_id=1, source_target_pairs={{0,16},{16,0},{1,17},{17,1},{2,18},{18,2},{3,19},{19,3},{4,20},{20... | collective-permute-start | bytes 196616 | tf_op jit(solution)/shard_map/ppermute | solution.py:275
  49.1 4.6 %collective-permute-start.13 = (f32[16,128]{1,0:T(8,128)S(1)}, f32[16,128]{1,0:T(8,128)S(1)}, u32[]{:S(2)}, u32[]{:S(2)}) collective-permute-start(f32[16,128]{1,0:T(8,128)S(1)} %shard_map.56.w0), channel_id=1, source_target_pairs={{0,96},{32,0},{64,32},{96,64},{1,97},{33,1},{65,33},{97,65},{2,98}... | collective-permute-start | bytes 24584 | tf_op jit(solution)/shard_map/ppermute | solution.py:271
  49.7 4.0 %collective-permute-start.12 = (f32[16,128]{1,0:T(8,128)S(1)}, f32[16,128]{1,0:T(8,128)S(1)}, u32[]{:S(2)}, u32[]{:S(2)}) collective-permute-start(f32[16,128]{1,0:T(8,128)S(1)} %shard_map.56.w0), channel_id=1, source_target_pairs={{0,64},{32,96},{64,0},{96,32},{1,65},{33,97},{65,1},{97,33},{2,66}... | collective-permute-start | bytes 24584 | tf_op jit(solution)/shard_map/ppermute | solution.py:271
  50.6 3.7 %collective-permute-start.11 = (f32[16,128]{1,0:T(8,128)S(1)}, f32[16,128]{1,0:T(8,128)S(1)}, u32[]{:S(2)}, u32[]{:S(2)}) collective-permute-start(f32[16,128]{1,0:T(8,128)S(1)} %shard_map.56.w0), channel_id=1, source_target_pairs={{0,32},{32,64},{64,96},{96,0},{1,33},{33,65},{65,97},{97,1},{2,34}... | collective-permute-start | bytes 24584 | tf_op jit(solution)/shard_map/ppermute | solution.py:271
  66.9 5.3 %collective-permute-start.14 = (f32[16,40,128]{2,1,0:T(8,128)S(1)}, f32[16,40,128]{2,1,0:T(8,128)S(1)}, u32[]{:S(2)}, u32[]{:S(2)}) collective-permute-start(f32[16,40,128]{2,1,0:T(8,128)S(1)} %all_to_all.11.received), channel_id=1, source_target_pairs={{0,16},{16,0},{1,17},{17,1},{2,18},{18,2},{3,19},{19,3},{4,20},{20... | collective-permute-start | bytes 983048 | tf_op jit(solution)/shard_map/ppermute | solution.py:275

commit v5 on v4

--- a/solution.py
+++ b/solution.py
@@ -224,8 +224,10 @@
     whole = jnp.concatenate(panels, axis=0)
     pivots = jnp.sum(jnp.where(lane == row, whole, 0.0), axis=1, keepdims=True)
     inverse = jnp.where(lane >= RANK, whole * lax.rsqrt(pivots), 0.0)
-    out[:RANK, :] = swap_halves(inverse)
-    out[RANK:, :] = inverse
+    twice = jnp.concatenate([swap_halves(inverse), inverse], axis=0)
+    out[...] = lax.dot_general(
+        twice, twice, (((0,), (0,)), ((), ())), precision=HIGH, preferred_element_type=jnp.float32
+    )
 
 
 def finish_kernel(w0, w1, w2, w3, inverse, out, every, rows):
@@ -233,9 +235,7 @@
     for s, part in enumerate((w0, w1, w2, w3)):
         at = lax.rem(z - s + N_Z, N_Z) * 16
         every[pl.ds(pl.multiple_of(at, 16), 16), :] = part[...]
-    inv = inverse[...]
-    half = lax.dot_general(every[...], inv, (((1,), (1,)), ((), ())), precision=HIGH, preferred_element_type=jnp.float32)
-    solved = jnp.dot(half, inv, precision=HIGH, preferred_element_type=jnp.float32)
+    solved = jnp.dot(every[...], inverse[...], precision=HIGH, preferred_element_type=jnp.float32)
     rows[...] = solved
     gram = fold(rows_gram(solved) * (1.0 / I_ALL))
     own = rows[pl.ds(pl.multiple_of(z * 16, 16), 16), :]

time: 73.7 us -> 73.4 us (level)
  transfers between devices with their start and end apart: 15 -> 15, of which waited for: 10 -> 9; matrix products, arithmetic and copies ran while one was open for 0% -> 0% of each run, Pallas kernels for 8% -> 8%
where the time goes in v5:
time: 73.4 us; the launch traced here: 73.3 us
  blocking collectives  23.8 us (32%)
  starting transfers between devices  23.7 us (32%)
  Pallas kernels  12.7 us (17%)
  waiting for transfers between devices  12.3 us (17%)
    all_to_all x2, blocking collectives, on_device(): received = lax.all_to_all(sent, ('ja', 'ka'), 0, 0)  23.8 us
    ppermute x12, starting transfers between devices, around(): return [value] + [lax.ppermute(value, axis, perm) for perm in LINE]  15.1 us
    pallas_call x10, Pallas kernels, call(): pl.pallas_call(kernel, out_shape=out_shape, in_specs=[VMEM] * len(operand...  12.7 us
    ppermute x12, waiting for transfers between devices, around(): return [value] + [lax.ppermute(value, axis, perm) for perm in LINE]  9.15 us
    ppermute x3, starting transfers between devices, swap_cores(): return lax.ppermute(value, 'core', [(0, 1), (1, 0)])  8.64 us
    ppermute x3, waiting for transfers between devices, swap_cores(): return lax.ppermute(value, 'core', [(0, 1), (1, 0)])  3.17 us
  transfers between devices with their start and end apart: 15, of which 9 were waited for; matrix products, arithmetic and copies ran while one was open for 0% of the time, Pallas kernels for 8%

profile of v5, /device:TPU:1, one launch (start us, length us, event | category | flops | bytes accessed | tf_op | source)
XLA Modules:
  0.0 73.3 jit_solution(2761951606341841234)
XLA Ops:
  0.6 1.1 %shard_map.50.m0 = f32[16,8,128]{2,1,0:T(8,128)S(1)} custom-call(f32[32,2,64]{2,1,0:T(2,128)} %bitcast.3, f32[32,4,64]{2,1,0:T(4,128)} %bitcast.2, f32[32,16,64,128]{3,2,1,0:T(8,128)} %tensor.5), custom_call_target="tpu_custom_call" | custom-call | tf_op jit(solution)/shard_map/pallas_call | solution.py:26
  1.8 4.7 %collective-permute-start.2 = (f32[16,8,128]{2,1,0:T(8,128)S(1)}, f32[16,8,128]{2,1,0:T(8,128)S(1)}, u32[]{:S(2)}, u32[]{:S(2)}) collective-permute-start(f32[16,8,128]{2,1,0:T(8,128)S(1)} %shard_map.50.m0), channel_id=1, source_target_pairs={{0,96},{32,0},{64,32},{96,64},{1,97},{33,1},{65,33},{97,65},{2,98}... | collective-permute-start | bytes 196616 | tf_op jit(solution)/shard_map/ppermute | solution.py:271
  6.4 0.7 collective-permute-start
  7.1 0.6 collective-permute-done.2.m3
  7.8 3.4 %collective-permute-done.1.m2 = f32[16,8,128]{2,1,0:T(8,128)S(1)} collective-permute-done((f32[16,8,128]{2,1,0:T(8,128)S(1)}, f32[16,8,128]{2,1,0:T(8,128)S(1)}, u32[]{:S(2)}, u32[]{:S(2)}) %collective-permute-start.1) | collective-permute-done | bytes 65568 | tf_op jit(solution)/shard_map/ppermute | solution.py:271
  11.2 0.3 collective-permute-done.m1
  11.5 2.8 %collective-permute-start.5 = (f32[16,8,128]{2,1,0:T(8,128)S(1)}, f32[16,8,128]{2,1,0:T(8,128)S(1)}, u32[]{:S(2)}, u32[]{:S(2)}) collective-permute-start(f32[16,8,128]{2,1,0:T(8,128)S(1)} %get-tuple-element.4.b0), channel_id=1, source_target_pairs={{0,3},{1,0},{2,1},{3,2},{4,7},{5,4},{6,5},{7,6},{8,11},{9,8},{10,9... | collective-permute-start | bytes 196616 | tf_op jit(solution)/shard_map/ppermute | solution.py:271
  14.3 2.5 %collective-permute-start.8 = (f32[16,16,128]{2,1,0:T(8,128)S(1)}, f32[16,16,128]{2,1,0:T(8,128)S(1)}, u32[]{:S(2)}, u32[]{:S(2)}) collective-permute-start(f32[16,16,128]{2,1,0:T(8,128)S(1)} %get-tuple-element.5.c0), channel_id=1, source_target_pairs={{0,12},{4,0},{8,4},{12,8},{1,13},{5,1},{9,5},{13,9},{2,14},{6,2},{... | collective-permute-start | bytes 393224 | tf_op jit(solution)/shard_map/ppermute | solution.py:271
  16.8 0.5 collective-permute-start.7
  17.3 0.6 collective-permute-start.6
  17.9 0.3 collective-permute-start.4
  18.3 0.7 collective-permute-start.3
  19.0 3.6 %collective-permute-done.4.b2 = f32[16,8,128]{2,1,0:T(8,128)S(1)} collective-permute-done((f32[16,8,128]{2,1,0:T(8,128)S(1)}, f32[16,8,128]{2,1,0:T(8,128)S(1)}, u32[]{:S(2)}, u32[]{:S(2)}) %collective-permute-start.4) | collective-permute-done | bytes 65568 | tf_op jit(solution)/shard_map/ppermute | solution.py:271
  22.6 0.6 collective-permute-done.3.b1
  23.2 0.3 collective-permute-done.6.c1
  23.5 0.2 shard_map.52.mine
  23.7 4.2 %collective-permute-start.9 = (f32[16,96,128]{2,1,0:T(8,128)S(1)}, f32[16,96,128]{2,1,0:T(8,128)S(1)}, u32[]{:S(2)}, u32[]{:S(2)}) collective-permute-start(f32[16,96,128]{2,1,0:T(8,128)S(1)} %shard_map.52.mine), channel_id=1, source_target_pairs={{0,16},{16,0},{1,17},{17,1},{2,18},{18,2},{3,19},{19,3},{4,20},{20... | collective-permute-start | bytes 2359304 | tf_op jit(solution)/shard_map/ppermute | solution.py:275
  27.9 1.9 %collective-permute-done.9.other = f32[16,96,128]{2,1,0:T(8,128)S(1)} collective-permute-done((f32[16,96,128]{2,1,0:T(8,128)S(1)}, f32[16,96,128]{2,1,0:T(8,128)S(1)}, u32[]{:S(2)}, u32[]{:S(2)}) %collective-permute-start.9) | collective-permute-done | bytes 786464 | tf_op jit(solution)/shard_map/ppermute | solution.py:275
  29.8 3.2 %shard_map.54 = f32[16,8,128]{2,1,0:T(8,128)S(1)} custom-call(f32[32,16,64,128]{3,2,1,0:T(8,128)S(1)} %copy-done, f32[16,96,128]{2,1,0:T(8,128)S(1)} %shard_map.52.mine, f32[16,96,128]{2,1,0:T(8,128)S(1)} %collective-permute-done.9.other), custom_call_target="tpu_custom_call" | custom-call | flops 2147483648 | bytes 8388608 | tf_op jit(solution)/shard_map/pallas_call | solution.py:26
  33.0 0.4 collective-permute-start.10
  33.4 3.3 %shard_map.53.sums = f32[16,40,128]{2,1,0:T(8,128)S(1)} custom-call(f32[32,16,64,128]{3,2,1,0:T(8,128)S(1)} %copy-done, f32[16,96,128]{2,1,0:T(8,128)S(1)} %shard_map.52.mine, f32[16,96,128]{2,1,0:T(8,128)S(1)} %collective-permute-done.9.other), custom_call_target="tpu_custom_call" | custom-call | flops 2147483648 | bytes 8388608 | tf_op jit(solution)/shard_map/pallas_call | solution.py:26
  36.8 12.2 %all_to_all.10.received = f32[16,40,128]{2,1,0:T(8,128)S(1)} all-to-all(f32[16,40,128]{2,1,0:T(8,128)S(1)} %shard_map.55), channel_id=1, replica_groups=mesh['z'=4,'core'=2,'ja'=4,'ka'=4] {'ja','ka'}, dimensions={0} | all-to-all | bytes 655360 | tf_op jit(solution)/shard_map/all_to_all | solution.py:301
  49.1 0.6 collective-permute-start.13
  49.7 0.9 %collective-permute-start.12 = (f32[16,128]{1,0:T(8,128)S(1)}, f32[16,128]{1,0:T(8,128)S(1)}, u32[]{:S(2)}, u32[]{:S(2)}) collective-permute-start(f32[16,128]{1,0:T(8,128)S(1)} %shard_map.56.w0), channel_id=1, source_target_pairs={{0,64},{32,96},{64,0},{96,32},{1,65},{33,97},{65,1},{97,33},{2,66}... | collective-permute-start | bytes 24584 | tf_op jit(solution)/shard_map/ppermute | solution.py:271
  50.6 0.8 %collective-permute-start.11 = (f32[16,128]{1,0:T(8,128)S(1)}, f32[16,128]{1,0:T(8,128)S(1)}, u32[]{:S(2)}, u32[]{:S(2)}) collective-permute-start(f32[16,128]{1,0:T(8,128)S(1)} %shard_map.56.w0), channel_id=1, source_target_pairs={{0,32},{32,64},{64,96},{96,0},{1,33},{33,65},{65,97},{97,1},{2,34}... | collective-permute-start | bytes 24584 | tf_op jit(solution)/shard_map/ppermute | solution.py:271
  51.4 2.7 %shard_map.57.inverse = f32[128,128]{1,0:T(8,128)S(1)} custom-call(f32[16,40,128]{2,1,0:T(8,128)S(1)} %all_to_all.10.received), custom_call_target="tpu_custom_call" | custom-call | flops 1048576 | bytes 10485760 | tf_op jit(solution)/shard_map/pallas_call | solution.py:26
  54.0 0.3 collective-permute-done.11.w1
  54.3 0.7 shard_map.58
  55.0 11.6 %all_to_all.11.received = f32[16,40,128]{2,1,0:T(8,128)S(1)} all-to-all(f32[16,40,128]{2,1,0:T(8,128)S(1)} %shard_map.58), channel_id=1, replica_groups=mesh['z'=4,'core'=2,'ja'=4,'ka'=4] {'ja','ka'}, dimensions={0} | all-to-all | bytes 655360 | tf_op jit(solution)/shard_map/all_to_all | solution.py:316
  66.6 4.0 %collective-permute-start.14 = (f32[16,40,128]{2,1,0:T(8,128)S(1)}, f32[16,40,128]{2,1,0:T(8,128)S(1)}, u32[]{:S(2)}, u32[]{:S(2)}) collective-permute-start(f32[16,40,128]{2,1,0:T(8,128)S(1)} %all_to_all.11.received), channel_id=1, source_target_pairs={{0,16},{16,0},{1,17},{17,1},{2,18},{18,2},{3,19},{19,3},{4,20},{20... | collective-permute-start | bytes 983048 | tf_op jit(solution)/shard_map/ppermute | solution.py:275
  70.6 1.3 %collective-permute-done.14.swapped = f32[16,40,128]{2,1,0:T(8,128)S(1)} collective-permute-done((f32[16,40,128]{2,1,0:T(8,128)S(1)}, f32[16,40,128]{2,1,0:T(8,128)S(1)}, u32[]{:S(2)}, u32[]{:S(2)}) %collective-permute-start.14) | collective-permute-done | bytes 327712 | tf_op jit(solution)/shard_map/ppermute | solution.py:275
  71.9 1.4 %shard_map.59 = (f32[32,1,1,64]{3,2,1,0:T(1,128)}, f32[32,64,64]{2,1,0:T(8,128)}) custom-call(f32[16,40,128]{2,1,0:T(8,128)S(1)} %all_to_all.11.received, f32[16,40,128]{2,1,0:T(8,128)S(1)} %collective-permute-done.14.swapped), custom_call_target="tpu_custom_call" | custom-call | tf_op jit(solution)/shard_map/pallas_call | solution.py:26
  (12 shorter events, 0.1 us)
Async XLA Ops:
  0.6 29.2 %copy-start = (f32[32,16,64,128]{3,2,1,0:T(8,128)S(1)}, f32[32,16,64,128]{3,2,1,0:T(8,128)}, u32[]{:S(2)}) copy-start(f32[32,16,64,128]{3,2,1,0:T(8,128)} %tensor.5) | copy-start | bytes 50331652
  1.8 6.0 %collective-permute-start.2 = (f32[16,8,128]{2,1,0:T(8,128)S(1)}, f32[16,8,128]{2,1,0:T(8,128)S(1)}, u32[]{:S(2)}, u32[]{:S(2)}) collective-permute-start(f32[16,8,128]{2,1,0:T(8,128)S(1)} %shard_map.50.m0), channel_id=1, source_target_pairs={{0,96},{32,0},{64,32},{96,64},{1,97},{33,1},{65,33},{97,65},{2,98}... | collective-permute-start | bytes 196616 | tf_op jit(solution)/shard_map/ppermute | solution.py:271
  6.4 4.7 %collective-permute-start.1 = (f32[16,8,128]{2,1,0:T(8,128)S(1)}, f32[16,8,128]{2,1,0:T(8,128)S(1)}, u32[]{:S(2)}, u32[]{:S(2)}) collective-permute-start(f32[16,8,128]{2,1,0:T(8,128)S(1)} %shard_map.50.m0), channel_id=1, source_target_pairs={{0,64},{32,96},{64,0},{96,32},{1,65},{33,97},{65,1},{97,33},{2,66}... | collective-permute-start | bytes 196616 | tf_op jit(solution)/shard_map/ppermute | solution.py:271
  6.4 5.0 %collective-permute-start = (f32[16,8,128]{2,1,0:T(8,128)S(1)}, f32[16,8,128]{2,1,0:T(8,128)S(1)}, u32[]{:S(2)}, u32[]{:S(2)}) collective-permute-start(f32[16,8,128]{2,1,0:T(8,128)S(1)} %shard_map.50.m0), channel_id=1, source_target_pairs={{0,32},{32,64},{64,96},{96,0},{1,33},{33,65},{65,97},{97,1},{2,34}... | collective-permute-start | bytes 196616 | tf_op jit(solution)/shard_map/ppermute | solution.py:271
  11.5 6.8 %collective-permute-start.5 = (f32[16,8,128]{2,1,0:T(8,128)S(1)}, f32[16,8,128]{2,1,0:T(8,128)S(1)}, u32[]{:S(2)}, u32[]{:S(2)}) collective-permute-start(f32[16,8,128]{2,1,0:T(8,128)S(1)} %get-tuple-element.4.b0), channel_id=1, source_target_pairs={{0,3},{1,0},{2,1},{3,2},{4,7},{5,4},{6,5},{7,6},{8,11},{9,8},{10,9... | collective-permute-start | bytes 196616 | tf_op jit(solution)/shard_map/ppermute | solution.py:271
  14.3 8.9 %collective-permute-start.8 = (f32[16,16,128]{2,1,0:T(8,128)S(1)}, f32[16,16,128]{2,1,0:T(8,128)S(1)}, u32[]{:S(2)}, u32[]{:S(2)}) collective-permute-start(f32[16,16,128]{2,1,0:T(8,128)S(1)} %get-tuple-element.5.c0), channel_id=1, source_target_pairs={{0,12},{4,0},{8,4},{12,8},{1,13},{5,1},{9,5},{13,9},{2,14},{6,2},{... | collective-permute-start | bytes 393224 | tf_op jit(solution)/shard_map/ppermute | solution.py:271
  16.8 6.5 %collective-permute-start.7 = (f32[16,16,128]{2,1,0:T(8,128)S(1)}, f32[16,16,128]{2,1,0:T(8,128)S(1)}, u32[]{:S(2)}, u32[]{:S(2)}) collective-permute-start(f32[16,16,128]{2,1,0:T(8,128)S(1)} %get-tuple-element.5.c0), channel_id=1, source_target_pairs={{0,8},{4,12},{8,0},{12,4},{1,9},{5,13},{9,1},{13,5},{2,10},{6,14},... | collective-permute-start | bytes 393224 | tf_op jit(solution)/shard_map/ppermute | solution.py:271
  17.3 6.2 %collective-permute-start.6 = (f32[16,16,128]{2,1,0:T(8,128)S(1)}, f32[16,16,128]{2,1,0:T(8,128)S(1)}, u32[]{:S(2)}, u32[]{:S(2)}) collective-permute-start(f32[16,16,128]{2,1,0:T(8,128)S(1)} %get-tuple-element.5.c0), channel_id=1, source_target_pairs={{0,4},{4,8},{8,12},{12,0},{1,5},{5,9},{9,13},{13,1},{2,6},{6,10},{... | collective-permute-start | bytes 393224 | tf_op jit(solution)/shard_map/ppermute | solution.py:271
  17.9 4.7 %collective-permute-start.4 = (f32[16,8,128]{2,1,0:T(8,128)S(1)}, f32[16,8,128]{2,1,0:T(8,128)S(1)}, u32[]{:S(2)}, u32[]{:S(2)}) collective-permute-start(f32[16,8,128]{2,1,0:T(8,128)S(1)} %get-tuple-element.4.b0), channel_id=1, source_target_pairs={{0,2},{1,3},{2,0},{3,1},{4,6},{5,7},{6,4},{7,5},{8,10},{9,11},{10,... | collective-permute-start | bytes 196616 | tf_op jit(solution)/shard_map/ppermute | solution.py:271
  18.3 5.0 %collective-permute-start.3 = (f32[16,8,128]{2,1,0:T(8,128)S(1)}, f32[16,8,128]{2,1,0:T(8,128)S(1)}, u32[]{:S(2)}, u32[]{:S(2)}) collective-permute-start(f32[16,8,128]{2,1,0:T(8,128)S(1)} %get-tuple-element.4.b0), channel_id=1, source_target_pairs={{0,1},{1,2},{2,3},{3,0},{4,5},{5,6},{6,7},{7,4},{8,9},{9,10},{10,1... | collective-permute-start | bytes 196616 | tf_op jit(solution)/shard_map/ppermute | solution.py:271
  23.7 6.1 %collective-permute-start.9 = (f32[16,96,128]{2,1,0:T(8,128)S(1)}, f32[16,96,128]{2,1,0:T(8,128)S(1)}, u32[]{:S(2)}, u32[]{:S(2)}) collective-permute-start(f32[16,96,128]{2,1,0:T(8,128)S(1)} %shard_map.52.mine), channel_id=1, source_target_pairs={{0,16},{16,0},{1,17},{17,1},{2,18},{18,2},{3,19},{19,3},{4,20},{20... | collective-permute-start | bytes 2359304 | tf_op jit(solution)/shard_map/ppermute | solution.py:275
  33.0 3.8 %collective-permute-start.10 = (f32[16,8,128]{2,1,0:T(8,128)S(1)}, f32[16,8,128]{2,1,0:T(8,128)S(1)}, u32[]{:S(2)}, u32[]{:S(2)}) collective-permute-start(f32[16,8,128]{2,1,0:T(8,128)S(1)} %shard_map.54), channel_id=1, source_target_pairs={{0,16},{16,0},{1,17},{17,1},{2,18},{18,2},{3,19},{19,3},{4,20},{20... | collective-permute-start | bytes 196616 | tf_op jit(solution)/shard_map/ppermute | solution.py:275
  49.1 5.0 %collective-permute-start.13 = (f32[16,128]{1,0:T(8,128)S(1)}, f32[16,128]{1,0:T(8,128)S(1)}, u32[]{:S(2)}, u32[]{:S(2)}) collective-permute-start(f32[16,128]{1,0:T(8,128)S(1)} %shard_map.56.w0), channel_id=1, source_target_pairs={{0,96},{32,0},{64,32},{96,64},{1,97},{33,1},{65,33},{97,65},{2,98}... | collective-permute-start | bytes 24584 | tf_op jit(solution)/shard_map/ppermute | solution.py:271
  49.7 4.3 %collective-permute-start.12 = (f32[16,128]{1,0:T(8,128)S(1)}, f32[16,128]{1,0:T(8,128)S(1)}, u32[]{:S(2)}, u32[]{:S(2)}) collective-permute-start(f32[16,128]{1,0:T(8,128)S(1)} %shard_map.56.w0), channel_id=1, source_target_pairs={{0,64},{32,96},{64,0},{96,32},{1,65},{33,97},{65,1},{97,33},{2,66}... | collective-permute-start | bytes 24584 | tf_op jit(solution)/shard_map/ppermute | solution.py:271
  50.6 3.7 %collective-permute-start.11 = (f32[16,128]{1,0:T(8,128)S(1)}, f32[16,128]{1,0:T(8,128)S(1)}, u32[]{:S(2)}, u32[]{:S(2)}) collective-permute-start(f32[16,128]{1,0:T(8,128)S(1)} %shard_map.56.w0), channel_id=1, source_target_pairs={{0,32},{32,64},{64,96},{96,0},{1,33},{33,65},{65,97},{97,1},{2,34}... | collective-permute-start | bytes 24584 | tf_op jit(solution)/shard_map/ppermute | solution.py:271
  66.6 5.3 %collective-permute-start.14 = (f32[16,40,128]{2,1,0:T(8,128)S(1)}, f32[16,40,128]{2,1,0:T(8,128)S(1)}, u32[]{:S(2)}, u32[]{:S(2)}) collective-permute-start(f32[16,40,128]{2,1,0:T(8,128)S(1)} %all_to_all.11.received), channel_id=1, source_target_pairs={{0,16},{16,0},{1,17},{17,1},{2,18},{18,2},{3,19},{19,3},{4,20},{20... | collective-permute-start | bytes 983048 | tf_op jit(solution)/shard_map/ppermute | solution.py:275

commit v6 on v5

--- a/solution.py
+++ b/solution.py
@@ -18,8 +18,9 @@
 MIB = 1024 * 1024
 VMEM = pl.BlockSpec(memory_space=pltpu.VMEM)
 ANY = pl.BlockSpec(memory_space=pl.ANY)
+STEPS = 2
 PANEL = 16
-UNROLL = 8
+UNROLL = 16
 
 
 def call(kernel, out_shape, operands, *, specs=None, scratch=(), vmem=16, cost=None):
@@ -104,7 +105,7 @@
         return [jnp.where(first_core, here, there), jnp.where(first_core, there, here)]
 
     def chosen(v):
-        return jnp.where(side == 0, v, swap_halves(v))
+        return pltpu.roll(v, RANK * side, 1)
 
     b = chosen(jnp.concatenate([part for z in range(N_Z) for part in both(z * nb, nb)], axis=0))
     c = chosen(jnp.concatenate([part for z in range(N_Z) for part in both(JD // 2 + z * nc, nc)], axis=0))
@@ -250,15 +251,16 @@
     _, core, x, y = place()
     upper = x * N_KA + y >= 8
     half = RANK // 2
+    first = pl.program_id(0) * (PAIRS // STEPS)
 
     def unpack(here):
-        for p in range(PAIRS):
+        for n in range(PAIRS // STEPS):
             for side in range(2):
                 source = received if side == here else swapped
-                gram[2 * p + side, :half] = source[p, :half, :RANK]
-                gram[2 * p + side, half:] = source[p, :half, RANK:]
-                row = source[p, half + 4 * here : half + 4 * here + 1, :]
-                rows[2 * p + side, 0] = jnp.where(upper, row[:, RANK:], row[:, :RANK])
+                gram[2 * n + side, :half] = source[first + n, :half, :RANK]
+                gram[2 * n + side, half:] = source[first + n, :half, RANK:]
+                row = source[first + n, half + 4 * here : half + 4 * here + 1, :]
+                rows[2 * n + side, 0] = jnp.where(upper, row[:, RANK:], row[:, :RANK])
 
     for here in range(2):
         pl.when(core == here)(lambda here=here: unpack(here))
@@ -315,8 +317,18 @@
     )
     received = lax.all_to_all(sent, ("ja", "ka"), 0, 0)
     swapped = swap_cores(received)
-    rows, gram = call(unpack_kernel, (f32(FIELDS, 1, 1, RANK), f32(FIELDS, RANK, RANK)), (received, swapped))
-    return rows, gram
+    n = FIELDS // STEPS
+    return pl.pallas_call(
+        unpack_kernel,
+        out_shape=(f32(FIELDS, 1, 1, RANK), f32(FIELDS, RANK, RANK)),
+        grid=(STEPS,),
+        in_specs=[VMEM, VMEM],
+        out_specs=(
+            pl.BlockSpec((n, 1, 1, RANK), lambda i: (i, 0, 0, 0)),
+            pl.BlockSpec((n, RANK, RANK), lambda i: (i, 0, 0)),
+        ),
+        compiler_params=pltpu.CompilerParams(vmem_limit_bytes=16 * MIB),
+    )(received, swapped)
 
 
 def solution(mesh):

time: 73.4 us -> 73.1 us (level)
    pallas_call x10 -> x9, Pallas kernels: 12.7 us -> 11.1 us  [call(): pl.pallas_call(kernel, out_shape=out_shape, in_specs=[VMEM] * len(operand...]
    pallas_call x0 -> x1, Pallas kernels: none -> 1.24 us  [on_device(): pl.pallas_call(unpack_kernel, out_shape=(f32(FIELDS, 1, 1, RANK), f32(FIE...]
where the time goes in v6:
time: 73.1 us; the launch traced here: 73 us
  blocking collectives  23.8 us (33%)
  starting transfers between devices  23.7 us (32%)
  Pallas kernels  12.4 us (17%)
  waiting for transfers between devices  12.3 us (17%)
    all_to_all x2, blocking collectives, on_device(): received = lax.all_to_all(sent, ('ja', 'ka'), 0, 0)  23.8 us
    ppermute x12, starting transfers between devices, around(): return [value] + [lax.ppermute(value, axis, perm) for perm in LINE]  15.1 us
    pallas_call x9, Pallas kernels, call(): pl.pallas_call(kernel, out_shape=out_shape, in_specs=[VMEM] * len(operand...  11.1 us
    ppermute x12, waiting for transfers between devices, around(): return [value] + [lax.ppermute(value, axis, perm) for perm in LINE]  9.15 us
    ppermute x3, starting transfers between devices, swap_cores(): return lax.ppermute(value, 'core', [(0, 1), (1, 0)])  8.65 us
    ppermute x3, waiting for transfers between devices, swap_cores(): return lax.ppermute(value, 'core', [(0, 1), (1, 0)])  3.17 us
  transfers between devices with their start and end apart: 15, of which 9 were waited for; matrix products, arithmetic and copies ran while one was open for 0% of the time, Pallas kernels for 8%

profile of v6, /device:TPU:1, one launch (start us, length us, event | category | flops | bytes accessed | tf_op | source)
XLA Modules:
  0.0 73.0 jit_solution(8083236109252153858)
XLA Ops:
  0.6 1.1 %shard_map.50.m0 = f32[16,8,128]{2,1,0:T(8,128)S(1)} custom-call(f32[32,2,64]{2,1,0:T(2,128)} %bitcast.3, f32[32,4,64]{2,1,0:T(4,128)} %bitcast.2, f32[32,16,64,128]{3,2,1,0:T(8,128)} %tensor.5), custom_call_target="tpu_custom_call" | custom-call | tf_op jit(solution)/shard_map/pallas_call | solution.py:27
  1.8 4.7 %collective-permute-start.2 = (f32[16,8,128]{2,1,0:T(8,128)S(1)}, f32[16,8,128]{2,1,0:T(8,128)S(1)}, u32[]{:S(2)}, u32[]{:S(2)}) collective-permute-start(f32[16,8,128]{2,1,0:T(8,128)S(1)} %shard_map.50.m0), channel_id=1, source_target_pairs={{0,96},{32,0},{64,32},{96,64},{1,97},{33,1},{65,33},{97,65},{2,98}... | collective-permute-start | bytes 196616 | tf_op jit(solution)/shard_map/ppermute | solution.py:273
  6.4 0.7 collective-permute-start
  7.1 0.6 collective-permute-done.2.m3
  7.8 3.4 %collective-permute-done.1.m2 = f32[16,8,128]{2,1,0:T(8,128)S(1)} collective-permute-done((f32[16,8,128]{2,1,0:T(8,128)S(1)}, f32[16,8,128]{2,1,0:T(8,128)S(1)}, u32[]{:S(2)}, u32[]{:S(2)}) %collective-permute-start.1) | collective-permute-done | bytes 65568 | tf_op jit(solution)/shard_map/ppermute | solution.py:273
  11.2 0.3 collective-permute-done.m1
  11.5 2.8 %collective-permute-start.5 = (f32[16,8,128]{2,1,0:T(8,128)S(1)}, f32[16,8,128]{2,1,0:T(8,128)S(1)}, u32[]{:S(2)}, u32[]{:S(2)}) collective-permute-start(f32[16,8,128]{2,1,0:T(8,128)S(1)} %get-tuple-element.4.b0), channel_id=1, source_target_pairs={{0,3},{1,0},{2,1},{3,2},{4,7},{5,4},{6,5},{7,6},{8,11},{9,8},{10,9... | collective-permute-start | bytes 196616 | tf_op jit(solution)/shard_map/ppermute | solution.py:273
  14.3 2.5 %collective-permute-start.8 = (f32[16,16,128]{2,1,0:T(8,128)S(1)}, f32[16,16,128]{2,1,0:T(8,128)S(1)}, u32[]{:S(2)}, u32[]{:S(2)}) collective-permute-start(f32[16,16,128]{2,1,0:T(8,128)S(1)} %get-tuple-element.5.c0), channel_id=1, source_target_pairs={{0,12},{4,0},{8,4},{12,8},{1,13},{5,1},{9,5},{13,9},{2,14},{6,2},{... | collective-permute-start | bytes 393224 | tf_op jit(solution)/shard_map/ppermute | solution.py:273
  16.8 0.5 collective-permute-start.7
  17.3 0.6 collective-permute-start.6
  17.9 0.3 collective-permute-start.4
  18.3 0.7 collective-permute-start.3
  19.0 3.6 %collective-permute-done.4.b2 = f32[16,8,128]{2,1,0:T(8,128)S(1)} collective-permute-done((f32[16,8,128]{2,1,0:T(8,128)S(1)}, f32[16,8,128]{2,1,0:T(8,128)S(1)}, u32[]{:S(2)}, u32[]{:S(2)}) %collective-permute-start.4) | collective-permute-done | bytes 65568 | tf_op jit(solution)/shard_map/ppermute | solution.py:273
  22.6 0.6 collective-permute-done.3.b1
  23.2 0.3 collective-permute-done.6.c1
  23.5 0.2 shard_map.52.mine
  23.7 4.2 %collective-permute-start.9 = (f32[16,96,128]{2,1,0:T(8,128)S(1)}, f32[16,96,128]{2,1,0:T(8,128)S(1)}, u32[]{:S(2)}, u32[]{:S(2)}) collective-permute-start(f32[16,96,128]{2,1,0:T(8,128)S(1)} %shard_map.52.mine), channel_id=1, source_target_pairs={{0,16},{16,0},{1,17},{17,1},{2,18},{18,2},{3,19},{19,3},{4,20},{20... | collective-permute-start | bytes 2359304 | tf_op jit(solution)/shard_map/ppermute | solution.py:277
  27.9 1.9 %collective-permute-done.9.other = f32[16,96,128]{2,1,0:T(8,128)S(1)} collective-permute-done((f32[16,96,128]{2,1,0:T(8,128)S(1)}, f32[16,96,128]{2,1,0:T(8,128)S(1)}, u32[]{:S(2)}, u32[]{:S(2)}) %collective-permute-start.9) | collective-permute-done | bytes 786464 | tf_op jit(solution)/shard_map/ppermute | solution.py:277
  29.8 3.1 %shard_map.54 = f32[16,8,128]{2,1,0:T(8,128)S(1)} custom-call(f32[32,16,64,128]{3,2,1,0:T(8,128)S(1)} %copy-done, f32[16,96,128]{2,1,0:T(8,128)S(1)} %shard_map.52.mine, f32[16,96,128]{2,1,0:T(8,128)S(1)} %collective-permute-done.9.other), custom_call_target="tpu_custom_call" | custom-call | flops 2147483648 | bytes 8388608 | tf_op jit(solution)/shard_map/pallas_call | solution.py:27
  32.9 0.4 collective-permute-start.10
  33.3 3.4 %shard_map.53.sums = f32[16,40,128]{2,1,0:T(8,128)S(1)} custom-call(f32[32,16,64,128]{3,2,1,0:T(8,128)S(1)} %copy-done, f32[16,96,128]{2,1,0:T(8,128)S(1)} %shard_map.52.mine, f32[16,96,128]{2,1,0:T(8,128)S(1)} %collective-permute-done.9.other), custom_call_target="tpu_custom_call" | custom-call | flops 2147483648 | bytes 8388608 | tf_op jit(solution)/shard_map/pallas_call | solution.py:27
  36.7 12.2 %all_to_all.10.received = f32[16,40,128]{2,1,0:T(8,128)S(1)} all-to-all(f32[16,40,128]{2,1,0:T(8,128)S(1)} %shard_map.55), channel_id=1, replica_groups=mesh['z'=4,'core'=2,'ja'=4,'ka'=4] {'ja','ka'}, dimensions={0} | all-to-all | bytes 655360 | tf_op jit(solution)/shard_map/all_to_all | solution.py:303
  48.9 0.7 collective-permute-start.13
  49.6 0.9 %collective-permute-start.12 = (f32[16,128]{1,0:T(8,128)S(1)}, f32[16,128]{1,0:T(8,128)S(1)}, u32[]{:S(2)}, u32[]{:S(2)}) collective-permute-start(f32[16,128]{1,0:T(8,128)S(1)} %shard_map.56.w0), channel_id=1, source_target_pairs={{0,64},{32,96},{64,0},{96,32},{1,65},{33,97},{65,1},{97,33},{2,66}... | collective-permute-start | bytes 24584 | tf_op jit(solution)/shard_map/ppermute | solution.py:273
  50.4 0.8 %collective-permute-start.11 = (f32[16,128]{1,0:T(8,128)S(1)}, f32[16,128]{1,0:T(8,128)S(1)}, u32[]{:S(2)}, u32[]{:S(2)}) collective-permute-start(f32[16,128]{1,0:T(8,128)S(1)} %shard_map.56.w0), channel_id=1, source_target_pairs={{0,32},{32,64},{64,96},{96,0},{1,33},{33,65},{65,97},{97,1},{2,34}... | collective-permute-start | bytes 24584 | tf_op jit(solution)/shard_map/ppermute | solution.py:273
  51.2 2.7 %shard_map.57.inverse = f32[128,128]{1,0:T(8,128)S(1)} custom-call(f32[16,40,128]{2,1,0:T(8,128)S(1)} %all_to_all.10.received), custom_call_target="tpu_custom_call" | custom-call | flops 1048576 | bytes 10485760 | tf_op jit(solution)/shard_map/pallas_call | solution.py:27
  53.9 0.3 collective-permute-done.11.w1
  54.1 0.7 shard_map.58
  54.8 11.6 %all_to_all.11.received = f32[16,40,128]{2,1,0:T(8,128)S(1)} all-to-all(f32[16,40,128]{2,1,0:T(8,128)S(1)} %shard_map.58), channel_id=1, replica_groups=mesh['z'=4,'core'=2,'ja'=4,'ka'=4] {'ja','ka'}, dimensions={0} | all-to-all | bytes 655360 | tf_op jit(solution)/shard_map/all_to_all | solution.py:318
  66.4 4.0 %collective-permute-start.14 = (f32[16,40,128]{2,1,0:T(8,128)S(1)}, f32[16,40,128]{2,1,0:T(8,128)S(1)}, u32[]{:S(2)}, u32[]{:S(2)}) collective-permute-start(f32[16,40,128]{2,1,0:T(8,128)S(1)} %all_to_all.11.received), channel_id=1, source_target_pairs={{0,16},{16,0},{1,17},{17,1},{2,18},{18,2},{3,19},{19,3},{4,20},{20... | collective-permute-start | bytes 983048 | tf_op jit(solution)/shard_map/ppermute | solution.py:277
  70.5 1.3 %collective-permute-done.14.swapped = f32[16,40,128]{2,1,0:T(8,128)S(1)} collective-permute-done((f32[16,40,128]{2,1,0:T(8,128)S(1)}, f32[16,40,128]{2,1,0:T(8,128)S(1)}, u32[]{:S(2)}, u32[]{:S(2)}) %collective-permute-start.14) | collective-permute-done | bytes 327712 | tf_op jit(solution)/shard_map/ppermute | solution.py:277
  71.7 1.2 %shard_map.59 = (f32[32,1,1,64]{3,2,1,0:T(1,128)}, f32[32,64,64]{2,1,0:T(8,128)}) custom-call(f32[16,40,128]{2,1,0:T(8,128)S(1)} %all_to_all.11.received, f32[16,40,128]{2,1,0:T(8,128)S(1)} %collective-permute-done.14.swapped), custom_call_target="tpu_custom_call" | custom-call | tf_op jit(solution)/shard_map/pallas_call | solution.py:321
  (12 shorter events, 0.1 us)
Async XLA Ops:
  0.6 29.2 %copy-start = (f32[32,16,64,128]{3,2,1,0:T(8,128)S(1)}, f32[32,16,64,128]{3,2,1,0:T(8,128)}, u32[]{:S(2)}) copy-start(f32[32,16,64,128]{3,2,1,0:T(8,128)} %tensor.5) | copy-start | bytes 50331652
  1.8 6.0 %collective-permute-start.2 = (f32[16,8,128]{2,1,0:T(8,128)S(1)}, f32[16,8,128]{2,1,0:T(8,128)S(1)}, u32[]{:S(2)}, u32[]{:S(2)}) collective-permute-start(f32[16,8,128]{2,1,0:T(8,128)S(1)} %shard_map.50.m0), channel_id=1, source_target_pairs={{0,96},{32,0},{64,32},{96,64},{1,97},{33,1},{65,33},{97,65},{2,98}... | collective-permute-start | bytes 196616 | tf_op jit(solution)/shard_map/ppermute | solution.py:273
  6.4 4.7 %collective-permute-start.1 = (f32[16,8,128]{2,1,0:T(8,128)S(1)}, f32[16,8,128]{2,1,0:T(8,128)S(1)}, u32[]{:S(2)}, u32[]{:S(2)}) collective-permute-start(f32[16,8,128]{2,1,0:T(8,128)S(1)} %shard_map.50.m0), channel_id=1, source_target_pairs={{0,64},{32,96},{64,0},{96,32},{1,65},{33,97},{65,1},{97,33},{2,66}... | collective-permute-start | bytes 196616 | tf_op jit(solution)/shard_map/ppermute | solution.py:273
  6.4 5.0 %collective-permute-start = (f32[16,8,128]{2,1,0:T(8,128)S(1)}, f32[16,8,128]{2,1,0:T(8,128)S(1)}, u32[]{:S(2)}, u32[]{:S(2)}) collective-permute-start(f32[16,8,128]{2,1,0:T(8,128)S(1)} %shard_map.50.m0), channel_id=1, source_target_pairs={{0,32},{32,64},{64,96},{96,0},{1,33},{33,65},{65,97},{97,1},{2,34}... | collective-permute-start | bytes 196616 | tf_op jit(solution)/shard_map/ppermute | solution.py:273
  11.5 6.8 %collective-permute-start.5 = (f32[16,8,128]{2,1,0:T(8,128)S(1)}, f32[16,8,128]{2,1,0:T(8,128)S(1)}, u32[]{:S(2)}, u32[]{:S(2)}) collective-permute-start(f32[16,8,128]{2,1,0:T(8,128)S(1)} %get-tuple-element.4.b0), channel_id=1, source_target_pairs={{0,3},{1,0},{2,1},{3,2},{4,7},{5,4},{6,5},{7,6},{8,11},{9,8},{10,9... | collective-permute-start | bytes 196616 | tf_op jit(solution)/shard_map/ppermute | solution.py:273
  14.3 8.9 %collective-permute-start.8 = (f32[16,16,128]{2,1,0:T(8,128)S(1)}, f32[16,16,128]{2,1,0:T(8,128)S(1)}, u32[]{:S(2)}, u32[]{:S(2)}) collective-permute-start(f32[16,16,128]{2,1,0:T(8,128)S(1)} %get-tuple-element.5.c0), channel_id=1, source_target_pairs={{0,12},{4,0},{8,4},{12,8},{1,13},{5,1},{9,5},{13,9},{2,14},{6,2},{... | collective-permute-start | bytes 393224 | tf_op jit(solution)/shard_map/ppermute | solution.py:273
  16.8 6.5 %collective-permute-start.7 = (f32[16,16,128]{2,1,0:T(8,128)S(1)}, f32[16,16,128]{2,1,0:T(8,128)S(1)}, u32[]{:S(2)}, u32[]{:S(2)}) collective-permute-start(f32[16,16,128]{2,1,0:T(8,128)S(1)} %get-tuple-element.5.c0), channel_id=1, source_target_pairs={{0,8},{4,12},{8,0},{12,4},{1,9},{5,13},{9,1},{13,5},{2,10},{6,14},... | collective-permute-start | bytes 393224 | tf_op jit(solution)/shard_map/ppermute | solution.py:273
  17.3 6.2 %collective-permute-start.6 = (f32[16,16,128]{2,1,0:T(8,128)S(1)}, f32[16,16,128]{2,1,0:T(8,128)S(1)}, u32[]{:S(2)}, u32[]{:S(2)}) collective-permute-start(f32[16,16,128]{2,1,0:T(8,128)S(1)} %get-tuple-element.5.c0), channel_id=1, source_target_pairs={{0,4},{4,8},{8,12},{12,0},{1,5},{5,9},{9,13},{13,1},{2,6},{6,10},{... | collective-permute-start | bytes 393224 | tf_op jit(solution)/shard_map/ppermute | solution.py:273
  17.9 4.7 %collective-permute-start.4 = (f32[16,8,128]{2,1,0:T(8,128)S(1)}, f32[16,8,128]{2,1,0:T(8,128)S(1)}, u32[]{:S(2)}, u32[]{:S(2)}) collective-permute-start(f32[16,8,128]{2,1,0:T(8,128)S(1)} %get-tuple-element.4.b0), channel_id=1, source_target_pairs={{0,2},{1,3},{2,0},{3,1},{4,6},{5,7},{6,4},{7,5},{8,10},{9,11},{10,... | collective-permute-start | bytes 196616 | tf_op jit(solution)/shard_map/ppermute | solution.py:273
  18.3 5.0 %collective-permute-start.3 = (f32[16,8,128]{2,1,0:T(8,128)S(1)}, f32[16,8,128]{2,1,0:T(8,128)S(1)}, u32[]{:S(2)}, u32[]{:S(2)}) collective-permute-start(f32[16,8,128]{2,1,0:T(8,128)S(1)} %get-tuple-element.4.b0), channel_id=1, source_target_pairs={{0,1},{1,2},{2,3},{3,0},{4,5},{5,6},{6,7},{7,4},{8,9},{9,10},{10,1... | collective-permute-start | bytes 196616 | tf_op jit(solution)/shard_map/ppermute | solution.py:273
  23.7 6.1 %collective-permute-start.9 = (f32[16,96,128]{2,1,0:T(8,128)S(1)}, f32[16,96,128]{2,1,0:T(8,128)S(1)}, u32[]{:S(2)}, u32[]{:S(2)}) collective-permute-start(f32[16,96,128]{2,1,0:T(8,128)S(1)} %shard_map.52.mine), channel_id=1, source_target_pairs={{0,16},{16,0},{1,17},{17,1},{2,18},{18,2},{3,19},{19,3},{4,20},{20... | collective-permute-start | bytes 2359304 | tf_op jit(solution)/shard_map/ppermute | solution.py:277
  32.9 3.8 %collective-permute-start.10 = (f32[16,8,128]{2,1,0:T(8,128)S(1)}, f32[16,8,128]{2,1,0:T(8,128)S(1)}, u32[]{:S(2)}, u32[]{:S(2)}) collective-permute-start(f32[16,8,128]{2,1,0:T(8,128)S(1)} %shard_map.54), channel_id=1, source_target_pairs={{0,16},{16,0},{1,17},{17,1},{2,18},{18,2},{3,19},{19,3},{4,20},{20... | collective-permute-start | bytes 196616 | tf_op jit(solution)/shard_map/ppermute | solution.py:277
  48.9 5.0 %collective-permute-start.13 = (f32[16,128]{1,0:T(8,128)S(1)}, f32[16,128]{1,0:T(8,128)S(1)}, u32[]{:S(2)}, u32[]{:S(2)}) collective-permute-start(f32[16,128]{1,0:T(8,128)S(1)} %shard_map.56.w0), channel_id=1, source_target_pairs={{0,96},{32,0},{64,32},{96,64},{1,97},{33,1},{65,33},{97,65},{2,98}... | collective-permute-start | bytes 24584 | tf_op jit(solution)/shard_map/ppermute | solution.py:273
  49.6 4.3 %collective-permute-start.12 = (f32[16,128]{1,0:T(8,128)S(1)}, f32[16,128]{1,0:T(8,128)S(1)}, u32[]{:S(2)}, u32[]{:S(2)}) collective-permute-start(f32[16,128]{1,0:T(8,128)S(1)} %shard_map.56.w0), channel_id=1, source_target_pairs={{0,64},{32,96},{64,0},{96,32},{1,65},{33,97},{65,1},{97,33},{2,66}... | collective-permute-start | bytes 24584 | tf_op jit(solution)/shard_map/ppermute | solution.py:273
  50.4 3.7 %collective-permute-start.11 = (f32[16,128]{1,0:T(8,128)S(1)}, f32[16,128]{1,0:T(8,128)S(1)}, u32[]{:S(2)}, u32[]{:S(2)}) collective-permute-start(f32[16,128]{1,0:T(8,128)S(1)} %shard_map.56.w0), channel_id=1, source_target_pairs={{0,32},{32,64},{64,96},{96,0},{1,33},{33,65},{65,97},{97,1},{2,34}... | collective-permute-start | bytes 24584 | tf_op jit(solution)/shard_map/ppermute | solution.py:273
  66.4 5.3 %collective-permute-start.14 = (f32[16,40,128]{2,1,0:T(8,128)S(1)}, f32[16,40,128]{2,1,0:T(8,128)S(1)}, u32[]{:S(2)}, u32[]{:S(2)}) collective-permute-start(f32[16,40,128]{2,1,0:T(8,128)S(1)} %all_to_all.11.received), channel_id=1, source_target_pairs={{0,16},{16,0},{1,17},{17,1},{2,18},{18,2},{3,19},{19,3},{4,20},{20... | collective-permute-start | bytes 983048 | tf_op jit(solution)/shard_map/ppermute | solution.py:277

commit v7 on v3

--- a/solution.py
+++ b/solution.py
@@ -19,8 +19,9 @@
 MIB = 1024 * 1024
 VMEM = pl.BlockSpec(memory_space=pltpu.VMEM)
 ANY = pl.BlockSpec(memory_space=pl.ANY)
+STEPS = 2
 PANEL = 16
-UNROLL = 4
+UNROLL = 16
 
 
 def call(kernel, out_shape, operands, *, specs=None, scratch=(), vmem=16, cost=None):
@@ -202,8 +203,10 @@
     whole = jnp.concatenate(panels, axis=0)
     pivots = jnp.sum(jnp.where(lane == row, whole, 0.0), axis=1, keepdims=True)
     inverse = jnp.where(lane >= RANK, whole * lax.rsqrt(pivots), 0.0)
-    out[:RANK, :] = swap_halves(inverse)
-    out[RANK:, :] = inverse
+    twice = jnp.concatenate([swap_halves(inverse), inverse], axis=0)
+    out[...] = lax.dot_general(
+        twice, twice, (((0,), (0,)), ((), ())), precision=HIGH, preferred_element_type=jnp.float32
+    )
 
 
 def finish_kernel(w0, w1, w2, w3, inverse, out, every, rows):
@@ -211,30 +214,34 @@
     for s, part in enumerate((w0, w1, w2, w3)):
         at = lax.rem(z - s + N_Z, N_Z) * 16
         every[pl.ds(pl.multiple_of(at, 16), 16), :] = part[...]
-    inv = inverse[...]
-    half = lax.dot_general(every[...], inv, (((1,), (1,)), ((), ())), precision=HIGH, preferred_element_type=jnp.float32)
-    solved = jnp.dot(half, inv, precision=HIGH, preferred_element_type=jnp.float32)
+    solved = jnp.dot(every[...], inverse[...], precision=HIGH, preferred_element_type=jnp.float32)
     rows[...] = solved
     gram = fold(rows_gram(solved) * (1.0 / I_ALL))
     own = rows[pl.ds(pl.multiple_of(z * 16, 16), 16), :]
-    for core in range(2):
-        for q in range(ID):
-            out[core * PAIRS + q, : RANK // 2, :] = gram
-            row = core * 8 + q % 8
-            out[core * PAIRS + q, RANK // 2 :, :] = jnp.broadcast_to(own[row : row + 1], (8, 2 * RANK))
-
-
-def unpack_kernel(received, rows, gram):
-    _, _, x, y = place()
+    for q in range(ID):
+        out[q, : RANK // 2, :] = gram
+        for core in range(2):
+            row, at = core * 8 + q % 8, RANK // 2 + core * 4
+            out[q, at : at + 4, :] = jnp.broadcast_to(own[row : row + 1], (4, 2 * RANK))
+
+
+def unpack_kernel(received, swapped, rows, gram):
+    _, core, x, y = place()
     upper = x * N_KA + y >= 8
     half = RANK // 2
-    for p in range(PAIRS):
-        for side in range(2):
-            source = side * PAIRS + p
-            gram[2 * p + side, :half] = received[source, :half, :RANK]
-            gram[2 * p + side, half:] = received[source, :half, RANK:]
-            row = received[source, half : half + 1, :]
-            rows[2 * p + side, 0] = jnp.where(upper, row[:, RANK:], row[:, :RANK])
+    first = pl.program_id(0) * (PAIRS // STEPS)
+
+    def unpack(here):
+        for n in range(PAIRS // STEPS):
+            for side in range(2):
+                source = received if side == here else swapped
+                gram[2 * n + side, :half] = source[first + n, :half, :RANK]
+                gram[2 * n + side, half:] = source[first + n, :half, RANK:]
+                row = source[first + n, half + 4 * here : half + 4 * here + 1, :]
+                rows[2 * n + side, 0] = jnp.where(upper, row[:, RANK:], row[:, :RANK])
+
+    for here in range(2):
+        pl.when(core == here)(lambda here=here: unpack(here))
 
 
 LINE = [[(i, (i + s) % 4) for i in range(4)] for s in range(1, 4)]
@@ -242,6 +249,10 @@
 
 def around(value, axis):
     return [value] + [lax.ppermute(value, axis, perm) for perm in LINE]
+
+
+def swap_cores(value):
+    return lax.ppermute(value, "core", [(0, 1), (1, 0)])
 
 
 def on_device(tensor, factor_b, factor_c):
@@ -261,7 +272,7 @@
     b, c = call(along_z_kernel, (f32(PAIRS, 8, 2 * RANK), f32(PAIRS, 16, 2 * RANK)), parts)
     parts = around(b, "ka") + around(c, "ja")
     mine = call(along_xy_kernel, f32(PAIRS, 96, 2 * RANK), parts)
-    other = lax.ppermute(mine, "core", [(0, 1), (1, 0)])
+    other = swap_cores(mine)
     sent = call(
         mttkrp_kernel,
         f32(OWNERS, 24, 2 * RANK),
@@ -280,13 +291,24 @@
     )
     sent = call(
         finish_kernel,
-        f32(OWNERS, RANK // 2 + 8, 2 * RANK),
+        f32(PAIRS, RANK // 2 + 8, 2 * RANK),
         (*parts, inverse),
         scratch=[pltpu.VMEM((I_ALL // 2, 2 * RANK), jnp.float32)] * 2,
     )
-    received = lax.all_to_all(sent, ("core", "ja", "ka"), 0, 0)
-    rows, gram = call(unpack_kernel, (f32(FIELDS, 1, 1, RANK), f32(FIELDS, RANK, RANK)), (received,))
-    return rows, gram
+    received = lax.all_to_all(sent, ("ja", "ka"), 0, 0)
+    swapped = swap_cores(received)
+    n = FIELDS // STEPS
+    return pl.pallas_call(
+        unpack_kernel,
+        out_shape=(f32(FIELDS, 1, 1, RANK), f32(FIELDS, RANK, RANK)),
+        grid=(STEPS,),
+        in_specs=[VMEM, VMEM],
+        out_specs=(
+            pl.BlockSpec((n, 1, 1, RANK), lambda i: (i, 0, 0, 0)),
+            pl.BlockSpec((n, RANK, RANK), lambda i: (i, 0, 0)),
+        ),
+        compiler_params=pltpu.CompilerParams(vmem_limit_bytes=16 * MIB),
+    )(received, swapped)
 
 
 def solution(mesh):

time: 76 us -> 72.1 us (0.949)
  blocking collectives: 32.4 us -> 25.5 us
  starting transfers between devices: 19.3 us -> 22.4 us
  Pallas kernels: 12 us -> 11 us
  waiting for transfers between devices: 11.4 us -> 12.3 us
    all_to_all x2 -> x1, blocking collectives: 32.4 us -> 14.7 us  [on_device(): received = lax.all_to_all(sent, ('core', 'ja', 'ka'), 0, 0)]
    all_to_all x0 -> x1, blocking collectives: none -> 10.8 us  [on_device(): received = lax.all_to_all(sent, ('ja', 'ka'), 0, 0)]
    ppermute x1 -> x2, starting transfers between devices: 4.2 us -> 7.36 us  [swap_cores(): return lax.ppermute(value, 'core', [(0, 1), (1, 0)])]
    pallas_call x8 -> x7, Pallas kernels: 12 us -> 9.79 us  [call(): pl.pallas_call(kernel, out_shape=out_shape, in_specs=[VMEM] * len(operand...]
    ppermute x1 -> x2, waiting for transfers between devices: 1.91 us -> 3.17 us  [swap_cores(): return lax.ppermute(value, 'core', [(0, 1), (1, 0)])]
    pallas_call x0 -> x1, Pallas kernels: none -> 1.24 us  [on_device(): pl.pallas_call(unpack_kernel, out_shape=(f32(FIELDS, 1, 1, RANK), f32(FIE...]
  transfers between devices with their start and end apart: 13 -> 14, of which waited for: 9 -> 9; matrix products, arithmetic and copies ran while one was open for 0% -> 0% of each run, Pallas kernels for 3% -> 4%
where the time goes in v7:
time: 72.1 us; the launch traced here: 72 us
  blocking collectives  25.5 us (35%)
  starting transfers between devices  22.4 us (31%)
  waiting for transfers between devices  12.3 us (17%)
  Pallas kernels  11 us (15%)
    ppermute x12, starting transfers between devices, around(): return [value] + [lax.ppermute(value, axis, perm) for perm in LINE]  15.1 us
    all_to_all x1, blocking collectives, on_device(): received = lax.all_to_all(sent, ('core', 'ja', 'ka'), 0, 0)  14.7 us
    all_to_all x1, blocking collectives, on_device(): received = lax.all_to_all(sent, ('ja', 'ka'), 0, 0)  10.8 us
    pallas_call x7, Pallas kernels, call(): pl.pallas_call(kernel, out_shape=out_shape, in_specs=[VMEM] * len(operand...  9.79 us
    ppermute x12, waiting for transfers between devices, around(): return [value] + [lax.ppermute(value, axis, perm) for perm in LINE]  9.15 us
    ppermute x2, starting transfers between devices, swap_cores(): return lax.ppermute(value, 'core', [(0, 1), (1, 0)])  7.36 us
    ppermute x2, waiting for transfers between devices, swap_cores(): return lax.ppermute(value, 'core', [(0, 1), (1, 0)])  3.17 us
  transfers between devices with their start and end apart: 14, of which 9 were waited for; matrix products, arithmetic and copies ran while one was open for 0% of the time, Pallas kernels for 4%

profile of v7, /device:TPU:1, one launch (start us, length us, event | category | flops | bytes accessed | tf_op | source)
XLA Modules:
  0.0 72.0 jit_solution(14467129087800483474)
XLA Ops:
  0.6 1.1 %shard_map.50.m0 = f32[16,8,128]{2,1,0:T(8,128)S(1)} custom-call(f32[32,2,64]{2,1,0:T(2,128)} %bitcast.3, f32[32,4,64]{2,1,0:T(4,128)} %bitcast.2, f32[32,16,64,128]{3,2,1,0:T(8,128)} %tensor.3), custom_call_target="tpu_custom_call" | custom-call | tf_op jit(solution)/shard_map/pallas_call | solution.py:28
  1.8 4.7 %collective-permute-start.2 = (f32[16,8,128]{2,1,0:T(8,128)S(1)}, f32[16,8,128]{2,1,0:T(8,128)S(1)}, u32[]{:S(2)}, u32[]{:S(2)}) collective-permute-start(f32[16,8,128]{2,1,0:T(8,128)S(1)} %shard_map.50.m0), channel_id=1, source_target_pairs={{0,96},{32,0},{64,32},{96,64},{1,97},{33,1},{65,33},{97,65},{2,98}... | collective-permute-start | bytes 196616 | tf_op jit(solution)/shard_map/ppermute | solution.py:251
  6.4 0.0 collective-permute-start.1
  6.4 0.7 collective-permute-start
  7.1 0.6 collective-permute-done.2.m3
  7.8 3.4 %collective-permute-done.1.m2 = f32[16,8,128]{2,1,0:T(8,128)S(1)} collective-permute-done((f32[16,8,128]{2,1,0:T(8,128)S(1)}, f32[16,8,128]{2,1,0:T(8,128)S(1)}, u32[]{:S(2)}, u32[]{:S(2)}) %collective-permute-start.1) | collective-permute-done | bytes 65568 | tf_op jit(solution)/shard_map/ppermute | solution.py:251
  11.2 0.3 collective-permute-done.m1
  11.5 2.8 %collective-permute-start.5 = (f32[16,8,128]{2,1,0:T(8,128)S(1)}, f32[16,8,128]{2,1,0:T(8,128)S(1)}, u32[]{:S(2)}, u32[]{:S(2)}) collective-permute-start(f32[16,8,128]{2,1,0:T(8,128)S(1)} %get-tuple-element.4.b0), channel_id=1, source_target_pairs={{0,3},{1,0},{2,1},{3,2},{4,7},{5,4},{6,5},{7,6},{8,11},{9,8},{10,9... | collective-permute-start | bytes 196616 | tf_op jit(solution)/shard_map/ppermute | solution.py:251
  14.3 2.5 %collective-permute-start.8 = (f32[16,16,128]{2,1,0:T(8,128)S(1)}, f32[16,16,128]{2,1,0:T(8,128)S(1)}, u32[]{:S(2)}, u32[]{:S(2)}) collective-permute-start(f32[16,16,128]{2,1,0:T(8,128)S(1)} %get-tuple-element.5.c0), channel_id=1, source_target_pairs={{0,12},{4,0},{8,4},{12,8},{1,13},{5,1},{9,5},{13,9},{2,14},{6,2},{... | collective-permute-start | bytes 393224 | tf_op jit(solution)/shard_map/ppermute | solution.py:251
  16.8 0.5 collective-permute-start.7
  17.3 0.6 collective-permute-start.6
  17.9 0.3 collective-permute-start.4
  18.3 0.0 collective-permute-done.5.b3
  18.3 0.7 collective-permute-start.3
  19.0 3.6 %collective-permute-done.4.b2 = f32[16,8,128]{2,1,0:T(8,128)S(1)} collective-permute-done((f32[16,8,128]{2,1,0:T(8,128)S(1)}, f32[16,8,128]{2,1,0:T(8,128)S(1)}, u32[]{:S(2)}, u32[]{:S(2)}) %collective-permute-start.4) | collective-permute-done | bytes 65568 | tf_op jit(solution)/shard_map/ppermute | solution.py:251
  22.6 0.6 collective-permute-done.3.b1
  23.2 0.3 collective-permute-done.6.c1
  23.5 0.2 shard_map.52.mine
  23.7 4.2 %collective-permute-start.9 = (f32[16,96,128]{2,1,0:T(8,128)S(1)}, f32[16,96,128]{2,1,0:T(8,128)S(1)}, u32[]{:S(2)}, u32[]{:S(2)}) collective-permute-start(f32[16,96,128]{2,1,0:T(8,128)S(1)} %shard_map.52.mine), channel_id=1, source_target_pairs={{0,16},{16,0},{1,17},{17,1},{2,18},{18,2},{3,19},{19,3},{4,20},{20... | collective-permute-start | bytes 2359304 | tf_op jit(solution)/shard_map/ppermute | solution.py:255
  27.9 1.9 %collective-permute-done.9.other = f32[16,96,128]{2,1,0:T(8,128)S(1)} collective-permute-done((f32[16,96,128]{2,1,0:T(8,128)S(1)}, f32[16,96,128]{2,1,0:T(8,128)S(1)}, u32[]{:S(2)}, u32[]{:S(2)}) %collective-permute-start.9) | collective-permute-done | bytes 786464 | tf_op jit(solution)/shard_map/ppermute | solution.py:255
  29.8 5.1 %shard_map.53 = f32[32,24,128]{2,1,0:T(8,128)S(1)} custom-call(f32[32,16,64,128]{3,2,1,0:T(8,128)S(1)} %copy-done, f32[16,96,128]{2,1,0:T(8,128)S(1)} %shard_map.52.mine, f32[16,96,128]{2,1,0:T(8,128)S(1)} %collective-permute-done.9.other), custom_call_target="tpu_custom_call" | custom-call | flops 4294967296 | bytes 16777216 | tf_op jit(solution)/shard_map/pallas_call | solution.py:28
  34.9 14.7 %all_to_all.10.received = f32[32,24,128]{2,1,0:T(8,128)S(1)} all-to-all(f32[32,24,128]{2,1,0:T(8,128)S(1)} %shard_map.53), channel_id=1, replica_groups=mesh['z'=4,'core'=2,'ja'=4,'ka'=4] {'core','ja','ka'}, dimensions={0} | all-to-all | bytes 786432 | tf_op jit(solution)/shard_map/all_to_all | solution.py:283
  49.6 0.6 collective-permute-start.12
  50.3 0.9 %collective-permute-start.11 = (f32[16,128]{1,0:T(8,128)S(1)}, f32[16,128]{1,0:T(8,128)S(1)}, u32[]{:S(2)}, u32[]{:S(2)}) collective-permute-start(f32[16,128]{1,0:T(8,128)S(1)} %shard_map.54.w0), channel_id=1, source_target_pairs={{0,64},{32,96},{64,0},{96,32},{1,65},{33,97},{65,1},{97,33},{2,66}... | collective-permute-start | bytes 24584 | tf_op jit(solution)/shard_map/ppermute | solution.py:251
  51.1 0.8 %collective-permute-start.10 = (f32[16,128]{1,0:T(8,128)S(1)}, f32[16,128]{1,0:T(8,128)S(1)}, u32[]{:S(2)}, u32[]{:S(2)}) collective-permute-start(f32[16,128]{1,0:T(8,128)S(1)} %shard_map.54.w0), channel_id=1, source_target_pairs={{0,32},{32,64},{64,96},{96,0},{1,33},{33,65},{65,97},{97,1},{2,34}... | collective-permute-start | bytes 24584 | tf_op jit(solution)/shard_map/ppermute | solution.py:251
  51.9 2.7 %shard_map.55.inverse = f32[128,128]{1,0:T(8,128)S(1)} custom-call(f32[32,24,128]{2,1,0:T(8,128)S(1)} %all_to_all.10.received), custom_call_target="tpu_custom_call" | custom-call | flops 1048576 | bytes 10485760 | tf_op jit(solution)/shard_map/pallas_call | solution.py:28
  54.6 0.3 collective-permute-done.10.w1
  54.8 0.7 shard_map.56
  55.5 10.8 %all_to_all.11.received = f32[16,40,128]{2,1,0:T(8,128)S(1)} all-to-all(f32[16,40,128]{2,1,0:T(8,128)S(1)} %shard_map.56), channel_id=1, replica_groups=mesh['z'=4,'core'=2,'ja'=4,'ka'=4] {'ja','ka'}, dimensions={0} | all-to-all | bytes 655360 | tf_op jit(solution)/shard_map/all_to_all | solution.py:298
  66.3 3.2 %collective-permute-start.13 = (f32[16,40,128]{2,1,0:T(8,128)S(1)}, f32[16,40,128]{2,1,0:T(8,128)S(1)}, u32[]{:S(2)}, u32[]{:S(2)}) collective-permute-start(f32[16,40,128]{2,1,0:T(8,128)S(1)} %all_to_all.11.received), channel_id=1, source_target_pairs={{0,16},{16,0},{1,17},{17,1},{2,18},{18,2},{3,19},{19,3},{4,20},{20... | collective-permute-start | bytes 983048 | tf_op jit(solution)/shard_map/ppermute | solution.py:255
  69.5 1.3 %collective-permute-done.13.swapped = f32[16,40,128]{2,1,0:T(8,128)S(1)} collective-permute-done((f32[16,40,128]{2,1,0:T(8,128)S(1)}, f32[16,40,128]{2,1,0:T(8,128)S(1)}, u32[]{:S(2)}, u32[]{:S(2)}) %collective-permute-start.13) | collective-permute-done | bytes 327712 | tf_op jit(solution)/shard_map/ppermute | solution.py:255
  70.7 1.2 %shard_map.57 = (f32[32,1,1,64]{3,2,1,0:T(1,128)}, f32[32,64,64]{2,1,0:T(8,128)}) custom-call(f32[16,40,128]{2,1,0:T(8,128)S(1)} %all_to_all.11.received, f32[16,40,128]{2,1,0:T(8,128)S(1)} %collective-permute-done.13.swapped), custom_call_target="tpu_custom_call" | custom-call | tf_op jit(solution)/shard_map/pallas_call | solution.py:301
  (8 shorter events, 0.1 us)
Async XLA Ops:
  0.6 29.2 %copy-start = (f32[32,16,64,128]{3,2,1,0:T(8,128)S(1)}, f32[32,16,64,128]{3,2,1,0:T(8,128)}, u32[]{:S(2)}) copy-start(f32[32,16,64,128]{3,2,1,0:T(8,128)} %tensor.3) | copy-start | bytes 50331652
  1.8 6.0 %collective-permute-start.2 = (f32[16,8,128]{2,1,0:T(8,128)S(1)}, f32[16,8,128]{2,1,0:T(8,128)S(1)}, u32[]{:S(2)}, u32[]{:S(2)}) collective-permute-start(f32[16,8,128]{2,1,0:T(8,128)S(1)} %shard_map.50.m0), channel_id=1, source_target_pairs={{0,96},{32,0},{64,32},{96,64},{1,97},{33,1},{65,33},{97,65},{2,98}... | collective-permute-start | bytes 196616 | tf_op jit(solution)/shard_map/ppermute | solution.py:251
  6.4 4.7 %collective-permute-start.1 = (f32[16,8,128]{2,1,0:T(8,128)S(1)}, f32[16,8,128]{2,1,0:T(8,128)S(1)}, u32[]{:S(2)}, u32[]{:S(2)}) collective-permute-start(f32[16,8,128]{2,1,0:T(8,128)S(1)} %shard_map.50.m0), channel_id=1, source_target_pairs={{0,64},{32,96},{64,0},{96,32},{1,65},{33,97},{65,1},{97,33},{2,66}... | collective-permute-start | bytes 196616 | tf_op jit(solution)/shard_map/ppermute | solution.py:251
  6.4 5.0 %collective-permute-start = (f32[16,8,128]{2,1,0:T(8,128)S(1)}, f32[16,8,128]{2,1,0:T(8,128)S(1)}, u32[]{:S(2)}, u32[]{:S(2)}) collective-permute-start(f32[16,8,128]{2,1,0:T(8,128)S(1)} %shard_map.50.m0), channel_id=1, source_target_pairs={{0,32},{32,64},{64,96},{96,0},{1,33},{33,65},{65,97},{97,1},{2,34}... | collective-permute-start | bytes 196616 | tf_op jit(solution)/shard_map/ppermute | solution.py:251
  11.5 6.8 %collective-permute-start.5 = (f32[16,8,128]{2,1,0:T(8,128)S(1)}, f32[16,8,128]{2,1,0:T(8,128)S(1)}, u32[]{:S(2)}, u32[]{:S(2)}) collective-permute-start(f32[16,8,128]{2,1,0:T(8,128)S(1)} %get-tuple-element.4.b0), channel_id=1, source_target_pairs={{0,3},{1,0},{2,1},{3,2},{4,7},{5,4},{6,5},{7,6},{8,11},{9,8},{10,9... | collective-permute-start | bytes 196616 | tf_op jit(solution)/shard_map/ppermute | solution.py:251
  14.3 8.9 %collective-permute-start.8 = (f32[16,16,128]{2,1,0:T(8,128)S(1)}, f32[16,16,128]{2,1,0:T(8,128)S(1)}, u32[]{:S(2)}, u32[]{:S(2)}) collective-permute-start(f32[16,16,128]{2,1,0:T(8,128)S(1)} %get-tuple-element.5.c0), channel_id=1, source_target_pairs={{0,12},{4,0},{8,4},{12,8},{1,13},{5,1},{9,5},{13,9},{2,14},{6,2},{... | collective-permute-start | bytes 393224 | tf_op jit(solution)/shard_map/ppermute | solution.py:251
  16.8 6.5 %collective-permute-start.7 = (f32[16,16,128]{2,1,0:T(8,128)S(1)}, f32[16,16,128]{2,1,0:T(8,128)S(1)}, u32[]{:S(2)}, u32[]{:S(2)}) collective-permute-start(f32[16,16,128]{2,1,0:T(8,128)S(1)} %get-tuple-element.5.c0), channel_id=1, source_target_pairs={{0,8},{4,12},{8,0},{12,4},{1,9},{5,13},{9,1},{13,5},{2,10},{6,14},... | collective-permute-start | bytes 393224 | tf_op jit(solution)/shard_map/ppermute | solution.py:251
  17.3 6.2 %collective-permute-start.6 = (f32[16,16,128]{2,1,0:T(8,128)S(1)}, f32[16,16,128]{2,1,0:T(8,128)S(1)}, u32[]{:S(2)}, u32[]{:S(2)}) collective-permute-start(f32[16,16,128]{2,1,0:T(8,128)S(1)} %get-tuple-element.5.c0), channel_id=1, source_target_pairs={{0,4},{4,8},{8,12},{12,0},{1,5},{5,9},{9,13},{13,1},{2,6},{6,10},{... | collective-permute-start | bytes 393224 | tf_op jit(solution)/shard_map/ppermute | solution.py:251
  17.9 4.7 %collective-permute-start.4 = (f32[16,8,128]{2,1,0:T(8,128)S(1)}, f32[16,8,128]{2,1,0:T(8,128)S(1)}, u32[]{:S(2)}, u32[]{:S(2)}) collective-permute-start(f32[16,8,128]{2,1,0:T(8,128)S(1)} %get-tuple-element.4.b0), channel_id=1, source_target_pairs={{0,2},{1,3},{2,0},{3,1},{4,6},{5,7},{6,4},{7,5},{8,10},{9,11},{10,... | collective-permute-start | bytes 196616 | tf_op jit(solution)/shard_map/ppermute | solution.py:251
  18.3 5.0 %collective-permute-start.3 = (f32[16,8,128]{2,1,0:T(8,128)S(1)}, f32[16,8,128]{2,1,0:T(8,128)S(1)}, u32[]{:S(2)}, u32[]{:S(2)}) collective-permute-start(f32[16,8,128]{2,1,0:T(8,128)S(1)} %get-tuple-element.4.b0), channel_id=1, source_target_pairs={{0,1},{1,2},{2,3},{3,0},{4,5},{5,6},{6,7},{7,4},{8,9},{9,10},{10,1... | collective-permute-start | bytes 196616 | tf_op jit(solution)/shard_map/ppermute | solution.py:251
  23.7 6.1 %collective-permute-start.9 = (f32[16,96,128]{2,1,0:T(8,128)S(1)}, f32[16,96,128]{2,1,0:T(8,128)S(1)}, u32[]{:S(2)}, u32[]{:S(2)}) collective-permute-start(f32[16,96,128]{2,1,0:T(8,128)S(1)} %shard_map.52.mine), channel_id=1, source_target_pairs={{0,16},{16,0},{1,17},{17,1},{2,18},{18,2},{3,19},{19,3},{4,20},{20... | collective-permute-start | bytes 2359304 | tf_op jit(solution)/shard_map/ppermute | solution.py:255
  49.6 4.9 %collective-permute-start.12 = (f32[16,128]{1,0:T(8,128)S(1)}, f32[16,128]{1,0:T(8,128)S(1)}, u32[]{:S(2)}, u32[]{:S(2)}) collective-permute-start(f32[16,128]{1,0:T(8,128)S(1)} %shard_map.54.w0), channel_id=1, source_target_pairs={{0,96},{32,0},{64,32},{96,64},{1,97},{33,1},{65,33},{97,65},{2,98}... | collective-permute-start | bytes 24584 | tf_op jit(solution)/shard_map/ppermute | solution.py:251
  50.3 4.3 %collective-permute-start.11 = (f32[16,128]{1,0:T(8,128)S(1)}, f32[16,128]{1,0:T(8,128)S(1)}, u32[]{:S(2)}, u32[]{:S(2)}) collective-permute-start(f32[16,128]{1,0:T(8,128)S(1)} %shard_map.54.w0), channel_id=1, source_target_pairs={{0,64},{32,96},{64,0},{96,32},{1,65},{33,97},{65,1},{97,33},{2,66}... | collective-permute-start | bytes 24584 | tf_op jit(solution)/shard_map/ppermute | solution.py:251
  51.1 3.7 %collective-permute-start.10 = (f32[16,128]{1,0:T(8,128)S(1)}, f32[16,128]{1,0:T(8,128)S(1)}, u32[]{:S(2)}, u32[]{:S(2)}) collective-permute-start(f32[16,128]{1,0:T(8,128)S(1)} %shard_map.54.w0), channel_id=1, source_target_pairs={{0,32},{32,64},{64,96},{96,0},{1,33},{33,65},{65,97},{97,1},{2,34}... | collective-permute-start | bytes 24584 | tf_op jit(solution)/shard_map/ppermute | solution.py:251
  66.3 4.4 %collective-permute-start.13 = (f32[16,40,128]{2,1,0:T(8,128)S(1)}, f32[16,40,128]{2,1,0:T(8,128)S(1)}, u32[]{:S(2)}, u32[]{:S(2)}) collective-permute-start(f32[16,40,128]{2,1,0:T(8,128)S(1)} %all_to_all.11.received), channel_id=1, source_target_pairs={{0,16},{16,0},{1,17},{17,1},{2,18},{18,2},{3,19},{19,3},{4,20},{20... | collective-permute-start | bytes 983048 | tf_op jit(solution)/shard_map/ppermute | solution.py:255

commit v8 on v7

--- a/solution.py
+++ b/solution.py
@@ -53,9 +53,9 @@
     for p in range(PAIRS):
         for side in range(2):
             lanes = slice(side * RANK, (side + 1) * RANK)
-            out[p, 0:B_OWN, lanes] = b[2 * p + side]
-            out[p, B_OWN : B_OWN + C_OWN, lanes] = c[2 * p + side]
-        out[p, B_OWN + C_OWN :, :] = jnp.zeros((8 - B_OWN - C_OWN, 2 * RANK), jnp.float32)
+            out[p * B_OWN : (p + 1) * B_OWN, lanes] = b[2 * p + side]
+            at = PAIRS * B_OWN + p * C_OWN
+            out[at : at + C_OWN, lanes] = c[2 * p + side]
 
 
 def in_order(pieces, first, rows):
@@ -78,8 +78,9 @@
     z, _, _, _ = place()
     parts = (m0, m1, m2, m3)
     for p in range(PAIRS):
-        b[p] = in_order([m[p, :B_OWN, :] for m in parts], z, B_OWN)
-        c[p] = in_order([m[p, B_OWN : B_OWN + C_OWN, :] for m in parts], z, C_OWN)
+        b[p] = in_order([m[p * B_OWN : (p + 1) * B_OWN, :] for m in parts], z, B_OWN)
+        at = PAIRS * B_OWN + p * C_OWN
+        c[p] = in_order([m[at : at + C_OWN, :] for m in parts], z, C_OWN)
 
 
 def along_xy_kernel(b0, b1, b2, b3, c0, c1, c2, c3, out):
@@ -113,7 +114,7 @@
         part_b = mine[p, pl.ds(pl.multiple_of(y * nb, nb), nb), :]
         part_c = mine[p, pl.ds(pl.multiple_of(JD // 2 + x * nc, nc), nc), :]
         for side in range(2):
-            d = side * PAIRS + p
+            d = 2 * p + side
             out[d, 8:16, :] = fold(swap_halves(part_c) if side else part_c)
             part = fold(swap_halves(part_b) if side else part_b)
             out[d, 16:24, :] = jnp.concatenate([part, jnp.zeros_like(part)], axis=0)
@@ -140,7 +141,7 @@
             )
             product = (product[:, :KD] + product[:, KD:]).reshape(ID, JD, KD) * weight
             total = jnp.sum(product.reshape(ID, JD // 8, 8, KD).sum(axis=1), axis=1)
-            out[side * PAIRS + p, :8, :] = fold(total + swap_halves(total))
+            out[2 * p + side, :8, :] = fold(total + swap_halves(total))
 
     def step(n, carry):
         for u in range(UNROLL):
@@ -152,9 +153,9 @@
 
 def total_kernel(received, out):
     for core in range(2):
-        total = received[core * PAIRS, :8, :]
+        total = received[core, :8, :]
         for s in range(1, PAIRS):
-            total = total + received[core * PAIRS + s, :8, :]
+            total = total + received[2 * s + core, :8, :]
         out[8 * core : 8 * core + 8, :] = total
 
 
@@ -258,7 +259,7 @@
 def on_device(tensor, factor_b, factor_c):
     packed = call(
         pack_kernel,
-        f32(PAIRS, 8, 2 * RANK),
+        f32(PAIRS * (B_OWN + C_OWN), 2 * RANK),
         [pltpu.with_memory_space_constraint(f, pltpu.HBM) for f in (factor_b[:, 0], factor_c[:, 0], tensor)],
         specs=[ANY, ANY, ANY],
         scratch=[
@@ -280,7 +281,7 @@
         vmem=28,
         cost=pl.CostEstimate(flops=8 * 2 * tensor.size * RANK, bytes_accessed=4 * tensor.size, transcendentals=0),
     )
-    received = lax.all_to_all(sent, ("core", "ja", "ka"), 0, 0)
+    received = lax.all_to_all(sent, ("ja", "ka", "core"), 0, 0)
     owned = call(total_kernel, f32(16, 2 * RANK), (received,))
     parts = around(owned, "z")
     inverse = call(

time: 72.1 us -> 71.9 us (level)
  no operation moved by 1% of the time
where the time goes in v8:
time: 71.9 us; the launch traced here: 71.7 us
  blocking collectives  25.5 us (35%)
  starting transfers between devices  22.3 us (31%)
  waiting for transfers between devices  12.1 us (17%)
  Pallas kernels  11 us (15%)
    ppermute x12, starting transfers between devices, around(): return [value] + [lax.ppermute(value, axis, perm) for perm in LINE]  15.2 us
    all_to_all x1, blocking collectives, on_device(): received = lax.all_to_all(sent, ('ja', 'ka', 'core'), 0, 0)  15 us
    all_to_all x1, blocking collectives, on_device(): received = lax.all_to_all(sent, ('ja', 'ka'), 0, 0)  10.5 us
    pallas_call x7, Pallas kernels, call(): pl.pallas_call(kernel, out_shape=out_shape, in_specs=[VMEM] * len(operand...  9.79 us
    ppermute x12, waiting for transfers between devices, around(): return [value] + [lax.ppermute(value, axis, perm) for perm in LINE]  8.98 us
    ppermute x2, starting transfers between devices, swap_cores(): return lax.ppermute(value, 'core', [(0, 1), (1, 0)])  7.05 us
    ppermute x2, waiting for transfers between devices, swap_cores(): return lax.ppermute(value, 'core', [(0, 1), (1, 0)])  3.17 us
  transfers between devices with their start and end apart: 14, of which 9 were waited for; matrix products, arithmetic and copies ran while one was open for 0% of the time, Pallas kernels for 4%

profile of v8, /device:TPU:1, one launch (start us, length us, event | category | flops | bytes accessed | tf_op | source)
XLA Modules:
  0.0 71.7 jit_solution(1142257911299675140)
XLA Ops:
  0.6 1.1 %shard_map.50.m0 = f32[96,128]{1,0:T(8,128)S(1)} custom-call(f32[32,2,64]{2,1,0:T(2,128)} %bitcast.3, f32[32,4,64]{2,1,0:T(4,128)} %bitcast.2, f32[32,16,64,128]{3,2,1,0:T(8,128)} %tensor.3), custom_call_target="tpu_custom_call" | custom-call | tf_op jit(solution)/shard_map/pallas_call | solution.py:28
  1.8 4.7 %collective-permute-start.2 = (f32[96,128]{1,0:T(8,128)S(1)}, f32[96,128]{1,0:T(8,128)S(1)}, u32[]{:S(2)}, u32[]{:S(2)}) collective-permute-start(f32[96,128]{1,0:T(8,128)S(1)} %shard_map.50.m0), channel_id=1, source_target_pairs={{0,96},{32,0},{64,32},{96,64},{1,97},{33,1},{65,33},{97,65},{2,98}... | collective-permute-start | bytes 147464 | tf_op jit(solution)/shard_map/ppermute | solution.py:252
  6.4 0.0 collective-permute-start.1
  6.4 0.7 collective-permute-start
  7.1 0.5 collective-permute-done.2.m3
  7.6 3.4 %collective-permute-done.1.m2 = f32[96,128]{1,0:T(8,128)S(1)} collective-permute-done((f32[96,128]{1,0:T(8,128)S(1)}, f32[96,128]{1,0:T(8,128)S(1)}, u32[]{:S(2)}, u32[]{:S(2)}) %collective-permute-start.1) | collective-permute-done | bytes 49184 | tf_op jit(solution)/shard_map/ppermute | solution.py:252
  11.0 0.1 collective-permute-done.m1
  11.2 2.8 %collective-permute-start.5 = (f32[16,8,128]{2,1,0:T(8,128)S(1)}, f32[16,8,128]{2,1,0:T(8,128)S(1)}, u32[]{:S(2)}, u32[]{:S(2)}) collective-permute-start(f32[16,8,128]{2,1,0:T(8,128)S(1)} %get-tuple-element.4.b0), channel_id=1, source_target_pairs={{0,3},{1,0},{2,1},{3,2},{4,7},{5,4},{6,5},{7,6},{8,11},{9,8},{10,9... | collective-permute-start | bytes 196616 | tf_op jit(solution)/shard_map/ppermute | solution.py:252
  14.0 2.5 %collective-permute-start.8 = (f32[16,16,128]{2,1,0:T(8,128)S(1)}, f32[16,16,128]{2,1,0:T(8,128)S(1)}, u32[]{:S(2)}, u32[]{:S(2)}) collective-permute-start(f32[16,16,128]{2,1,0:T(8,128)S(1)} %get-tuple-element.5.c0), channel_id=1, source_target_pairs={{0,12},{4,0},{8,4},{12,8},{1,13},{5,1},{9,5},{13,9},{2,14},{6,2},{... | collective-permute-start | bytes 393224 | tf_op jit(solution)/shard_map/ppermute | solution.py:252
  16.4 0.5 collective-permute-start.7
  17.0 0.6 collective-permute-start.6
  17.6 0.3 collective-permute-start.4
  17.9 0.7 collective-permute-start.3
  18.6 3.6 %collective-permute-done.4.b2 = f32[16,8,128]{2,1,0:T(8,128)S(1)} collective-permute-done((f32[16,8,128]{2,1,0:T(8,128)S(1)}, f32[16,8,128]{2,1,0:T(8,128)S(1)}, u32[]{:S(2)}, u32[]{:S(2)}) %collective-permute-start.4) | collective-permute-done | bytes 65568 | tf_op jit(solution)/shard_map/ppermute | solution.py:252
  22.3 0.6 collective-permute-done.3.b1
  22.9 0.3 collective-permute-done.6.c1
  23.2 0.2 shard_map.52.mine
  23.3 4.2 %collective-permute-start.9 = (f32[16,96,128]{2,1,0:T(8,128)S(1)}, f32[16,96,128]{2,1,0:T(8,128)S(1)}, u32[]{:S(2)}, u32[]{:S(2)}) collective-permute-start(f32[16,96,128]{2,1,0:T(8,128)S(1)} %shard_map.52.mine), channel_id=1, source_target_pairs={{0,16},{16,0},{1,17},{17,1},{2,18},{18,2},{3,19},{19,3},{4,20},{20... | collective-permute-start | bytes 2359304 | tf_op jit(solution)/shard_map/ppermute | solution.py:256
  27.5 1.9 %collective-permute-done.9.other = f32[16,96,128]{2,1,0:T(8,128)S(1)} collective-permute-done((f32[16,96,128]{2,1,0:T(8,128)S(1)}, f32[16,96,128]{2,1,0:T(8,128)S(1)}, u32[]{:S(2)}, u32[]{:S(2)}) %collective-permute-start.9) | collective-permute-done | bytes 786464 | tf_op jit(solution)/shard_map/ppermute | solution.py:256
  29.4 5.1 %shard_map.53 = f32[32,24,128]{2,1,0:T(8,128)S(1)} custom-call(f32[32,16,64,128]{3,2,1,0:T(8,128)S(1)} %copy-done, f32[16,96,128]{2,1,0:T(8,128)S(1)} %shard_map.52.mine, f32[16,96,128]{2,1,0:T(8,128)S(1)} %collective-permute-done.9.other), custom_call_target="tpu_custom_call" | custom-call | flops 4294967296 | bytes 16777216 | tf_op jit(solution)/shard_map/pallas_call | solution.py:28
  34.6 15.0 %all_to_all.10.received = f32[32,24,128]{2,1,0:T(8,128)S(1)} all-to-all(f32[32,24,128]{2,1,0:T(8,128)S(1)} %shard_map.53), channel_id=1, replica_groups=mesh['z'=4,'core'=2,'ja'=4,'ka'=4] {'ja','ka','core'}, dimensions={0} | all-to-all | bytes 786432 | tf_op jit(solution)/shard_map/all_to_all | solution.py:284
  49.6 0.6 collective-permute-start.12
  50.2 1.0 %collective-permute-start.11 = (f32[16,128]{1,0:T(8,128)S(1)}, f32[16,128]{1,0:T(8,128)S(1)}, u32[]{:S(2)}, u32[]{:S(2)}) collective-permute-start(f32[16,128]{1,0:T(8,128)S(1)} %shard_map.54.w0), channel_id=1, source_target_pairs={{0,64},{32,96},{64,0},{96,32},{1,65},{33,97},{65,1},{97,33},{2,66}... | collective-permute-start | bytes 24584 | tf_op jit(solution)/shard_map/ppermute | solution.py:252
  51.3 0.8 %collective-permute-start.10 = (f32[16,128]{1,0:T(8,128)S(1)}, f32[16,128]{1,0:T(8,128)S(1)}, u32[]{:S(2)}, u32[]{:S(2)}) collective-permute-start(f32[16,128]{1,0:T(8,128)S(1)} %shard_map.54.w0), channel_id=1, source_target_pairs={{0,32},{32,64},{64,96},{96,0},{1,33},{33,65},{65,97},{97,1},{2,34}... | collective-permute-start | bytes 24584 | tf_op jit(solution)/shard_map/ppermute | solution.py:252
  52.0 2.7 %shard_map.55.inverse = f32[128,128]{1,0:T(8,128)S(1)} custom-call(f32[32,24,128]{2,1,0:T(8,128)S(1)} %all_to_all.10.received), custom_call_target="tpu_custom_call" | custom-call | flops 1048576 | bytes 10485760 | tf_op jit(solution)/shard_map/pallas_call | solution.py:28
  54.7 0.0 collective-permute-done.12.w3
  54.7 0.4 collective-permute-done.10.w1
  55.2 0.7 shard_map.56
  55.8 10.5 %all_to_all.11.received = f32[16,40,128]{2,1,0:T(8,128)S(1)} all-to-all(f32[16,40,128]{2,1,0:T(8,128)S(1)} %shard_map.56), channel_id=1, replica_groups=mesh['z'=4,'core'=2,'ja'=4,'ka'=4] {'ja','ka'}, dimensions={0} | all-to-all | bytes 655360 | tf_op jit(solution)/shard_map/all_to_all | solution.py:299
  66.4 2.9 %collective-permute-start.13 = (f32[16,40,128]{2,1,0:T(8,128)S(1)}, f32[16,40,128]{2,1,0:T(8,128)S(1)}, u32[]{:S(2)}, u32[]{:S(2)}) collective-permute-start(f32[16,40,128]{2,1,0:T(8,128)S(1)} %all_to_all.11.received), channel_id=1, source_target_pairs={{0,16},{16,0},{1,17},{17,1},{2,18},{18,2},{3,19},{19,3},{4,20},{20... | collective-permute-start | bytes 983048 | tf_op jit(solution)/shard_map/ppermute | solution.py:256
  69.2 1.3 %collective-permute-done.13.swapped = f32[16,40,128]{2,1,0:T(8,128)S(1)} collective-permute-done((f32[16,40,128]{2,1,0:T(8,128)S(1)}, f32[16,40,128]{2,1,0:T(8,128)S(1)}, u32[]{:S(2)}, u32[]{:S(2)}) %collective-permute-start.13) | collective-permute-done | bytes 327712 | tf_op jit(solution)/shard_map/ppermute | solution.py:256
  70.5 1.2 %shard_map.57 = (f32[32,1,1,64]{3,2,1,0:T(1,128)}, f32[32,64,64]{2,1,0:T(8,128)}) custom-call(f32[16,40,128]{2,1,0:T(8,128)S(1)} %all_to_all.11.received, f32[16,40,128]{2,1,0:T(8,128)S(1)} %collective-permute-done.13.swapped), custom_call_target="tpu_custom_call" | custom-call | tf_op jit(solution)/shard_map/pallas_call | solution.py:302
  (8 shorter events, 0.1 us)
Async XLA Ops:
  0.6 28.8 %copy-start = (f32[32,16,64,128]{3,2,1,0:T(8,128)S(1)}, f32[32,16,64,128]{3,2,1,0:T(8,128)}, u32[]{:S(2)}) copy-start(f32[32,16,64,128]{3,2,1,0:T(8,128)} %tensor.3) | copy-start | bytes 50331652
  1.8 5.8 %collective-permute-start.2 = (f32[96,128]{1,0:T(8,128)S(1)}, f32[96,128]{1,0:T(8,128)S(1)}, u32[]{:S(2)}, u32[]{:S(2)}) collective-permute-start(f32[96,128]{1,0:T(8,128)S(1)} %shard_map.50.m0), channel_id=1, source_target_pairs={{0,96},{32,0},{64,32},{96,64},{1,97},{33,1},{65,33},{97,65},{2,98}... | collective-permute-start | bytes 147464 | tf_op jit(solution)/shard_map/ppermute | solution.py:252
  6.4 4.5 %collective-permute-start.1 = (f32[96,128]{1,0:T(8,128)S(1)}, f32[96,128]{1,0:T(8,128)S(1)}, u32[]{:S(2)}, u32[]{:S(2)}) collective-permute-start(f32[96,128]{1,0:T(8,128)S(1)} %shard_map.50.m0), channel_id=1, source_target_pairs={{0,64},{32,96},{64,0},{96,32},{1,65},{33,97},{65,1},{97,33},{2,66}... | collective-permute-start | bytes 147464 | tf_op jit(solution)/shard_map/ppermute | solution.py:252
  6.4 4.7 %collective-permute-start = (f32[96,128]{1,0:T(8,128)S(1)}, f32[96,128]{1,0:T(8,128)S(1)}, u32[]{:S(2)}, u32[]{:S(2)}) collective-permute-start(f32[96,128]{1,0:T(8,128)S(1)} %shard_map.50.m0), channel_id=1, source_target_pairs={{0,32},{32,64},{64,96},{96,0},{1,33},{33,65},{65,97},{97,1},{2,34}... | collective-permute-start | bytes 147464 | tf_op jit(solution)/shard_map/ppermute | solution.py:252
  11.2 6.8 %collective-permute-start.5 = (f32[16,8,128]{2,1,0:T(8,128)S(1)}, f32[16,8,128]{2,1,0:T(8,128)S(1)}, u32[]{:S(2)}, u32[]{:S(2)}) collective-permute-start(f32[16,8,128]{2,1,0:T(8,128)S(1)} %get-tuple-element.4.b0), channel_id=1, source_target_pairs={{0,3},{1,0},{2,1},{3,2},{4,7},{5,4},{6,5},{7,6},{8,11},{9,8},{10,9... | collective-permute-start | bytes 196616 | tf_op jit(solution)/shard_map/ppermute | solution.py:252
  14.0 8.9 %collective-permute-start.8 = (f32[16,16,128]{2,1,0:T(8,128)S(1)}, f32[16,16,128]{2,1,0:T(8,128)S(1)}, u32[]{:S(2)}, u32[]{:S(2)}) collective-permute-start(f32[16,16,128]{2,1,0:T(8,128)S(1)} %get-tuple-element.5.c0), channel_id=1, source_target_pairs={{0,12},{4,0},{8,4},{12,8},{1,13},{5,1},{9,5},{13,9},{2,14},{6,2},{... | collective-permute-start | bytes 393224 | tf_op jit(solution)/shard_map/ppermute | solution.py:252
  16.4 6.5 %collective-permute-start.7 = (f32[16,16,128]{2,1,0:T(8,128)S(1)}, f32[16,16,128]{2,1,0:T(8,128)S(1)}, u32[]{:S(2)}, u32[]{:S(2)}) collective-permute-start(f32[16,16,128]{2,1,0:T(8,128)S(1)} %get-tuple-element.5.c0), channel_id=1, source_target_pairs={{0,8},{4,12},{8,0},{12,4},{1,9},{5,13},{9,1},{13,5},{2,10},{6,14},... | collective-permute-start | bytes 393224 | tf_op jit(solution)/shard_map/ppermute | solution.py:252
  17.0 6.2 %collective-permute-start.6 = (f32[16,16,128]{2,1,0:T(8,128)S(1)}, f32[16,16,128]{2,1,0:T(8,128)S(1)}, u32[]{:S(2)}, u32[]{:S(2)}) collective-permute-start(f32[16,16,128]{2,1,0:T(8,128)S(1)} %get-tuple-element.5.c0), channel_id=1, source_target_pairs={{0,4},{4,8},{8,12},{12,0},{1,5},{5,9},{9,13},{13,1},{2,6},{6,10},{... | collective-permute-start | bytes 393224 | tf_op jit(solution)/shard_map/ppermute | solution.py:252
  17.6 4.7 %collective-permute-start.4 = (f32[16,8,128]{2,1,0:T(8,128)S(1)}, f32[16,8,128]{2,1,0:T(8,128)S(1)}, u32[]{:S(2)}, u32[]{:S(2)}) collective-permute-start(f32[16,8,128]{2,1,0:T(8,128)S(1)} %get-tuple-element.4.b0), channel_id=1, source_target_pairs={{0,2},{1,3},{2,0},{3,1},{4,6},{5,7},{6,4},{7,5},{8,10},{9,11},{10,... | collective-permute-start | bytes 196616 | tf_op jit(solution)/shard_map/ppermute | solution.py:252
  17.9 5.0 %collective-permute-start.3 = (f32[16,8,128]{2,1,0:T(8,128)S(1)}, f32[16,8,128]{2,1,0:T(8,128)S(1)}, u32[]{:S(2)}, u32[]{:S(2)}) collective-permute-start(f32[16,8,128]{2,1,0:T(8,128)S(1)} %get-tuple-element.4.b0), channel_id=1, source_target_pairs={{0,1},{1,2},{2,3},{3,0},{4,5},{5,6},{6,7},{7,4},{8,9},{9,10},{10,1... | collective-permute-start | bytes 196616 | tf_op jit(solution)/shard_map/ppermute | solution.py:252
  23.3 6.1 %collective-permute-start.9 = (f32[16,96,128]{2,1,0:T(8,128)S(1)}, f32[16,96,128]{2,1,0:T(8,128)S(1)}, u32[]{:S(2)}, u32[]{:S(2)}) collective-permute-start(f32[16,96,128]{2,1,0:T(8,128)S(1)} %shard_map.52.mine), channel_id=1, source_target_pairs={{0,16},{16,0},{1,17},{17,1},{2,18},{18,2},{3,19},{19,3},{4,20},{20... | collective-permute-start | bytes 2359304 | tf_op jit(solution)/shard_map/ppermute | solution.py:256
  49.6 5.1 %collective-permute-start.12 = (f32[16,128]{1,0:T(8,128)S(1)}, f32[16,128]{1,0:T(8,128)S(1)}, u32[]{:S(2)}, u32[]{:S(2)}) collective-permute-start(f32[16,128]{1,0:T(8,128)S(1)} %shard_map.54.w0), channel_id=1, source_target_pairs={{0,96},{32,0},{64,32},{96,64},{1,97},{33,1},{65,33},{97,65},{2,98}... | collective-permute-start | bytes 24584 | tf_op jit(solution)/shard_map/ppermute | solution.py:252
  50.2 4.5 %collective-permute-start.11 = (f32[16,128]{1,0:T(8,128)S(1)}, f32[16,128]{1,0:T(8,128)S(1)}, u32[]{:S(2)}, u32[]{:S(2)}) collective-permute-start(f32[16,128]{1,0:T(8,128)S(1)} %shard_map.54.w0), channel_id=1, source_target_pairs={{0,64},{32,96},{64,0},{96,32},{1,65},{33,97},{65,1},{97,33},{2,66}... | collective-permute-start | bytes 24584 | tf_op jit(solution)/shard_map/ppermute | solution.py:252
  51.3 3.9 %collective-permute-start.10 = (f32[16,128]{1,0:T(8,128)S(1)}, f32[16,128]{1,0:T(8,128)S(1)}, u32[]{:S(2)}, u32[]{:S(2)}) collective-permute-start(f32[16,128]{1,0:T(8,128)S(1)} %shard_map.54.w0), channel_id=1, source_target_pairs={{0,32},{32,64},{64,96},{96,0},{1,33},{33,65},{65,97},{97,1},{2,34}... | collective-permute-start | bytes 24584 | tf_op jit(solution)/shard_map/ppermute | solution.py:252
  66.4 4.1 %collective-permute-start.13 = (f32[16,40,128]{2,1,0:T(8,128)S(1)}, f32[16,40,128]{2,1,0:T(8,128)S(1)}, u32[]{:S(2)}, u32[]{:S(2)}) collective-permute-start(f32[16,40,128]{2,1,0:T(8,128)S(1)} %all_to_all.11.received), channel_id=1, source_target_pairs={{0,16},{16,0},{1,17},{17,1},{2,18},{18,2},{3,19},{19,3},{4,20},{20... | collective-permute-start | bytes 983048 | tf_op jit(solution)/shard_map/ppermute | solution.py:256

commit v9 on v8

--- a/solution.py
+++ b/solution.py
@@ -220,10 +220,11 @@
     gram = fold(rows_gram(solved) * (1.0 / I_ALL))
     own = rows[pl.ds(pl.multiple_of(z * 16, 16), 16), :]
     for q in range(ID):
-        out[q, : RANK // 2, :] = gram
+        d = q % N_KA * N_JA + q // N_KA
+        out[d, : RANK // 2, :] = gram
         for core in range(2):
             row, at = core * 8 + q % 8, RANK // 2 + core * 4
-            out[q, at : at + 4, :] = jnp.broadcast_to(own[row : row + 1], (4, 2 * RANK))
+            out[d, at : at + 4, :] = jnp.broadcast_to(own[row : row + 1], (4, 2 * RANK))
 
 
 def unpack_kernel(received, swapped, rows, gram):
@@ -234,11 +235,12 @@
 
     def unpack(here):
         for n in range(PAIRS // STEPS):
+            at = n % N_KA * N_JA + first // N_KA + n // N_KA
             for side in range(2):
                 source = received if side == here else swapped
-                gram[2 * n + side, :half] = source[first + n, :half, :RANK]
-                gram[2 * n + side, half:] = source[first + n, :half, RANK:]
-                row = source[first + n, half + 4 * here : half + 4 * here + 1, :]
+                gram[2 * n + side, :half] = source[at, :half, :RANK]
+                gram[2 * n + side, half:] = source[at, :half, RANK:]
+                row = source[at, half + 4 * here : half + 4 * here + 1, :]
                 rows[2 * n + side, 0] = jnp.where(upper, row[:, RANK:], row[:, :RANK])
 
     for here in range(2):
@@ -296,7 +298,7 @@
         (*parts, inverse),
         scratch=[pltpu.VMEM((I_ALL // 2, 2 * RANK), jnp.float32)] * 2,
     )
-    received = lax.all_to_all(sent, ("ja", "ka"), 0, 0)
+    received = lax.all_to_all(sent, ("ka", "ja"), 0, 0)
     swapped = swap_cores(received)
     n = FIELDS // STEPS
     return pl.pallas_call(

time: 71.9 us -> 72.1 us (level)
  no operation moved by 1% of the time
where the time goes in v9:
time: 72.1 us; the launch traced here: 71.9 us
  blocking collectives  25.8 us (36%)
  starting transfers between devices  22.3 us (31%)
  waiting for transfers between devices  12.1 us (17%)
  Pallas kernels  11 us (15%)
    ppermute x12, starting transfers between devices, around(): return [value] + [lax.ppermute(value, axis, perm) for perm in LINE]  15.2 us
    all_to_all x1, blocking collectives, on_device(): received = lax.all_to_all(sent, ('ja', 'ka', 'core'), 0, 0)  15 us
    all_to_all x1, blocking collectives, on_device(): received = lax.all_to_all(sent, ('ka', 'ja'), 0, 0)  10.7 us
    pallas_call x7, Pallas kernels, call(): pl.pallas_call(kernel, out_shape=out_shape, in_specs=[VMEM] * len(operand...  9.79 us
    ppermute x12, waiting for transfers between devices, around(): return [value] + [lax.ppermute(value, axis, perm) for perm in LINE]  8.98 us
    ppermute x2, starting transfers between devices, swap_cores(): return lax.ppermute(value, 'core', [(0, 1), (1, 0)])  7.05 us
    ppermute x2, waiting for transfers between devices, swap_cores(): return lax.ppermute(value, 'core', [(0, 1), (1, 0)])  3.17 us
  transfers between devices with their start and end apart: 14, of which 9 were waited for; matrix products, arithmetic and copies ran while one was open for 0% of the time, Pallas kernels for 4%

profile of v9, /device:TPU:1, one launch (start us, length us, event | category | flops | bytes accessed | tf_op | source)
XLA Modules:
  0.0 71.9 jit_solution(6594218800774336080)
XLA Ops:
  0.6 1.1 %shard_map.50.m0 = f32[96,128]{1,0:T(8,128)S(1)} custom-call(f32[32,2,64]{2,1,0:T(2,128)} %bitcast.3, f32[32,4,64]{2,1,0:T(4,128)} %bitcast.2, f32[32,16,64,128]{3,2,1,0:T(8,128)} %tensor.3), custom_call_target="tpu_custom_call" | custom-call | tf_op jit(solution)/shard_map/pallas_call | solution.py:28
  1.8 4.7 %collective-permute-start.2 = (f32[96,128]{1,0:T(8,128)S(1)}, f32[96,128]{1,0:T(8,128)S(1)}, u32[]{:S(2)}, u32[]{:S(2)}) collective-permute-start(f32[96,128]{1,0:T(8,128)S(1)} %shard_map.50.m0), channel_id=1, source_target_pairs={{0,96},{32,0},{64,32},{96,64},{1,97},{33,1},{65,33},{97,65},{2,98}... | collective-permute-start | bytes 147464 | tf_op jit(solution)/shard_map/ppermute | solution.py:254
  6.4 0.0 collective-permute-start.1
  6.4 0.7 collective-permute-start
  7.1 0.5 collective-permute-done.2.m3
  7.6 3.4 %collective-permute-done.1.m2 = f32[96,128]{1,0:T(8,128)S(1)} collective-permute-done((f32[96,128]{1,0:T(8,128)S(1)}, f32[96,128]{1,0:T(8,128)S(1)}, u32[]{:S(2)}, u32[]{:S(2)}) %collective-permute-start.1) | collective-permute-done | bytes 49184 | tf_op jit(solution)/shard_map/ppermute | solution.py:254
  11.0 0.1 collective-permute-done.m1
  11.2 2.8 %collective-permute-start.5 = (f32[16,8,128]{2,1,0:T(8,128)S(1)}, f32[16,8,128]{2,1,0:T(8,128)S(1)}, u32[]{:S(2)}, u32[]{:S(2)}) collective-permute-start(f32[16,8,128]{2,1,0:T(8,128)S(1)} %get-tuple-element.4.b0), channel_id=1, source_target_pairs={{0,3},{1,0},{2,1},{3,2},{4,7},{5,4},{6,5},{7,6},{8,11},{9,8},{10,9... | collective-permute-start | bytes 196616 | tf_op jit(solution)/shard_map/ppermute | solution.py:254
  14.0 2.5 %collective-permute-start.8 = (f32[16,16,128]{2,1,0:T(8,128)S(1)}, f32[16,16,128]{2,1,0:T(8,128)S(1)}, u32[]{:S(2)}, u32[]{:S(2)}) collective-permute-start(f32[16,16,128]{2,1,0:T(8,128)S(1)} %get-tuple-element.5.c0), channel_id=1, source_target_pairs={{0,12},{4,0},{8,4},{12,8},{1,13},{5,1},{9,5},{13,9},{2,14},{6,2},{... | collective-permute-start | bytes 393224 | tf_op jit(solution)/shard_map/ppermute | solution.py:254
  16.4 0.5 collective-permute-start.7
  17.0 0.6 collective-permute-start.6
  17.6 0.3 collective-permute-start.4
  17.9 0.7 collective-permute-start.3
  18.6 3.6 %collective-permute-done.4.b2 = f32[16,8,128]{2,1,0:T(8,128)S(1)} collective-permute-done((f32[16,8,128]{2,1,0:T(8,128)S(1)}, f32[16,8,128]{2,1,0:T(8,128)S(1)}, u32[]{:S(2)}, u32[]{:S(2)}) %collective-permute-start.4) | collective-permute-done | bytes 65568 | tf_op jit(solution)/shard_map/ppermute | solution.py:254
  22.3 0.6 collective-permute-done.3.b1
  22.9 0.3 collective-permute-done.6.c1
  23.2 0.2 shard_map.52.mine
  23.3 4.2 %collective-permute-start.9 = (f32[16,96,128]{2,1,0:T(8,128)S(1)}, f32[16,96,128]{2,1,0:T(8,128)S(1)}, u32[]{:S(2)}, u32[]{:S(2)}) collective-permute-start(f32[16,96,128]{2,1,0:T(8,128)S(1)} %shard_map.52.mine), channel_id=1, source_target_pairs={{0,16},{16,0},{1,17},{17,1},{2,18},{18,2},{3,19},{19,3},{4,20},{20... | collective-permute-start | bytes 2359304 | tf_op jit(solution)/shard_map/ppermute | solution.py:258
  27.5 1.9 %collective-permute-done.9.other = f32[16,96,128]{2,1,0:T(8,128)S(1)} collective-permute-done((f32[16,96,128]{2,1,0:T(8,128)S(1)}, f32[16,96,128]{2,1,0:T(8,128)S(1)}, u32[]{:S(2)}, u32[]{:S(2)}) %collective-permute-start.9) | collective-permute-done | bytes 786464 | tf_op jit(solution)/shard_map/ppermute | solution.py:258
  29.4 5.1 %shard_map.53 = f32[32,24,128]{2,1,0:T(8,128)S(1)} custom-call(f32[32,16,64,128]{3,2,1,0:T(8,128)S(1)} %copy-done, f32[16,96,128]{2,1,0:T(8,128)S(1)} %shard_map.52.mine, f32[16,96,128]{2,1,0:T(8,128)S(1)} %collective-permute-done.9.other), custom_call_target="tpu_custom_call" | custom-call | flops 4294967296 | bytes 16777216 | tf_op jit(solution)/shard_map/pallas_call | solution.py:28
  34.6 15.0 %all_to_all.10.received = f32[32,24,128]{2,1,0:T(8,128)S(1)} all-to-all(f32[32,24,128]{2,1,0:T(8,128)S(1)} %shard_map.53), channel_id=1, replica_groups=mesh['z'=4,'core'=2,'ja'=4,'ka'=4] {'ja','ka','core'}, dimensions={0} | all-to-all | bytes 786432 | tf_op jit(solution)/shard_map/all_to_all | solution.py:286
  49.6 0.6 collective-permute-start.12
  50.2 1.0 %collective-permute-start.11 = (f32[16,128]{1,0:T(8,128)S(1)}, f32[16,128]{1,0:T(8,128)S(1)}, u32[]{:S(2)}, u32[]{:S(2)}) collective-permute-start(f32[16,128]{1,0:T(8,128)S(1)} %shard_map.54.w0), channel_id=1, source_target_pairs={{0,64},{32,96},{64,0},{96,32},{1,65},{33,97},{65,1},{97,33},{2,66}... | collective-permute-start | bytes 24584 | tf_op jit(solution)/shard_map/ppermute | solution.py:254
  51.3 0.8 %collective-permute-start.10 = (f32[16,128]{1,0:T(8,128)S(1)}, f32[16,128]{1,0:T(8,128)S(1)}, u32[]{:S(2)}, u32[]{:S(2)}) collective-permute-start(f32[16,128]{1,0:T(8,128)S(1)} %shard_map.54.w0), channel_id=1, source_target_pairs={{0,32},{32,64},{64,96},{96,0},{1,33},{33,65},{65,97},{97,1},{2,34}... | collective-permute-start | bytes 24584 | tf_op jit(solution)/shard_map/ppermute | solution.py:254
  52.0 2.7 %shard_map.55.inverse = f32[128,128]{1,0:T(8,128)S(1)} custom-call(f32[32,24,128]{2,1,0:T(8,128)S(1)} %all_to_all.10.received), custom_call_target="tpu_custom_call" | custom-call | flops 1048576 | bytes 10485760 | tf_op jit(solution)/shard_map/pallas_call | solution.py:28
  54.7 0.0 collective-permute-done.12.w3
  54.7 0.4 collective-permute-done.10.w1
  55.2 0.7 shard_map.56
  55.8 10.7 %all_to_all.11.received = f32[16,40,128]{2,1,0:T(8,128)S(1)} all-to-all(f32[16,40,128]{2,1,0:T(8,128)S(1)} %shard_map.56), channel_id=1, replica_groups=mesh['z'=4,'core'=2,'ja'=4,'ka'=4] {'ka','ja'}, dimensions={0} | all-to-all | bytes 655360 | tf_op jit(solution)/shard_map/all_to_all | solution.py:301
  66.6 2.9 %collective-permute-start.13 = (f32[16,40,128]{2,1,0:T(8,128)S(1)}, f32[16,40,128]{2,1,0:T(8,128)S(1)}, u32[]{:S(2)}, u32[]{:S(2)}) collective-permute-start(f32[16,40,128]{2,1,0:T(8,128)S(1)} %all_to_all.11.received), channel_id=1, source_target_pairs={{0,16},{16,0},{1,17},{17,1},{2,18},{18,2},{3,19},{19,3},{4,20},{20... | collective-permute-start | bytes 983048 | tf_op jit(solution)/shard_map/ppermute | solution.py:258
  69.4 1.3 %collective-permute-done.13.swapped = f32[16,40,128]{2,1,0:T(8,128)S(1)} collective-permute-done((f32[16,40,128]{2,1,0:T(8,128)S(1)}, f32[16,40,128]{2,1,0:T(8,128)S(1)}, u32[]{:S(2)}, u32[]{:S(2)}) %collective-permute-start.13) | collective-permute-done | bytes 327712 | tf_op jit(solution)/shard_map/ppermute | solution.py:258
  70.7 1.2 %shard_map.57 = (f32[32,1,1,64]{3,2,1,0:T(1,128)}, f32[32,64,64]{2,1,0:T(8,128)}) custom-call(f32[16,40,128]{2,1,0:T(8,128)S(1)} %all_to_all.11.received, f32[16,40,128]{2,1,0:T(8,128)S(1)} %collective-permute-done.13.swapped), custom_call_target="tpu_custom_call" | custom-call | tf_op jit(solution)/shard_map/pallas_call | solution.py:304
  (8 shorter events, 0.1 us)
Async XLA Ops:
  0.6 28.8 %copy-start = (f32[32,16,64,128]{3,2,1,0:T(8,128)S(1)}, f32[32,16,64,128]{3,2,1,0:T(8,128)}, u32[]{:S(2)}) copy-start(f32[32,16,64,128]{3,2,1,0:T(8,128)} %tensor.3) | copy-start | bytes 50331652
  1.8 5.8 %collective-permute-start.2 = (f32[96,128]{1,0:T(8,128)S(1)}, f32[96,128]{1,0:T(8,128)S(1)}, u32[]{:S(2)}, u32[]{:S(2)}) collective-permute-start(f32[96,128]{1,0:T(8,128)S(1)} %shard_map.50.m0), channel_id=1, source_target_pairs={{0,96},{32,0},{64,32},{96,64},{1,97},{33,1},{65,33},{97,65},{2,98}... | collective-permute-start | bytes 147464 | tf_op jit(solution)/shard_map/ppermute | solution.py:254
  6.4 4.5 %collective-permute-start.1 = (f32[96,128]{1,0:T(8,128)S(1)}, f32[96,128]{1,0:T(8,128)S(1)}, u32[]{:S(2)}, u32[]{:S(2)}) collective-permute-start(f32[96,128]{1,0:T(8,128)S(1)} %shard_map.50.m0), channel_id=1, source_target_pairs={{0,64},{32,96},{64,0},{96,32},{1,65},{33,97},{65,1},{97,33},{2,66}... | collective-permute-start | bytes 147464 | tf_op jit(solution)/shard_map/ppermute | solution.py:254
  6.4 4.7 %collective-permute-start = (f32[96,128]{1,0:T(8,128)S(1)}, f32[96,128]{1,0:T(8,128)S(1)}, u32[]{:S(2)}, u32[]{:S(2)}) collective-permute-start(f32[96,128]{1,0:T(8,128)S(1)} %shard_map.50.m0), channel_id=1, source_target_pairs={{0,32},{32,64},{64,96},{96,0},{1,33},{33,65},{65,97},{97,1},{2,34}... | collective-permute-start | bytes 147464 | tf_op jit(solution)/shard_map/ppermute | solution.py:254
  11.2 6.8 %collective-permute-start.5 = (f32[16,8,128]{2,1,0:T(8,128)S(1)}, f32[16,8,128]{2,1,0:T(8,128)S(1)}, u32[]{:S(2)}, u32[]{:S(2)}) collective-permute-start(f32[16,8,128]{2,1,0:T(8,128)S(1)} %get-tuple-element.4.b0), channel_id=1, source_target_pairs={{0,3},{1,0},{2,1},{3,2},{4,7},{5,4},{6,5},{7,6},{8,11},{9,8},{10,9... | collective-permute-start | bytes 196616 | tf_op jit(solution)/shard_map/ppermute | solution.py:254
  14.0 8.9 %collective-permute-start.8 = (f32[16,16,128]{2,1,0:T(8,128)S(1)}, f32[16,16,128]{2,1,0:T(8,128)S(1)}, u32[]{:S(2)}, u32[]{:S(2)}) collective-permute-start(f32[16,16,128]{2,1,0:T(8,128)S(1)} %get-tuple-element.5.c0), channel_id=1, source_target_pairs={{0,12},{4,0},{8,4},{12,8},{1,13},{5,1},{9,5},{13,9},{2,14},{6,2},{... | collective-permute-start | bytes 393224 | tf_op jit(solution)/shard_map/ppermute | solution.py:254
  16.4 6.5 %collective-permute-start.7 = (f32[16,16,128]{2,1,0:T(8,128)S(1)}, f32[16,16,128]{2,1,0:T(8,128)S(1)}, u32[]{:S(2)}, u32[]{:S(2)}) collective-permute-start(f32[16,16,128]{2,1,0:T(8,128)S(1)} %get-tuple-element.5.c0), channel_id=1, source_target_pairs={{0,8},{4,12},{8,0},{12,4},{1,9},{5,13},{9,1},{13,5},{2,10},{6,14},... | collective-permute-start | bytes 393224 | tf_op jit(solution)/shard_map/ppermute | solution.py:254
  17.0 6.2 %collective-permute-start.6 = (f32[16,16,128]{2,1,0:T(8,128)S(1)}, f32[16,16,128]{2,1,0:T(8,128)S(1)}, u32[]{:S(2)}, u32[]{:S(2)}) collective-permute-start(f32[16,16,128]{2,1,0:T(8,128)S(1)} %get-tuple-element.5.c0), channel_id=1, source_target_pairs={{0,4},{4,8},{8,12},{12,0},{1,5},{5,9},{9,13},{13,1},{2,6},{6,10},{... | collective-permute-start | bytes 393224 | tf_op jit(solution)/shard_map/ppermute | solution.py:254
  17.6 4.7 %collective-permute-start.4 = (f32[16,8,128]{2,1,0:T(8,128)S(1)}, f32[16,8,128]{2,1,0:T(8,128)S(1)}, u32[]{:S(2)}, u32[]{:S(2)}) collective-permute-start(f32[16,8,128]{2,1,0:T(8,128)S(1)} %get-tuple-element.4.b0), channel_id=1, source_target_pairs={{0,2},{1,3},{2,0},{3,1},{4,6},{5,7},{6,4},{7,5},{8,10},{9,11},{10,... | collective-permute-start | bytes 196616 | tf_op jit(solution)/shard_map/ppermute | solution.py:254
  17.9 5.0 %collective-permute-start.3 = (f32[16,8,128]{2,1,0:T(8,128)S(1)}, f32[16,8,128]{2,1,0:T(8,128)S(1)}, u32[]{:S(2)}, u32[]{:S(2)}) collective-permute-start(f32[16,8,128]{2,1,0:T(8,128)S(1)} %get-tuple-element.4.b0), channel_id=1, source_target_pairs={{0,1},{1,2},{2,3},{3,0},{4,5},{5,6},{6,7},{7,4},{8,9},{9,10},{10,1... | collective-permute-start | bytes 196616 | tf_op jit(solution)/shard_map/ppermute | solution.py:254
  23.3 6.1 %collective-permute-start.9 = (f32[16,96,128]{2,1,0:T(8,128)S(1)}, f32[16,96,128]{2,1,0:T(8,128)S(1)}, u32[]{:S(2)}, u32[]{:S(2)}) collective-permute-start(f32[16,96,128]{2,1,0:T(8,128)S(1)} %shard_map.52.mine), channel_id=1, source_target_pairs={{0,16},{16,0},{1,17},{17,1},{2,18},{18,2},{3,19},{19,3},{4,20},{20... | collective-permute-start | bytes 2359304 | tf_op jit(solution)/shard_map/ppermute | solution.py:258
  49.6 5.1 %collective-permute-start.12 = (f32[16,128]{1,0:T(8,128)S(1)}, f32[16,128]{1,0:T(8,128)S(1)}, u32[]{:S(2)}, u32[]{:S(2)}) collective-permute-start(f32[16,128]{1,0:T(8,128)S(1)} %shard_map.54.w0), channel_id=1, source_target_pairs={{0,96},{32,0},{64,32},{96,64},{1,97},{33,1},{65,33},{97,65},{2,98}... | collective-permute-start | bytes 24584 | tf_op jit(solution)/shard_map/ppermute | solution.py:254
  50.2 4.5 %collective-permute-start.11 = (f32[16,128]{1,0:T(8,128)S(1)}, f32[16,128]{1,0:T(8,128)S(1)}, u32[]{:S(2)}, u32[]{:S(2)}) collective-permute-start(f32[16,128]{1,0:T(8,128)S(1)} %shard_map.54.w0), channel_id=1, source_target_pairs={{0,64},{32,96},{64,0},{96,32},{1,65},{33,97},{65,1},{97,33},{2,66}... | collective-permute-start | bytes 24584 | tf_op jit(solution)/shard_map/ppermute | solution.py:254
  51.3 3.9 %collective-permute-start.10 = (f32[16,128]{1,0:T(8,128)S(1)}, f32[16,128]{1,0:T(8,128)S(1)}, u32[]{:S(2)}, u32[]{:S(2)}) collective-permute-start(f32[16,128]{1,0:T(8,128)S(1)} %shard_map.54.w0), channel_id=1, source_target_pairs={{0,32},{32,64},{64,96},{96,0},{1,33},{33,65},{65,97},{97,1},{2,34}... | collective-permute-start | bytes 24584 | tf_op jit(solution)/shard_map/ppermute | solution.py:254
  66.6 4.1 %collective-permute-start.13 = (f32[16,40,128]{2,1,0:T(8,128)S(1)}, f32[16,40,128]{2,1,0:T(8,128)S(1)}, u32[]{:S(2)}, u32[]{:S(2)}) collective-permute-start(f32[16,40,128]{2,1,0:T(8,128)S(1)} %all_to_all.11.received), channel_id=1, source_target_pairs={{0,16},{16,0},{1,17},{17,1},{2,18},{18,2},{3,19},{19,3},{4,20},{20... | collective-permute-start | bytes 983048 | tf_op jit(solution)/shard_map/ppermute | solution.py:258
